TPU v7x, 32 devices: a whole 2x2x4 slice. The times are simulated.
32 devices in a mesh: seq: 2 (over x), fsdp: 4 (over y, core), rep: 4 (over z).
Axes of the slice: x: 2, y: 2, z: 4, core: 2. Of those that a mesh axis runs over, the one named last changes fastest.
Arguments:
- tokens: bfloat16 [4, 2048, 2304], P('fsdp', ('seq', 'rep')), may hold values from -40 to 40
- doc_lengths: int32 [4, 4], P('fsdp'), may hold values from 1 to 2045, as said below
- cotangent: bfloat16 [4, 2048, 2304], P('fsdp', ('seq', 'rep')), may hold values from -6 to 6
- attn_gain: bfloat16 [2304], P('fsdp'), may hold values from 0.5 to 1.5
- w_query: bfloat16 [2304, 2304], P('fsdp'), may hold values from -0.125 to 0.125
- w_key: bfloat16 [2304, 2304], P('fsdp'), may hold values from -0.125 to 0.125
- w_value: bfloat16 [2304, 2304], P('fsdp'), may hold values from -0.125 to 0.125
- w_out: bfloat16 [2304, 2304], P('fsdp'), may hold values from -1 to 1
- mlp_gain: bfloat16 [2304], P('fsdp'), may hold values from 0.5 to 1.5
- w_gate: bfloat16 [2304, 5760], P('fsdp'), may hold values from -0.125 to 0.125
- w_up: bfloat16 [2304, 5760], P('fsdp'), may hold values from -0.125 to 0.125
- w_down: bfloat16 [5760, 2304], P('fsdp'), may hold values from -0.625 to 0.625
Outputs:
- output: bfloat16 [4, 2048, 2304], P('fsdp', ('seq', 'rep'))
- grad_tokens: bfloat16 [4, 2048, 2304], P('fsdp', ('seq', 'rep'))
- grad_attn_gain: float32 [2304], P('fsdp')
- grad_w_query: float32 [2304, 2304], P('fsdp')
- grad_w_key: float32 [2304, 2304], P('fsdp')
- grad_w_value: float32 [2304, 2304], P('fsdp')
- grad_w_out: float32 [2304, 2304], P('fsdp')
- grad_mlp_gain: float32 [2304], P('fsdp')
- grad_w_gate: float32 [2304, 5760], P('fsdp')
- grad_w_up: float32 [2304, 5760], P('fsdp')
- grad_w_down: float32 [5760, 2304], P('fsdp')
Inputs may be any that keep to these rules, and one draw needn't show every extreme that they name: `doc_lengths`: each row holds 4 lengths that add up to 2048; they are the documents of that sequence in order.
All inputs are finite; a program needn't handle non-finite values.
Results may differ from a plain program's by a relative error of at most 0.02.
Values may be sent and summed in bfloat16 or wider, within the bound.
A program may use at most 512 MiB of HBM per device.

v0:
```python
from functools import partial
import math

import jax
import jax.numpy as jnp
from jax import lax
from jax.sharding import PartitionSpec as P

HEADS = 36
HEAD_DIM = 64
WINDOW = 1024


BETA = 1.4 / math.sqrt(40.0)
EPSILON = 1e-05
NEGATIVE = -1e30


def from_behind(shard, axis, by):
    length = lax.axis_size(axis)
    pairs = [(i, i + by) for i in range(length) if 0 <= i + by < length]
    return lax.ppermute(shard, axis, pairs)


def gather_attn_in(attn_gain, w_query, w_key, w_value):
    return (
        lax.all_gather(attn_gain, "fsdp", axis=0, tiled=True),
        lax.all_gather(w_query, "fsdp", axis=0, tiled=True),
        lax.all_gather(w_key, "fsdp", axis=0, tiled=True),
        lax.all_gather(w_value, "fsdp", axis=0, tiled=True),
    )


def gather_attn_out(w_out):
    return lax.all_gather(w_out, "fsdp", axis=0, tiled=True)


def gather_mlp_in(mlp_gain, w_gate, w_up):
    return (
        lax.all_gather(mlp_gain, "fsdp", axis=0, tiled=True),
        lax.all_gather(w_gate, "fsdp", axis=0, tiled=True),
        lax.all_gather(w_up, "fsdp", axis=0, tiled=True),
    )


def gather_mlp_out(w_down):
    return lax.all_gather(w_down, "fsdp", axis=0, tiled=True)


def layout(lengths, position):
    doc_ends = jnp.cumsum(lengths)
    doc_ids = jnp.sum((position[:, None] >= doc_ends[None, :]).astype(jnp.int32), axis=1)
    doc_starts = doc_ends - lengths
    choose = doc_ids[:, None] == jnp.arange(lengths.shape[0], dtype=jnp.int32)[None, :]
    doc_first = jnp.sum(jnp.where(choose, doc_starts[None, :], 0), axis=1)
    return (doc_ids, position - doc_first)


def rope_tables(offset):
    half_dim = HEAD_DIM // 2
    frequency = jnp.exp(
        jnp.arange(half_dim, dtype=jnp.float32) * (-2.0 * math.log(10000.0) / HEAD_DIM)
    )
    angles = offset.astype(jnp.float32)[:, None] * frequency[None, :]
    cosine = jnp.cos(angles)
    sine_table = jnp.sin(angles)
    return (jnp.concatenate([cosine, cosine], 1), jnp.concatenate([sine_table, sine_table], 1))


def rotate(heads_in, cosine, sine_table):
    half_dim = HEAD_DIM // 2
    turned = jnp.concatenate([-heads_in[..., half_dim:], heads_in[..., :half_dim]], -1)
    return heads_in * cosine[:, None, :] + turned * sine_table[:, None, :]


def rope_apply(matrix, cosine, sine_table):
    row_count = matrix.shape[0]
    return rotate(matrix.reshape(row_count, HEADS, HEAD_DIM), cosine, sine_table).reshape(
        row_count, HEADS * HEAD_DIM
    )


def head_block(heads_total):
    return max((divisor for divisor in range(1, 13) if heads_total % divisor == 0))


def head_groups(matrix, groups):
    row_count = matrix.shape[0]
    return jnp.moveaxis(matrix.reshape(row_count, groups, HEADS // groups, HEAD_DIM), 1, 0)


def heads_merged(grouped):
    row_count = grouped.shape[1]
    return jnp.moveaxis(grouped, 0, 1).reshape(row_count, HEADS * HEAD_DIM)


def masked_scores(query_grp, key_grp, visible):
    scores = (
        jnp.einsum("qhd,khd->hqk", query_grp, key_grp, preferred_element_type=jnp.float32) * 0.125
    )
    return jnp.where(visible[None], scores, NEGATIVE)


def attend_forward(group_parts, visible):
    query_grp, key_grp, value_grp = group_parts
    scores = masked_scores(query_grp, key_grp, visible)
    row_top = jnp.max(scores, -1, keepdims=True)
    exp_scores = jnp.exp(scores - row_top)
    row_total = jnp.sum(exp_scores, -1, keepdims=True)
    probability = (exp_scores / row_total).astype(jnp.bfloat16)
    context = jnp.einsum("hqk,khd->qhd", probability, value_grp, preferred_element_type=jnp.float32)
    return (context, row_top, row_total)


def attend_backward(group_parts, visible):
    query_grp, key_grp, value_grp, grad_grp, row_top, row_total = group_parts
    scores = masked_scores(query_grp, key_grp, visible)
    probability = jnp.exp(scores - row_top) / row_total
    grad_prob = jnp.einsum("qhd,khd->hqk", grad_grp, value_grp, preferred_element_type=jnp.float32)
    row_delta = jnp.sum(probability * grad_prob, -1, keepdims=True)
    grad_score = (probability * (grad_prob - row_delta)).astype(jnp.bfloat16)
    grad_query = (
        jnp.einsum("hqk,khd->qhd", grad_score, key_grp, preferred_element_type=jnp.float32) * 0.125
    )
    grad_key = (
        jnp.einsum("hqk,qhd->khd", grad_score, query_grp, preferred_element_type=jnp.float32)
        * 0.125
    )
    grad_value = jnp.einsum(
        "hqk,qhd->khd",
        probability.astype(jnp.bfloat16),
        grad_grp,
        preferred_element_type=jnp.float32,
    )
    return (grad_query, grad_key, grad_value)


def transposed_product(activations_in, grads_in):
    return lax.dot_general(
        activations_in, grads_in, (((0,), (0,)), ((), ())), preferred_element_type=jnp.float32
    )


def weight_grads(activations_in, grads_list):
    row_count = activations_in.shape[1] // lax.axis_size("fsdp")
    results = []
    for grad_one in grads_list:

        def owner_rows(first_row, count_rows, grad_one=grad_one):
            return transposed_product(activations_in, grad_one)

        results.append(
            lax.psum_scatter(
                owner_rows(jnp.int32(0), row_count * lax.axis_size("fsdp")).astype(jnp.bfloat16),
                "fsdp",
                scatter_dimension=0,
                tiled=True,
            ).astype(jnp.float32)
        )
    return tuple(results)


def back_product(grads_in, weight_full):
    return lax.dot_general(
        grads_in, weight_full, (((1,), (1,)), ((), ())), preferred_element_type=jnp.float32
    )


def norm_back(grad_normed, unit_rows, rms_rows, gain_rows):
    scaled = grad_normed * gain_rows
    return rms_rows * (scaled - unit_rows * jnp.mean(scaled * unit_rows, -1, keepdims=True))


def on_device(
    tokens,
    doc_lengths,
    cotangent,
    attn_gain,
    w_query,
    w_key,
    w_value,
    w_out,
    mlp_gain,
    w_gate,
    w_up,
    w_down,
):
    tok_rows = tokens.shape[1]
    reach_pieces = WINDOW // tok_rows
    piece_index = lax.axis_index(("seq", "rep"))
    own_place = piece_index * tok_rows + jnp.arange(tok_rows, dtype=jnp.int32)
    key_place = (piece_index - reach_pieces) * tok_rows + jnp.arange(
        (reach_pieces + 1) * tok_rows, dtype=jnp.int32
    )
    lengths = doc_lengths[0]
    own_doc, own_offset = layout(lengths, own_place)
    key_doc = layout(lengths, key_place)[0]
    visible = (
        (key_doc[None, :] == own_doc[:, None])
        & (key_place[None, :] >= 0)
        & (key_place[None, :] <= own_place[:, None])
        & (key_place[None, :] > own_place[:, None] - WINDOW)
    )
    cosine, sine_table = rope_tables(own_offset)
    groups = HEADS // head_block(HEADS)
    gain_one, full_query, full_key, full_value = gather_attn_in(attn_gain, w_query, w_key, w_value)
    inputs = tokens[0].astype(jnp.float32)
    rms_one = lax.rsqrt(jnp.mean(inputs * inputs, -1, keepdims=True) + EPSILON)
    unit_one = inputs * rms_one
    normed_one = (unit_one * gain_one.astype(jnp.float32)).astype(jnp.bfloat16)
    query_rot = rope_apply(
        jnp.dot(normed_one, full_query, preferred_element_type=jnp.float32), cosine, sine_table
    ).astype(jnp.bfloat16)
    key_rot = rope_apply(
        jnp.dot(normed_one, full_key, preferred_element_type=jnp.float32), cosine, sine_table
    ).astype(jnp.bfloat16)
    value_low = jnp.dot(normed_one, full_value, preferred_element_type=jnp.float32).astype(
        jnp.bfloat16
    )
    key_slots = [key_rot]
    value_slots = [value_low]
    for back_step in range(1, reach_pieces + 1):
        moved_key, moved_value = from_behind((key_rot, value_low), ("seq", "rep"), back_step)
        key_slots.insert(0, moved_key)
        value_slots.insert(0, moved_value)
    keys_all = jnp.concatenate(key_slots, 0)
    values_all = jnp.concatenate(value_slots, 0)
    query_grp = head_groups(query_rot, groups)
    key_grp = head_groups(keys_all, groups)
    value_grp = head_groups(values_all, groups)
    context_grp, row_top, row_total = lax.map(
        partial(attend_forward, visible=visible), (query_grp, key_grp, value_grp)
    )
    context = heads_merged(context_grp).astype(jnp.bfloat16)
    full_out = gather_attn_out(w_out)
    hidden_res = inputs + BETA * jnp.dot(context, full_out, preferred_element_type=jnp.float32)
    gain_two, full_gate, full_up = gather_mlp_in(mlp_gain, w_gate, w_up)
    rms_two = lax.rsqrt(jnp.mean(hidden_res * hidden_res, -1, keepdims=True) + EPSILON)
    unit_two = hidden_res * rms_two
    normed_two = (unit_two * gain_two.astype(jnp.float32)).astype(jnp.bfloat16)
    gate_proj = jnp.dot(normed_two, full_gate, preferred_element_type=jnp.float32)
    up_proj = jnp.dot(normed_two, full_up, preferred_element_type=jnp.float32)
    sigmoid_gate = jax.nn.sigmoid(gate_proj)
    silu_gate = gate_proj * sigmoid_gate
    activation = (silu_gate * up_proj).astype(jnp.bfloat16)
    full_down = gather_mlp_out(w_down)
    mlp_out = jnp.dot(activation, full_down, preferred_element_type=jnp.float32)
    output = (hidden_res + BETA * mlp_out).astype(jnp.bfloat16)[None]
    upstream = cotangent[0].astype(jnp.float32)
    grad_mlp = (BETA * upstream).astype(jnp.bfloat16)
    back_down = gather_mlp_out(w_down)
    grad_activation = back_product(grad_mlp, back_down)
    grad_w_down = weight_grads(activation, [grad_mlp])[0]
    grad_up = (grad_activation * silu_gate).astype(jnp.bfloat16)
    grad_gate = (
        grad_activation * up_proj * (sigmoid_gate * (1.0 + gate_proj * (1.0 - sigmoid_gate)))
    ).astype(jnp.bfloat16)
    back_gain_two, back_gate, back_up = gather_mlp_in(mlp_gain, w_gate, w_up)
    grad_normed_two = back_product(grad_gate, back_gate) + back_product(grad_up, back_up)
    grad_w_gate, grad_w_up = weight_grads(normed_two, [grad_gate, grad_up])
    grad_gain_two = jnp.sum(grad_normed_two * unit_two, 0)
    grad_hidden = upstream + norm_back(
        grad_normed_two, unit_two, rms_two, back_gain_two.astype(jnp.float32)
    )
    grad_attn = (BETA * grad_hidden).astype(jnp.bfloat16)
    back_out = gather_attn_out(w_out)
    grad_context = back_product(grad_attn, back_out).astype(jnp.bfloat16)
    grad_w_out = weight_grads(context, [grad_attn])[0]
    grad_query_grp, grad_key_grp, grad_value_grp = lax.map(
        partial(attend_backward, visible=visible),
        (query_grp, key_grp, value_grp, head_groups(grad_context, groups), row_top, row_total),
    )
    grad_query_rot = heads_merged(grad_query_grp)
    grad_keys_all = heads_merged(grad_key_grp)
    grad_values_all = heads_merged(grad_value_grp)
    own_row = reach_pieces * tok_rows
    grad_key_sum = grad_keys_all[own_row:]
    grad_value_sum = grad_values_all[own_row:]
    for back_step in range(1, reach_pieces + 1):
        low_row = (reach_pieces - back_step) * tok_rows
        sent_key = grad_keys_all[low_row : low_row + tok_rows]
        sent_value = grad_values_all[low_row : low_row + tok_rows]
        got_key, got_value = (
            from_behind(sent_key.astype(jnp.bfloat16), ("seq", "rep"), -back_step).astype(
                sent_key.dtype
            ),
            from_behind(sent_value.astype(jnp.bfloat16), ("seq", "rep"), -back_step).astype(
                sent_value.dtype
            ),
        )
        grad_key_sum = grad_key_sum + got_key
        grad_value_sum = grad_value_sum + got_value
    grad_query = rope_apply(grad_query_rot, cosine, -sine_table).astype(jnp.bfloat16)
    grad_key = rope_apply(grad_key_sum, cosine, -sine_table).astype(jnp.bfloat16)
    grad_value = grad_value_sum.astype(jnp.bfloat16)
    back_gain_one, back_query, back_key, back_value = gather_attn_in(
        attn_gain, w_query, w_key, w_value
    )
    grad_normed_one = (
        back_product(grad_query, back_query)
        + back_product(grad_key, back_key)
        + back_product(grad_value, back_value)
    )
    grad_w_query, grad_w_key, grad_w_value = weight_grads(
        normed_one, [grad_query, grad_key, grad_value]
    )
    grad_gain_one = jnp.sum(grad_normed_one * unit_one, 0)
    grad_inputs = grad_hidden + norm_back(
        grad_normed_one, unit_one, rms_one, back_gain_one.astype(jnp.float32)
    )
    grad_tokens = grad_inputs.astype(jnp.bfloat16)[None]
    gain_shards = (
        lax.psum_scatter(grad_gain_one, "fsdp", scatter_dimension=0, tiled=True),
        lax.psum_scatter(grad_gain_two, "fsdp", scatter_dimension=0, tiled=True),
    )
    summed = (
        lax.psum(gain_shards[0].astype(jnp.bfloat16), ("seq", "rep")).astype(jnp.float32),
        lax.psum(gain_shards[1].astype(jnp.bfloat16), ("seq", "rep")).astype(jnp.float32),
        lax.psum(grad_w_query.astype(jnp.bfloat16), ("seq", "rep")).astype(jnp.float32),
        lax.psum(grad_w_key.astype(jnp.bfloat16), ("seq", "rep")).astype(jnp.float32),
        lax.psum(grad_w_value.astype(jnp.bfloat16), ("seq", "rep")).astype(jnp.float32),
        lax.psum(grad_w_out.astype(jnp.bfloat16), ("seq", "rep")).astype(jnp.float32),
        lax.psum(grad_w_gate.astype(jnp.bfloat16), ("seq", "rep")).astype(jnp.float32),
        lax.psum(grad_w_up.astype(jnp.bfloat16), ("seq", "rep")).astype(jnp.float32),
        lax.psum(grad_w_down.astype(jnp.bfloat16), ("seq", "rep")).astype(jnp.float32),
    )
    return (
        output,
        grad_tokens,
        summed[0],
        summed[2],
        summed[3],
        summed[4],
        summed[5],
        summed[1],
        summed[6],
        summed[7],
        summed[8],
    )


def solution(mesh):
    placed = (
        P("fsdp", ("seq", "rep"), None),
        P("fsdp", None),
        P("fsdp", ("seq", "rep"), None),
        P("fsdp"),
        P("fsdp", None),
        P("fsdp", None),
        P("fsdp", None),
        P("fsdp", None),
        P("fsdp"),
        P("fsdp", None),
        P("fsdp", None),
        P("fsdp", None),
    )
    return jax.shard_map(
        on_device,
        mesh=mesh,
        in_specs=placed,
        out_specs=(
            P("fsdp", ("seq", "rep"), None),
            P("fsdp", ("seq", "rep"), None),
            P("fsdp"),
            P("fsdp", None),
            P("fsdp", None),
            P("fsdp", None),
            P("fsdp", None),
            P("fsdp"),
            P("fsdp", None),
            P("fsdp", None),
            P("fsdp", None),
        ),
        check_vma=False,
    )
```

profile of v0, /device:TPU:4, one launch (start us, length us, event | category | flops | bytes accessed | tf_op | source)
XLA Modules:
  0.0 2904.7 jit_solution(14065455652972637244)
XLA Ops:
  13.8 10.2 all-reduce.7
  29.4 51.3 %all-gather.8.cloned.1.call-done = bf16[2304,2304]{1,0:T(8,128)(2,1)} async-done(((bf16[576,2304]{1,0:T(8,128)(2,1)}), bf16[2304,2304]{1,0:T(8,128)(2,1)}) %all-gather.8.cloned.1.call-update) | async-done | bytes 10616848 | tf_op jit(solution)/shard_map/all_gather | solution.py:30
  80.7 7.0 convolution_convert_fusion.8
  92.3 6.3 collective-permute-start.1
  104.0 49.2 %all-gather.12.cloned.1.call-done = bf16[2304,2304]{1,0:T(8,128)(2,1)} async-done(((bf16[576,2304]{1,0:T(8,128)(2,1)}), bf16[2304,2304]{1,0:T(8,128)(2,1)}) %all-gather.12.cloned.1.call-update) | async-done | bytes 10616848 | tf_op jit(solution)/shard_map/all_gather | solution.py:29
  153.2 15.4 copy.37
  168.6 57.1 %all-gather.10.cloned.1.call-done = bf16[2304,2304]{1,0:T(8,128)(2,1)} async-done(((bf16[576,2304]{1,0:T(8,128)(2,1)}), bf16[2304,2304]{1,0:T(8,128)(2,1)}) %all-gather.10.cloned.1.call-update) | async-done | bytes 10616848 | tf_op jit(solution)/shard_map/all_gather | solution.py:28
  225.7 14.8 copy.36
  240.6 6.8 fusion.98
  259.4 6.3 collective-permute-start.5
  281.9 8.9 copy.35
  290.8 20.2 collective-permute-done.4
  318.0 22.7 collective-permute-done.7
  344.7 47.6 %while.32 = (s32[]{:T(128)}, bf16[3,256,12,64]{1,3,2,0:T(8,128)(2,1)S(1)}, f32[3,12,256,1]{2,1,3,0:T(8,128)}, f32[3,12,256,1]{2,1,3,0:T(8,128)}, bf16[3,1280,12,...) while((s32[]{:T(128)}, ...), condition=%wide.region_8.9_spmd.clone.clone, body=%wide.region_5.8_spmd.clone.sunk.clone | while | flops 1055778816 | bytes 53752200 | solution.py:231
  354.0 6.0 fusion.191
  369.9 5.9 fusion.191
  385.7 5.9 fusion.191
  393.3 6.6 multiply_reduce_fusion.3
  400.2 61.9 %all-gather.16.cloned.1.call-done = bf16[2304,5760]{1,0:T(8,128)(2,1)} async-done(((bf16[576,5760]{1,0:T(8,128)(2,1)}), bf16[2304,5760]{1,0:T(8,128)(2,1)}) %all-gather.16.cloned.1.call-update) | async-done | bytes 26542096 | tf_op jit(solution)/shard_map/all_gather | solution.py:41
  462.0 16.5 fusion.122
  478.5 147.4 %all-gather.18.cloned.1.call-done = bf16[2304,5760]{1,0:T(8,128)(2,1)} async-done(((bf16[576,5760]{1,0:T(8,128)(2,1)}), bf16[2304,5760]{1,0:T(8,128)(2,1)}) %all-gather.18.cloned.1.call-update) | async-done | bytes 26542096 | tf_op jit(solution)/shard_map/all_gather | solution.py:42
  625.9 16.9 fusion.123
  642.8 147.1 %all-gather.20.cloned.1.call-done = bf16[5760,2304]{1,0:T(8,128)(2,1)} async-done(((bf16[1440,2304]{1,0:T(8,128)(2,1)}), bf16[5760,2304]{1,0:T(8,128)(2,1)}) %all-gather.20.cloned.1.call-update) | async-done | bytes 26542096 | tf_op jit(solution)/shard_map/all_gather | solution.py:47
  789.9 20.2 multiply_convert_fusion.1
  810.1 14.8 fusion.124
  825.0 14.3 multiply_reduce_fusion.1
  841.3 7.4 convolution_convert_fusion.3
  848.7 7.7 convolution_convert_fusion.7
  857.7 127.4 %while.33 = (s32[]{:T(128)}, f32[3,256,12,64]{1,3,2,0:T(8,128)}, f32[3,1280,12,64]{1,3,2,0:T(8,128)}, f32[3,1280,12,64]{1,3,2,0:T(8,128)}, bf16[3,1280,12,64]{1,...) while((s32[]{:T(128)}, f32[3,256,12,64]{1,3,2,0:T(8,128)}, ...), condition=%wide.region_13.14_spmd.clone.clone, body=%wide.region_11.13_spmd.clone.sunk.clone | while | flops 2559046656 | bytes 134860208 | solution.py:269
  857.7 11.6 fusion.200
  870.6 12.1 multiply_reduce_fusion.6
  882.7 7.9 multiply_convert_fusion.10
  903.3 9.3 fusion.200
  914.0 10.6 multiply_reduce_fusion.6
  924.6 7.1 multiply_convert_fusion.10
  944.4 9.3 fusion.200
  955.1 10.3 multiply_reduce_fusion.6
  965.3 7.1 multiply_convert_fusion.10
  998.8 21.9 collective-permute-done.11
  1024.8 49.8 %collective-permute-done.9 = bf16[256,2304]{0,1:T(8,128)(2,1)S(1)} collective-permute-done((bf16[256,2304]{0,1:T(8,128)(2,1)S(1)}, bf16[256,2304]{0,1:T(8,128)(2,1)S(1)}, u32[]{:S(2)}, u32[]{:S(2)}) %collective-permute-start.9) | collective-permute-done | bytes 1179680 | tf_op jit(solution)/shard_map/ppermute | solution.py:22
  1080.7 6.0 convolution_convert_fusion.6
  1092.6 5.9 convolution_convert_fusion.5
  1098.6 5.2 bitcast_convert_fusion
  1111.5 22.6 collective-permute-done.15
  1134.2 31.8 %collective-permute-done.14 = bf16[256,2304]{0,1:T(8,128)(2,1)S(1)} collective-permute-done((bf16[256,2304]{0,1:T(8,128)(2,1)S(1)}, bf16[256,2304]{0,1:T(8,128)(2,1)S(1)}, u32[]{:S(2)}, u32[]{:S(2)}) %collective-permute-start.14) | collective-permute-done | bytes 1179680 | tf_op jit(solution)/shard_map/ppermute | solution.py:22
  1165.9 48.7 %collective-permute-done.13 = bf16[256,2304]{0,1:T(8,128)(2,1)S(1)} collective-permute-done((bf16[256,2304]{0,1:T(8,128)(2,1)S(1)}, bf16[256,2304]{0,1:T(8,128)(2,1)S(1)}, u32[]{:S(2)}, u32[]{:S(2)}) %collective-permute-start.13) | collective-permute-done | bytes 1179680 | tf_op jit(solution)/shard_map/ppermute | solution.py:22
  1216.5 6.0 convolution_convert_fusion.4
  1223.7 14.6 convolution_convert_fusion.2
  1238.4 14.8 convolution_convert_fusion.1
  1254.4 13.9 convolution_convert_fusion
  1268.6 17.0 reduce-scatter.10.cloned.1.call-done
  1285.6 89.3 %reduce-scatter.12.cloned.1.call-done = bf16[576,2304]{1,0:T(8,128)(2,1)} async-done(((bf16[2304,2304]{1,0:T(8,128)(2,1)}), bf16[576,2304]{1,0:T(8,128)(2,1)}) %reduce-scatter.12.cloned.1.call-update) | async-done | bytes 2654224 | tf_op jit(solution)/shard_map/reduce_scatter | solution.py:153
  1374.9 191.9 %reduce-scatter.16.cloned.1.call-done = bf16[576,5760]{1,0:T(8,128)(2,1)} async-done(((bf16[2304,5760]{1,0:T(8,128)(2,1)}), bf16[576,5760]{1,0:T(8,128)(2,1)}) %reduce-scatter.16.cloned.1.call-update) | async-done | bytes 6635536 | tf_op jit(solution)/shard_map/reduce_scatter | solution.py:153
  1566.8 192.2 %reduce-scatter.18.cloned.1.call-done = bf16[576,5760]{1,0:T(8,128)(2,1)} async-done(((bf16[2304,5760]{1,0:T(8,128)(2,1)}), bf16[576,5760]{1,0:T(8,128)(2,1)}) %reduce-scatter.18.cloned.1.call-update) | async-done | bytes 6635536 | tf_op jit(solution)/shard_map/reduce_scatter | solution.py:153
  1759.1 191.9 %reduce-scatter.20.cloned.1.call-done = bf16[1440,2304]{1,0:T(8,128)(2,1)} async-done(((bf16[5760,2304]{1,0:T(8,128)(2,1)}), bf16[1440,2304]{1,0:T(8,128)(2,1)}) %reduce-scatter.20.cloned.1.call-update) | async-done | bytes 6635536 | tf_op jit(solution)/shard_map/reduce_scatter | solution.py:153
  1952.6 14.6 fusion.62
  1967.3 6.3 fusion.125
  1973.6 6.3 convolution_add_fusion.2
  1984.0 13.3 all-reduce.4
  2000.0 23.9 all-reduce.5
  2030.5 833.1 %all-reduce.10.cloned.1.call-done = (bf16[576,2304]{1,0:T(8,128)(2,1)}, bf16[576,2304]{1,0:T(8,128)(2,1)}, bf16[576,2304]{1,0:T(8,128)(2,1)}, bf16[576,2304]{1,0...) async-done(((bf16[576,2304]{1,0:T(8,128)(2,1)}, bf16[576,2304]{1,0:T(8,128)(2,1)}, bf16[576,2304]{1,0:T(8,128)(2,1)}, ...) | async-done | bytes 30523408 | tf_op jit(solution)/shard_map/psum | solution.py:319
  2876.9 9.0 convert_element_type.311
  2885.9 6.0 convert_element_type.313
  2891.9 6.0 convert_element_type.315
  (267 shorter events, 206.5 us)
Async XLA Ops:
  7.2 73.5 %all-gather.8.cloned.1.call-start = ((), (), s32[]{:S(2)}) async-start(), calls=%async_computation.7 | async-start | bytes 13271040 | tf_op jit(solution)/shard_map/all_gather | solution.py:30
  7.9 145.3 %all-gather.12.cloned.1.call-start = ((), (), s32[]{:S(2)}) async-start(), calls=%async_computation.9 | async-start | bytes 13271040 | tf_op jit(solution)/shard_map/all_gather | solution.py:29
  8.7 217.1 %all-gather.10.cloned.1.call-start = ((), (), s32[]{:S(2)}) async-start(), calls=%async_computation.8 | async-start | bytes 13271040 | tf_op jit(solution)/shard_map/all_gather | solution.py:28
  9.4 382.9 %all-gather.14.cloned.1.call-start = ((), (), s32[]{:S(2)}) async-start(), calls=%async_computation.10 | async-start | bytes 13271040 | tf_op jit(solution)/shard_map/all_gather | solution.py:35
  10.0 452.0 %all-gather.16.cloned.1.call-start = ((), (), s32[]{:S(2)}) async-start(), calls=%async_computation.11 | async-start | bytes 33177600 | tf_op jit(solution)/shard_map/all_gather | solution.py:41
  10.6 615.3 %all-gather.18.cloned.1.call-start = ((), (), s32[]{:S(2)}) async-start(), calls=%async_computation.12 | async-start | bytes 33177600 | tf_op jit(solution)/shard_map/all_gather | solution.py:42
  11.1 2.2 copy-start.46
  11.2 2.4 copy-start.47
  11.2 13.4 copy-start.48
  11.2 778.7 %all-gather.20.cloned.1.call-start = ((), (), s32[]{:S(2)}) async-start(), calls=%async_computation.13 | async-start | bytes 33177600 | tf_op jit(solution)/shard_map/all_gather | solution.py:47
  11.9 16.5 copy-start.1
  11.9 1256.6 %reduce-scatter.14.cloned.1.call-start = ((), (), s32[]{:S(2)}) async-start(), calls=%async_computation.17 | async-start | bytes 13271040 | tf_op jit(solution)/shard_map/reduce_scatter | solution.py:153
  87.7 171.7 %collective-permute-start = (bf16[256,2304]{1,0:T(8,128)(2,1)S(1)}, bf16[256,2304]{1,0:T(8,128)(2,1)}, u32[]{:S(2)}, u32[]{:S(2)}) collective-permute-start(bf16[256,2304]{1,0:T(8,128)(2,1)S(1)} %convolution_convert_fusion.8), channel_id=1, source_target_pairs={{0,16},{1,17},{2,18},{3,19},{4,20},{5,21},{6,22},{7,23},{8,24},{9,... | collective-permute-start | bytes 3538952 | tf_op jit(solution)/shard_map/ppermute | solution.py:22
  92.3 175.7 %collective-permute-start.1 = (bf16[256,2304]{1,0:T(8,128)(2,1)S(1)}, bf16[256,2304]{1,0:T(8,128)(2,1)}, u32[]{:S(2)}, u32[]{:S(2)}) collective-permute-start(bf16[256,2304]{1,0:T(8,128)(2,1)S(1)} %convolution_convert_fusion.8), channel_id=1, source_target_pairs={{0,3},{1,16},{2,17},{3,18},{16,19},{4,7},{5,20},{6,21},{7,22},{20,... | collective-permute-start | bytes 3538952 | tf_op jit(solution)/shard_map/ppermute | solution.py:22
  98.6 174.1 %collective-permute-start.2 = (bf16[256,2304]{1,0:T(8,128)(2,1)S(1)}, bf16[256,2304]{1,0:T(8,128)(2,1)}, u32[]{:S(2)}, u32[]{:S(2)}) collective-permute-start(bf16[256,2304]{1,0:T(8,128)(2,1)S(1)} %convolution_convert_fusion.8), channel_id=1, source_target_pairs={{0,2},{1,3},{2,16},{3,17},{16,18},{17,19},{4,6},{5,7},{6,20},{7,21... | collective-permute-start | bytes 3538952 | tf_op jit(solution)/shard_map/ppermute | solution.py:22
  100.9 177.5 %collective-permute-start.3 = (bf16[256,2304]{1,0:T(8,128)(2,1)S(1)}, bf16[256,2304]{1,0:T(8,128)(2,1)}, u32[]{:S(2)}, u32[]{:S(2)}) collective-permute-start(bf16[256,2304]{1,0:T(8,128)(2,1)S(1)} %convolution_convert_fusion.8), channel_id=1, source_target_pairs={{0,1},{1,2},{2,3},{3,16},{16,17},{17,18},{18,19},{4,5},{5,6},{6,7}... | collective-permute-start | bytes 3538952 | tf_op jit(solution)/shard_map/ppermute | solution.py:22
  240.6 8.0 copy-start.10
  240.6 8.0 copy-start.27
  240.6 8.0 copy-start.43
  255.1 55.9 %collective-permute-start.4 = (bf16[256,2304]{0,1:T(8,128)(2,1)S(1)}, bf16[256,2304]{0,1:T(8,128)(2,1)}, u32[]{:S(2)}, u32[]{:S(2)}) collective-permute-start(bf16[256,2304]{0,1:T(8,128)(2,1)S(1)} %bitcast.325), channel_id=1, source_target_pairs={{0,16},{1,17},{2,18},{3,19},{4,20},{5,21},{6,22},{7,23},{8,24},{9,... | collective-permute-start | bytes 3538952 | tf_op jit(solution)/shard_map/ppermute | solution.py:22
  259.4 53.4 %collective-permute-start.5 = (bf16[256,2304]{0,1:T(8,128)(2,1)S(1)}, bf16[256,2304]{0,1:T(8,128)(2,1)}, u32[]{:S(2)}, u32[]{:S(2)}) collective-permute-start(bf16[256,2304]{0,1:T(8,128)(2,1)S(1)} %bitcast.326), channel_id=1, source_target_pairs={{0,3},{1,16},{2,17},{3,18},{16,19},{4,7},{5,20},{6,21},{7,22},{20,... | collective-permute-start | bytes 3538952 | tf_op jit(solution)/shard_map/ppermute | solution.py:22
  268.0 48.3 %collective-permute-start.6 = (bf16[256,2304]{0,1:T(8,128)(2,1)S(1)}, bf16[256,2304]{0,1:T(8,128)(2,1)}, u32[]{:S(2)}, u32[]{:S(2)}) collective-permute-start(bf16[256,2304]{0,1:T(8,128)(2,1)S(1)} %bitcast.327), channel_id=1, source_target_pairs={{0,2},{1,3},{2,16},{3,17},{16,18},{17,19},{4,6},{5,7},{6,20},{7,21... | collective-permute-start | bytes 3538952 | tf_op jit(solution)/shard_map/ppermute | solution.py:22
  272.7 68.0 %collective-permute-start.7 = (bf16[256,2304]{0,1:T(8,128)(2,1)S(1)}, bf16[256,2304]{0,1:T(8,128)(2,1)}, u32[]{:S(2)}, u32[]{:S(2)}) collective-permute-start(bf16[256,2304]{0,1:T(8,128)(2,1)S(1)} %bitcast.328), channel_id=1, source_target_pairs={{0,1},{1,2},{2,3},{3,16},{16,17},{17,18},{18,19},{4,5},{5,6},{6,7}... | collective-permute-start | bytes 3538952 | tf_op jit(solution)/shard_map/ppermute | solution.py:22
  317.9 26.7 copy-start.31
  317.9 26.7 copy-start.34
  318.0 26.7 copy-start.37
  318.0 26.7 copy-start.39
  342.1 2.6 copy-start
  344.7 48.6 %copy-start.2 = (bf16[1,256,2304]{2,1,0:T(8,128)(2,1)S(1)}, bf16[1,256,2304]{2,1,0:T(8,128)(2,1)}, u32[]{:S(2)}) copy-start(bf16[1,256,2304]{2,1,0:T(8,128)(2,1)} %param.16) | copy-start | bytes 3538948
  393.3 6.6 copy-start.41
  399.8 439.4 %copy-start.4 = (f32[256,2304]{1,0:T(8,128)}, f32[256,2304]{1,0:T(8,128)S(1)}, u32[]{:S(2)}) copy-start(f32[256,2304]{1,0:T(8,128)S(1)} %get-tuple-element.310) | copy-start | bytes 7077892
  400.1 225.8 %copy-start.11 = (bf16[256,2304]{1,0:T(8,128)(2,1)}, bf16[256,2304]{1,0:T(8,128)(2,1)S(1)}, u32[]{:S(2)}) copy-start(bf16[256,2304]{1,0:T(8,128)(2,1)S(1)} %multiply_convert_fusion.5) | copy-start | bytes 3538948
  810.1 14.8 copy-start.42
  825.0 14.3 copy-start.13
  857.1 411.6 %reduce-scatter.8.cloned.1.call-start = ((), (), s32[]{:S(2)}) async-start(), calls=%async_computation.14 | async-start | bytes 13271040 | tf_op jit(solution)/shard_map/reduce_scatter | solution.py:153
  990.8 29.9 %collective-permute-start.11 = (bf16[256,2304]{0,1:T(8,128)(2,1)S(1)}, bf16[256,2304]{0,1:T(8,128)(2,1)S(1)}, u32[]{:S(2)}, u32[]{:S(2)}) collective-permute-start(bf16[256,2304]{0,1:T(8,128)(2,1)S(1)} %bitcast.336), channel_id=1, source_target_pairs={{16,0},{17,1},{18,2},{19,3},{20,4},{21,5},{22,6},{23,7},{24,8},{25... | collective-permute-start | bytes 3538952 | tf_op jit(solution)/shard_map/ppermute | solution.py:22
  992.1 32.6 %collective-permute-start.10 = (bf16[256,2304]{0,1:T(8,128)(2,1)S(1)}, bf16[256,2304]{0,1:T(8,128)(2,1)S(1)}, u32[]{:S(2)}, u32[]{:S(2)}) collective-permute-start(bf16[256,2304]{0,1:T(8,128)(2,1)S(1)} %bitcast.334), channel_id=1, source_target_pairs={{3,0},{16,1},{17,2},{18,3},{19,16},{7,4},{20,5},{21,6},{22,7},{23,... | collective-permute-start | bytes 3538952 | tf_op jit(solution)/shard_map/ppermute | solution.py:22
  993.4 81.1 %collective-permute-start.9 = (bf16[256,2304]{0,1:T(8,128)(2,1)S(1)}, bf16[256,2304]{0,1:T(8,128)(2,1)S(1)}, u32[]{:S(2)}, u32[]{:S(2)}) collective-permute-start(bf16[256,2304]{0,1:T(8,128)(2,1)S(1)} %bitcast.332), channel_id=1, source_target_pairs={{2,0},{3,1},{16,2},{17,3},{18,16},{19,17},{6,4},{7,5},{20,6},{21,7... | collective-permute-start | bytes 3538952 | tf_op jit(solution)/shard_map/ppermute | solution.py:22
  994.7 79.8 %collective-permute-start.8 = (bf16[256,2304]{0,1:T(8,128)(2,1)S(1)}, bf16[256,2304]{0,1:T(8,128)(2,1)S(1)}, u32[]{:S(2)}, u32[]{:S(2)}) collective-permute-start(bf16[256,2304]{0,1:T(8,128)(2,1)S(1)} %bitcast.331), channel_id=1, source_target_pairs={{1,0},{2,1},{3,2},{16,3},{17,16},{18,17},{19,18},{5,4},{6,5},{7,6}... | collective-permute-start | bytes 3538952 | tf_op jit(solution)/shard_map/ppermute | solution.py:22
  996.2 2.4 copy-start.6
  1076.7 2.8 copy-start.26
  1086.7 198.9 %reduce-scatter.10.cloned.1.call-start = ((), (), s32[]{:S(2)}) async-start(), calls=%async_computation.15 | async-start | bytes 13271040 | tf_op jit(solution)/shard_map/reduce_scatter | solution.py:153
  1098.5 276.4 %reduce-scatter.12.cloned.1.call-start = ((), (), s32[]{:S(2)}) async-start(), calls=%async_computation.16 | async-start | bytes 13271040 | tf_op jit(solution)/shard_map/reduce_scatter | solution.py:153
  1104.4 29.7 %collective-permute-start.15 = (bf16[256,2304]{0,1:T(8,128)(2,1)S(1)}, bf16[256,2304]{0,1:T(8,128)(2,1)S(1)}, u32[]{:S(2)}, u32[]{:S(2)}) collective-permute-start(bf16[256,2304]{0,1:T(8,128)(2,1)S(1)} %bitcast.338), channel_id=1, source_target_pairs={{16,0},{17,1},{18,2},{19,3},{20,4},{21,5},{22,6},{23,7},{24,8},{25... | collective-permute-start | bytes 3538952 | tf_op jit(solution)/shard_map/ppermute | solution.py:22
  1105.7 60.2 %collective-permute-start.14 = (bf16[256,2304]{0,1:T(8,128)(2,1)S(1)}, bf16[256,2304]{0,1:T(8,128)(2,1)S(1)}, u32[]{:S(2)}, u32[]{:S(2)}) collective-permute-start(bf16[256,2304]{0,1:T(8,128)(2,1)S(1)} %bitcast.337), channel_id=1, source_target_pairs={{3,0},{16,1},{17,2},{18,3},{19,16},{7,4},{20,5},{21,6},{22,7},{23,... | collective-permute-start | bytes 3538952 | tf_op jit(solution)/shard_map/ppermute | solution.py:22
  1107.0 107.6 %collective-permute-start.13 = (bf16[256,2304]{0,1:T(8,128)(2,1)S(1)}, bf16[256,2304]{0,1:T(8,128)(2,1)S(1)}, u32[]{:S(2)}, u32[]{:S(2)}) collective-permute-start(bf16[256,2304]{0,1:T(8,128)(2,1)S(1)} %bitcast.335), channel_id=1, source_target_pairs={{2,0},{3,1},{16,2},{17,3},{18,16},{19,17},{6,4},{7,5},{20,6},{21,7... | collective-permute-start | bytes 3538952 | tf_op jit(solution)/shard_map/ppermute | solution.py:22
  1108.3 106.3 %collective-permute-start.12 = (bf16[256,2304]{0,1:T(8,128)(2,1)S(1)}, bf16[256,2304]{0,1:T(8,128)(2,1)S(1)}, u32[]{:S(2)}, u32[]{:S(2)}) collective-permute-start(bf16[256,2304]{0,1:T(8,128)(2,1)S(1)} %bitcast.333), channel_id=1, source_target_pairs={{1,0},{2,1},{3,2},{16,3},{17,16},{18,17},{19,18},{5,4},{6,5},{7,6}... | collective-permute-start | bytes 3538952 | tf_op jit(solution)/shard_map/ppermute | solution.py:22
  1222.4 344.4 %reduce-scatter.16.cloned.1.call-start = ((), (), s32[]{:S(2)}) async-start(), calls=%async_computation.18 | async-start | bytes 33177600 | tf_op jit(solution)/shard_map/reduce_scatter | solution.py:153
  1238.3 520.7 %reduce-scatter.18.cloned.1.call-start = ((), (), s32[]{:S(2)}) async-start(), calls=%async_computation.19 | async-start | bytes 33177600 | tf_op jit(solution)/shard_map/reduce_scatter | solution.py:153
  1253.2 697.8 %reduce-scatter.20.cloned.1.call-start = ((), (), s32[]{:S(2)}) async-start(), calls=%async_computation.20 | async-start | bytes 33177600 | tf_op jit(solution)/shard_map/reduce_scatter | solution.py:153
  1268.3 1595.2 %all-reduce.10.cloned.1.call-start = ((), (), s32[]{:S(2)}) async-start(), calls=%async_computation.21 | async-start | bytes 61046784 | tf_op jit(solution)/shard_map/psum | solution.py:319
  1952.6 14.7 copy-start.22
  1967.3 6.3 copy-start.16
  1967.3 12.6 slice-start.4
  1967.3 12.6 slice-start.5
  1973.6 6.3 copy-start.18
  1973.6 6.3 slice-start.6
  2863.6 4.7 copy-start.21
  2868.2 2.8 copy-start.20
  2871.0 2.8 copy-start.19
  2873.8 12.1 slice-start.2
  2876.9 9.0 slice-start.3
  2876.9 15.0 slice-start
  2885.9 6.0 slice-start.1
  (23 other events, 26.2 us)
Sparse Core Ops, SparseCore 0:
  9.6 71.0 all-gather.7
  82.2 70.9 all-gather.11
  154.8 70.9 all-gather.9
  227.2 70.9 all-gather.13
  299.6 162.4 all-gather.15
  463.4 162.4 all-gather.17
  627.5 162.4 all-gather.19
  857.2 86.1 reduce-scatter.13
  1086.8 109.4 reduce-scatter.7
  1199.4 86.1 reduce-scatter.9
  1288.8 86.1 reduce-scatter.11
  1377.4 189.3 reduce-scatter.15
  1569.6 189.3 reduce-scatter.17
  1761.5 189.3 reduce-scatter.19
  1957.6 905.8 all-reduce.9
where the time goes:
time: 2920 us; the launch traced here: 2900 us
  waiting for transfers between devices  2260 us (77%)
  matrix products  346 us (12%)
  other arithmetic  110 us (4%)
  local copies, waits for them, and re-layouts  82.5 us (3%)
  blocking collectives  47.4 us (2%)
  starting transfers between devices  44.3 us (2%)
    psum x1, waiting for transfers between devices, on_device(): lax.psum(grad_w_query.astype(jnp.bfloat16), ('seq', 'rep'))  833 us
    reduce_scatter x7, waiting for transfers between devices, weight_grads(): lax.psum_scatter(owner_rows(jnp.int32(0), row_count * lax.axis_size('fsdp...  682 us
    ppermute x16, waiting for transfers between devices, from_behind(): return lax.ppermute(shard, axis, pairs)  224 us
    all_gather x1, waiting for transfers between devices, gather_mlp_in(): lax.all_gather(w_up, 'fsdp', axis=0, tiled=True)  147 us
    all_gather x1, waiting for transfers between devices, gather_mlp_out(): return lax.all_gather(w_down, 'fsdp', axis=0, tiled=True)  147 us
    dot_general x7, matrix products, back_product(): lax.dot_general(grads_in, weight_full, (((1,), (1,)), ((), ())), preferre...  73.6 us
    dot_general x7, matrix products, transposed_product(): lax.dot_general(activations_in, grads_in, (((0,), (0,)), ((), ())), prefe...  68.5 us
    all_gather x1, waiting for transfers between devices, gather_mlp_in(): lax.all_gather(w_gate, 'fsdp', axis=0, tiled=True)  61.9 us
  transfers between devices with their start and end apart: 31, of which 21 were waited for; matrix products, arithmetic and copies ran while one was open for 15% of the time, Pallas kernels for 0%

commit v1 on v0

v1 whole, which is shorter than its diff:
```python
from functools import partial
import math

import jax
import jax.numpy as jnp
from jax import lax
from jax.experimental import pallas as pl
from jax.experimental.pallas import tpu as pltpu
from jax.sharding import Mesh, PartitionSpec as P

HEADS = 36
HEAD_DIM = 64
WINDOW = 1024

BETA = 1.4 / math.sqrt(40.0)
EPSILON = 1e-05
NEGATIVE = -1e30

PLANE = ("x", "y", "c")
LANES = 128
VMEM_LIMIT = 60 * 1024 * 1024
F32 = jnp.float32
BF16 = jnp.bfloat16


def dot(left, right):
    return jnp.dot(left, right, preferred_element_type=F32)


def dot_tn(left, right):
    return lax.dot_general(left, right, (((0,), (0,)), ((), ())), preferred_element_type=F32)


def dot_nt(left, right):
    return lax.dot_general(left, right, (((1,), (1,)), ((), ())), preferred_element_type=F32)


def swap(array, axis):
    return lax.ppermute(array, axis, [(0, 1), (1, 0)])


def layout(lengths, position):
    doc_ends = jnp.cumsum(lengths)
    doc_ids = jnp.sum((position[:, None] >= doc_ends[None, :]).astype(jnp.int32), axis=1)
    doc_starts = doc_ends - lengths
    choose = doc_ids[:, None] == jnp.arange(lengths.shape[0], dtype=jnp.int32)[None, :]
    doc_first = jnp.sum(jnp.where(choose, doc_starts[None, :], 0), axis=1)
    return (doc_ids, position - doc_first)


def rope_tables(offset):
    half_dim = HEAD_DIM // 2
    frequency = jnp.exp(
        jnp.arange(half_dim, dtype=F32) * (-2.0 * math.log(10000.0) / HEAD_DIM)
    )
    angles = offset.astype(F32)[:, None] * frequency[None, :]
    cosine = jnp.cos(angles)
    sine_table = jnp.sin(angles)
    return (
        jnp.concatenate([cosine, cosine] * 2, 1),
        jnp.concatenate([-sine_table, sine_table] * 2, 1),
    )


MESH_ID = pl.DeviceIdType.MESH
ANY = pl.BlockSpec(memory_space=pl.ANY)
IN_VMEM = pl.BlockSpec(memory_space=pltpu.VMEM)


def remote(src, dst, sems, index, device):
    return pltpu.make_async_remote_copy(
        src_ref=src,
        dst_ref=dst,
        send_sem=sems[0].at[index],
        recv_sem=sems[1].at[index],
        device_id=device,
        device_id_type=MESH_ID,
    )


def meet(devices):
    barrier = pltpu.get_barrier_semaphore()
    for device in devices:
        pl.semaphore_signal(barrier, inc=1, device_id=device, device_id_type=MESH_ID)
    pl.semaphore_wait(barrier, len(devices))


def gather_kernel(cores, block, out, send, recv, here):
    x, y, c = (lax.axis_index(a) for a in PLANE)
    slot = c if cores == 2 else 0
    to_x, to_y, to_c = {"x": 1 - x}, {"y": 1 - y}, {"c": 1 - c}
    sems = (send, recv)
    half = block.shape[0] // 2
    top, low = pl.ds(0, half), pl.ds(half, half)
    own, next_x = 2 * x + y, 2 * (1 - x) + y
    next_y, across = 2 * x + 1 - y, 2 * (1 - x) + 1 - y
    meet([to_x, to_y] + ([to_c] if cores == 2 else []))

    def give(index, rows, device):
        copy = remote(block.at[rows], out.at[own, slot, rows], sems, index, device)
        copy.start()
        return copy

    def forward(index, chip, rows, device):
        place = out.at[chip, slot, rows]
        copy = remote(place, place, sems, index, device)
        copy.start()
        return copy

    x_top = give(0, top, to_x)
    y_low = give(1, low, to_y)
    x_low = give(2, low, to_x)
    y_top = give(3, top, to_y)
    stay = pltpu.make_async_copy(block, out.at[own, slot], here)
    stay.start()
    sends = [x_top, y_low, x_low, y_top]
    passed = []
    if cores == 2:
        passed.append(give(4, pl.ds(0, 2 * half), to_c))
    x_top.wait_recv()
    y_across = forward(5, next_x, top, to_y)
    if cores == 2:
        passed.append(forward(6, next_x, top, to_c))
    y_low.wait_recv()
    x_across = forward(7, next_y, low, to_x)
    if cores == 2:
        passed.append(forward(8, next_y, low, to_c))
    x_low.wait_recv()
    if cores == 2:
        passed.append(forward(9, next_x, low, to_c))
    y_top.wait_recv()
    if cores == 2:
        passed.append(forward(10, next_y, top, to_c))
    y_across.wait_recv()
    if cores == 2:
        passed.append(forward(11, across, top, to_c))
    x_across.wait_recv()
    if cores == 2:
        passed.append(forward(12, across, low, to_c))
    for copy in passed:
        copy.wait_recv()
    stay.wait()
    for copy in sends + [y_across, x_across] + passed:
        copy.wait_send()


def gather_rows(block, cores, ident):
    rows, cols = block.shape
    out = pl.pallas_call(
        partial(gather_kernel, cores),
        out_shape=jax.ShapeDtypeStruct((4, cores, rows, cols), block.dtype),
        in_specs=[IN_VMEM],
        out_specs=ANY,
        scratch_shapes=[
            pltpu.SemaphoreType.DMA((13,)),
            pltpu.SemaphoreType.DMA((13,)),
            pltpu.SemaphoreType.DMA,
        ],
        compiler_params=pltpu.CompilerParams(
            collective_id=ident, has_side_effects=True, vmem_limit_bytes=VMEM_LIMIT
        ),
        name="gather_rows",
    )(block)
    return out.reshape(4 * cores * rows, cols)


def add_rows(target, first, rows, terms):
    step = 16

    @pl.loop(0, rows // step)
    def _(i):
        at = pl.ds(first + i * step, step)
        total = None
        for ref, ref_first in terms:
            part = ref[pl.ds(ref_first + i * step, step), :].astype(F32)
            total = part if total is None else total + part
        target[at, :] = total.astype(target.dtype)


def scatter_kernel(cores, part, out, side, ready, got_x, got_y, pass_x, pass_y, send, recv):
    x, y, c = (lax.axis_index(a) for a in PLANE)
    slot = c if cores == 2 else 0
    to_x, to_y, to_c = {"x": 1 - x}, {"y": 1 - y}, {"c": 1 - c}
    sems = (send, recv)
    rows = part.shape[2]
    half = rows // 2
    top, low = pl.ds(0, half), pl.ds(half, half)
    own, next_x = 2 * x + y, 2 * (1 - x) + y
    next_y, across = 2 * x + 1 - y, 2 * (1 - x) + 1 - y
    order = [across, next_x, next_y, own]
    meet([to_x, to_y] + ([to_c] if cores == 2 else []))
    from_side = []
    if cores == 2:
        for k, chip in enumerate(order):
            copy = remote(part.at[chip, 1 - c], side.at[k], sems, k, to_c)
            copy.start()
            from_side.append(copy)

    def terms(k, first):
        out_terms = [(part.at[order[k], slot], first)]
        if cores == 2:
            out_terms.append((side.at[k], first))
        return out_terms

    def arrived(k):
        if cores == 2:
            from_side[k].wait_recv()

    def launch(index, src, dst, device):
        copy = remote(src, dst, sems, index, device)
        copy.start()
        return copy

    arrived(0)
    add_rows(ready.at[0], 0, half, terms(0, 0))
    a_x = launch(4, ready.at[0, top], pass_x, to_x)
    add_rows(ready.at[0], half, half, terms(0, half))
    a_y = launch(5, ready.at[0, low], pass_y, to_y)
    arrived(1)
    add_rows(ready.at[1], 0, half, terms(1, 0))
    x_top = launch(6, ready.at[1, top], got_x.at[top], to_x)
    arrived(2)
    add_rows(ready.at[2], half, half, terms(2, half))
    y_low = launch(7, ready.at[2, low], got_y.at[low], to_y)
    a_y.wait_recv()
    add_rows(ready.at[1], half, half, terms(1, half) + [(pass_y, 0)])
    x_low = launch(8, ready.at[1, low], got_x.at[low], to_x)
    a_x.wait_recv()
    add_rows(ready.at[2], 0, half, terms(2, 0) + [(pass_x, 0)])
    y_top = launch(9, ready.at[2, top], got_y.at[top], to_y)
    arrived(3)
    x_top.wait_recv()
    y_low.wait_recv()
    x_low.wait_recv()
    y_top.wait_recv()
    add_rows(out, 0, rows, terms(3, 0) + [(got_x, 0), (got_y, 0)])
    for copy in from_side + [a_x, a_y, x_top, y_low, x_low, y_top]:
        copy.wait_send()


def scatter_rows(partial_rows, cores, ident):
    rows = partial_rows.shape[0] // (4 * cores)
    cols = partial_rows.shape[1]
    part = partial_rows.astype(BF16).reshape(4, cores, rows, cols)
    return pl.pallas_call(
        partial(scatter_kernel, cores),
        out_shape=jax.ShapeDtypeStruct((rows, cols), F32),
        in_specs=[IN_VMEM],
        out_specs=IN_VMEM,
        scratch_shapes=[
            pltpu.VMEM((4, rows if cores == 2 else 16, cols), BF16),
            pltpu.VMEM((3, rows, cols), BF16),
            pltpu.VMEM((rows, cols), BF16),
            pltpu.VMEM((rows, cols), BF16),
            pltpu.VMEM((rows // 2, cols), BF16),
            pltpu.VMEM((rows // 2, cols), BF16),
            pltpu.SemaphoreType.DMA((10,)),
            pltpu.SemaphoreType.DMA((10,)),
        ],
        compiler_params=pltpu.CompilerParams(
            collective_id=ident, has_side_effects=True, vmem_limit_bytes=VMEM_LIMIT
        ),
        name="scatter_rows",
    )(part)


def lanes(rows):
    return lax.broadcasted_iota(jnp.int32, (rows, LANES), 1)


def rotated(block, cosine, sine_signed):
    lane = lanes(block.shape[0])
    turned = jnp.where(
        lane % HEAD_DIM < HEAD_DIM // 2,
        pltpu.roll(block, LANES - HEAD_DIM // 2, 1),
        pltpu.roll(block, HEAD_DIM // 2, 1),
    )
    return block * cosine + turned * sine_signed


def key_spans(pieces, rows):
    reach = WINDOW // rows
    return [
        (max(0, 2 * j - reach) * rows, (2 * j + 2) * rows) for j in range(pieces // 2)
    ]


def seen(first_ref, place_ref, rows, low, high):
    keys = low + lax.broadcasted_iota(jnp.int32, (1, high - low), 1)
    return (keys >= first_ref[rows, :]) & (keys <= place_ref[rows, :])


def forward_kernel(
    spans, width, q_raw, k_raw, v_ref, cos_q, sin_q, cos_k, sin_k, first, place,
    q_out, k_out, ctx_out, lse_out, v_keep,
):
    valid = width - pl.program_id(0) * LANES
    k_rows = k_raw.shape[0]
    keep = lanes(k_rows) < valid
    k_out[...] = jnp.where(keep, rotated(k_raw[...], cos_k[...], sin_k[...]), 0.0).astype(BF16)
    v_keep[...] = jnp.where(keep, v_ref[...], jnp.zeros((), BF16))
    keep_q = lanes(q_raw.shape[0]) < valid
    q_out[...] = jnp.where(keep_q, rotated(q_raw[...], cos_q[...], sin_q[...]), 0.0).astype(BF16)
    rows_j = q_raw.shape[0] // len(spans)
    left = lanes(rows_j) < HEAD_DIM
    zero = jnp.zeros((), BF16)
    for j, (low, high) in enumerate(spans):
        rows = pl.ds(j * rows_j, rows_j)
        visible = seen(first, place, rows, low, high)
        query = q_out[rows, :]
        halves = []
        for side in range(2):
            mine = jnp.where(left if side == 0 else ~left, query, zero)
            scores = lax.dot_general(
                mine, k_out[low:high, :], (((1,), (1,)), ((), ())), preferred_element_type=F32
            )
            scores = jnp.where(visible, scores * 0.125, NEGATIVE)
            top = jnp.max(scores, -1, keepdims=True)
            grown = jnp.exp(scores - top)
            total = jnp.sum(grown, -1, keepdims=True)
            probs = (grown * (1.0 / total)).astype(BF16)
            ctx = jnp.dot(probs, v_keep[low:high, :], preferred_element_type=F32)
            halves.append((ctx, top + jnp.log(total)))
        ctx_out[rows, :] = jnp.where(left, halves[0][0], halves[1][0]).astype(BF16)
        lse_out[rows, :] = jnp.where(left, halves[0][1], halves[1][1])


def lane_block(rows):
    return pl.BlockSpec((rows, LANES), lambda p: (0, p))


def whole(rows, cols):
    return pl.BlockSpec((rows, cols), lambda p: (0, 0))


def attend_forward(q_raw, k_raw, value, tables, limits, pieces):
    q_rows, width = q_raw.shape
    k_rows = k_raw.shape[0]
    spans = key_spans(pieces, k_rows // pieces)
    steps = -(-width // LANES)
    shape = jax.ShapeDtypeStruct
    return pl.pallas_call(
        partial(forward_kernel, spans, width),
        grid=(steps,),
        out_shape=(
            shape((q_rows, width), BF16),
            shape((k_rows, width), BF16),
            shape((q_rows, width), BF16),
            shape((q_rows, width), F32),
        ),
        in_specs=[
            lane_block(q_rows),
            lane_block(k_rows),
            lane_block(k_rows),
            whole(q_rows, LANES),
            whole(q_rows, LANES),
            whole(k_rows, LANES),
            whole(k_rows, LANES),
            whole(q_rows, 1),
            whole(q_rows, 1),
        ],
        out_specs=(
            lane_block(q_rows),
            lane_block(k_rows),
            lane_block(q_rows),
            lane_block(q_rows),
        ),
        scratch_shapes=[pltpu.VMEM((k_rows, LANES), BF16)],
        compiler_params=pltpu.CompilerParams(vmem_limit_bytes=VMEM_LIMIT),
        name="attend_forward",
    )(q_raw, k_raw, value, *tables, *limits)


def backward_kernel(
    spans, width, q_ref, k_ref, v_ref, g_ref, lse, cos_q, sin_q, cos_k, sin_k, first, place,
    dq_out, dk_out, dv_out, k_keep, v_keep,
):
    valid = width - pl.program_id(0) * LANES
    zero = jnp.zeros((), BF16)
    keep = lanes(k_ref.shape[0]) < valid
    k_keep[...] = jnp.where(keep, k_ref[...], zero)
    v_keep[...] = jnp.where(keep, v_ref[...], zero)
    dk_out[...] = jnp.zeros_like(dk_out)
    dv_out[...] = jnp.zeros_like(dv_out)
    rows_j = q_ref.shape[0] // len(spans)
    lane = lanes(rows_j)
    left = (lane < HEAD_DIM) & (lane < valid)
    right = (lane >= HEAD_DIM) & (lane < valid)
    for j, (low, high) in enumerate(spans):
        rows = pl.ds(j * rows_j, rows_j)
        visible = seen(first, place, rows, low, high)
        query, grad = q_ref[rows, :], g_ref[rows, :]
        stats = lse[rows, :]
        halves = []
        for side in range(2):
            mask = left if side == 0 else right
            mine = jnp.where(mask, query, zero)
            grad_mine = jnp.where(mask, grad, zero)
            nt = (((1,), (1,)), ((), ()))
            tn = (((0,), (0,)), ((), ()))
            scores = lax.dot_general(mine, k_keep[low:high, :], nt, preferred_element_type=F32)
            column = side * HEAD_DIM
            log_total = stats[:, column : column + 1]
            probs = jnp.where(visible, jnp.exp(scores * 0.125 - log_total), 0.0)
            grad_probs = lax.dot_general(
                grad_mine, v_keep[low:high, :], nt, preferred_element_type=F32
            )
            mixed = probs * grad_probs
            delta = jnp.sum(mixed, -1, keepdims=True)
            grad_scores = (mixed - probs * delta).astype(BF16)
            halves.append(
                jnp.dot(grad_scores, k_keep[low:high, :], preferred_element_type=F32) * 0.125
            )
            dk_out[low:high, :] += (
                lax.dot_general(grad_scores, mine, tn, preferred_element_type=F32) * 0.125
            )
            dv_out[low:high, :] += lax.dot_general(
                probs.astype(BF16), grad_mine, tn, preferred_element_type=F32
            )
        grad_query = jnp.where(lane < HEAD_DIM, halves[0], halves[1])
        dq_out[rows, :] = rotated(grad_query, cos_q[rows, :], -sin_q[rows, :]).astype(BF16)
    dk_out[...] = rotated(dk_out[...], cos_k[...], -sin_k[...])


def attend_backward(query, key, value, grad, lse, tables, limits, pieces):
    q_rows, width = query.shape
    k_rows = key.shape[0]
    spans = key_spans(pieces, k_rows // pieces)
    steps = -(-width // LANES)
    shape = jax.ShapeDtypeStruct
    return pl.pallas_call(
        partial(backward_kernel, spans, width),
        grid=(steps,),
        out_shape=(
            shape((q_rows, width), BF16),
            shape((k_rows, width), F32),
            shape((k_rows, width), F32),
        ),
        in_specs=[
            lane_block(q_rows),
            lane_block(k_rows),
            lane_block(k_rows),
            lane_block(q_rows),
            lane_block(q_rows),
            whole(q_rows, LANES),
            whole(q_rows, LANES),
            whole(k_rows, LANES),
            whole(k_rows, LANES),
            whole(q_rows, 1),
            whole(q_rows, 1),
        ],
        out_specs=(lane_block(q_rows), lane_block(k_rows), lane_block(k_rows)),
        scratch_shapes=[pltpu.VMEM((k_rows, LANES), BF16)] * 2,
        compiler_params=pltpu.CompilerParams(vmem_limit_bytes=VMEM_LIMIT),
        name="attend_backward",
    )(query, key, value, grad, lse, *tables, *limits)


def norm_back(grad_normed, unit_rows, rms_rows, gain_rows):
    scaled = grad_normed * gain_rows
    return rms_rows * (scaled - unit_rows * jnp.mean(scaled * unit_rows, -1, keepdims=True))


def on_device(
    tokens,
    doc_lengths,
    cotangent,
    attn_gain,
    w_query,
    w_key,
    w_value,
    w_out,
    mlp_gain,
    w_gate,
    w_up,
    w_down,
):
    outer = lax.axis_size("g")
    pieces_z = lax.axis_size("z")
    x, y, c = (lax.axis_index(a) for a in PLANE)
    own = 2 * y + c

    def joined(shard):
        if outer == 1:
            return shard
        return lax.all_gather(shard, "g", axis=0, tiled=True)

    w_query, w_key, w_value, w_out = map(joined, (w_query, w_key, w_value, w_out))
    w_gate, w_up, w_down = map(joined, (w_gate, w_up, w_down))
    rows_d = w_query.shape[0]
    model = w_query.shape[1]
    tok_rows = tokens.shape[1]
    pieces = 2 * pieces_z
    seq_len = pieces * tok_rows
    cols_h = model // 4
    cols_f = w_gate.shape[1] // 8

    turn_pairs = [
        (i * pieces_z + z, z * pieces_z + i) for i in range(pieces_z) for z in range(pieces_z)
    ]

    def turned(block):
        return lax.ppermute(block, ("y", "c", "z"), turn_pairs)

    gains = lax.all_gather(
        jnp.stack([joined(attn_gain), joined(mlp_gain)]), ("y", "c"), axis=1, tiled=True
    ).astype(F32)
    gain_one, gain_two = gains[0:1], gains[1:2]
    lengths = turned(doc_lengths)[0]
    inputs = turned(tokens[0]).astype(F32)
    upstream = turned(cotangent[0]).astype(F32)

    def head_cols(weight, group):
        return lax.dynamic_slice_in_dim(weight, group * cols_h, cols_h, 1)

    def qkv_cols(group):
        return jnp.concatenate([head_cols(w, group) for w in (w_query, w_key, w_value)], 1)

    qkv_own = qkv_cols(2 * y + x)
    qkv_far = swap(qkv_cols(2 * (1 - y) + x), "y")
    qkv_pair = jnp.where(y == 0, jnp.stack([qkv_own, qkv_far]), jnp.stack([qkv_far, qkv_own]))
    qkv_side = swap(qkv_pair, "c")
    w_qkv = jnp.where(
        c == 0, jnp.stack([qkv_pair, qkv_side], 1), jnp.stack([qkv_side, qkv_pair], 1)
    ).reshape(4 * rows_d, 3 * cols_h)
    out_side = swap(w_out, "c")
    w_out_use = jnp.where(c == x, w_out, out_side)

    def ff_cols(dest):
        first = (2 * dest + x) * cols_f
        return jnp.concatenate(
            [lax.dynamic_slice_in_dim(w, first, cols_f, 1) for w in (w_gate, w_up)], 1
        )

    ff_own = ff_cols(own)
    ff_c = swap(ff_cols(2 * y + 1 - c), "c")
    ff_y = swap(ff_cols(2 * (1 - y) + c), "y")
    ff_yc = lax.ppermute(
        ff_cols(2 * (1 - y) + 1 - c), ("y", "c"), [(i, 3 - i) for i in range(4)]
    )

    def ordered(a, b, flag):
        return jnp.where(flag == 0, jnp.stack([a, b]), jnp.stack([b, a]))

    ff_near = ordered(ff_own, ff_c, c)
    ff_far = ordered(ff_y, ff_yc, c)
    w_ff = ordered(ff_near, ff_far, y).reshape(4 * rows_d, 2 * cols_f)
    down_use = lax.dynamic_slice_in_dim(w_down, x * cols_f, cols_f, 0)

    place = jnp.arange(seq_len, dtype=jnp.int32)
    docs, offset = layout(lengths, place)
    cosine, sine_table = rope_tables(offset)

    def own_rows(array):
        cols = array.shape[1:]
        split = array.reshape((pieces // 2, 2, tok_rows) + cols)
        return lax.dynamic_index_in_dim(split, c, 1, keepdims=False).reshape(
            (seq_len // 2,) + cols
        )

    def other_rows(array):
        cols = array.shape[1:]
        split = array.reshape((pieces // 2, 2, tok_rows) + cols)
        return lax.dynamic_index_in_dim(split, 1 - c, 1, keepdims=False).reshape(
            (seq_len // 2,) + cols
        )

    tables = (own_rows(cosine), own_rows(sine_table), cosine, sine_table)
    first_key = jnp.maximum(place - offset, place - (WINDOW - 1))
    limits = (own_rows(first_key)[:, None], own_rows(place)[:, None])

    grad_mlp = lax.all_gather((BETA * upstream).astype(BF16), PLANE, axis=0, tiled=True)

    rms_one = lax.rsqrt(jnp.mean(inputs * inputs, -1, keepdims=True) + EPSILON)
    unit_one = inputs * rms_one
    normed_one = gather_rows((unit_one * gain_one).astype(BF16), 2, 1)

    query_raw = dot(own_rows(normed_one), w_qkv[:, :cols_h])
    key_raw = dot(normed_one, w_qkv[:, cols_h : 2 * cols_h])
    value = dot(normed_one, w_qkv[:, 2 * cols_h :]).astype(BF16)
    query, key, context, lse = attend_forward(query_raw, key_raw, value, tables, limits, pieces)

    attn_out = scatter_rows(dot(context, w_out_use), 1, 2)
    hidden_res = inputs + BETA * attn_out
    rms_two = lax.rsqrt(jnp.mean(hidden_res * hidden_res, -1, keepdims=True) + EPSILON)
    unit_two = hidden_res * rms_two
    normed_two = gather_rows((unit_two * gain_two).astype(BF16), 2, 3)

    gate_up = dot(normed_two, w_ff)
    gate, up = gate_up[:, :cols_f], gate_up[:, cols_f:]
    sigmoid_gate = jax.nn.sigmoid(gate)
    silu_gate = gate * sigmoid_gate
    activation = (silu_gate * up).astype(BF16)
    mlp_out = lax.psum_scatter(
        dot(activation, down_use).astype(BF16), PLANE, scatter_dimension=0, tiled=True
    ).astype(F32)
    output = turned((hidden_res + BETA * mlp_out).astype(BF16))[None]

    grad_activation = dot_nt(grad_mlp, down_use)
    grad_up = (grad_activation * silu_gate).astype(BF16)
    grad_gate = (
        grad_activation * up * (sigmoid_gate * (1.0 + gate * (1.0 - sigmoid_gate)))
    ).astype(BF16)
    grad_ff = jnp.concatenate([grad_gate, grad_up], 1)
    grad_normed_two = scatter_rows(dot_nt(grad_ff, w_ff), 2, 4)

    def summed_z(grad):
        part = lax.psum_scatter(grad.astype(BF16), "z", scatter_dimension=0, tiled=True)
        return lax.all_gather(part, "z", axis=0, tiled=True)

    grad_down = summed_z(dot_tn(activation, grad_mlp))
    grad_ff_side = swap(grad_ff, "c")
    grad_ff_chip = jnp.concatenate(
        [
            jnp.where(c == 0, grad_ff, grad_ff_side),
            jnp.where(c == 0, grad_ff_side, grad_ff),
        ],
        1,
    )

    def row_block(normed, y_of):
        return lax.dynamic_slice_in_dim(normed, (2 * y_of + c) * rows_d, rows_d, 1)

    def row_grads(normed, grads):
        near = dot_tn(row_block(normed, y), grads).astype(BF16)
        far = dot_tn(row_block(normed, 1 - y), grads).astype(BF16)
        return (near, far)

    grad_ff_w = [summed_z(g) for g in row_grads(normed_two, grad_ff_chip)]

    gain_grad_two = jnp.sum(grad_normed_two * unit_two, 0)
    grad_hidden = upstream + norm_back(grad_normed_two, unit_two, rms_two, gain_two)
    grad_attn = gather_rows((BETA * grad_hidden).astype(BF16), 1, 5)
    grad_context = dot_nt(grad_attn, w_out_use).astype(BF16)

    grad_out_part = dot_tn(context, grad_attn).astype(BF16)
    half = model // 2
    keep = lax.dynamic_slice_in_dim(grad_out_part, c * half, half, 1)
    give = lax.dynamic_slice_in_dim(grad_out_part, (1 - c) * half, half, 1)
    grad_out_half = summed_z(keep.astype(F32) + swap(give, "c").astype(F32))

    grad_query, grad_key, grad_value = attend_backward(
        query, key, value, grad_context, lse, tables, limits, pieces
    )
    grad_kv = jnp.concatenate([grad_key, grad_value], 1)
    grad_kv = own_rows(grad_kv) + swap(other_rows(grad_kv).astype(BF16), "c").astype(F32)
    grad_key = grad_kv[:, :cols_h].astype(BF16)
    grad_value = grad_kv[:, cols_h:].astype(BF16)
    grad_qkv = jnp.concatenate([grad_query, grad_key, grad_value], 1)

    grad_normed_one = scatter_rows(dot_nt(grad_qkv, w_qkv), 1, 6)
    grad_qkv_side = swap(grad_qkv, "c")
    grad_qkv_all = (
        jnp.where(
            c == 0,
            jnp.stack([grad_qkv, grad_qkv_side]),
            jnp.stack([grad_qkv_side, grad_qkv]),
        )
        .reshape(2, pieces // 2, tok_rows, 3 * cols_h)
        .transpose(1, 0, 2, 3)
        .reshape(seq_len, 3 * cols_h)
    )
    grad_qkv_w = [summed_z(g) for g in row_grads(normed_one, grad_qkv_all)]

    gain_grad_one = jnp.sum(grad_normed_one * unit_one, 0)
    grad_inputs = grad_hidden + norm_back(grad_normed_one, unit_one, rms_one, gain_one)
    grad_tokens = turned(grad_inputs.astype(BF16))[None]

    gain_grads = lax.psum(jnp.stack([gain_grad_one, gain_grad_two]), ("x", "y", "c", "g", "z"))
    shard = attn_gain.shape[0]
    first = own * rows_d + lax.axis_index("g") * shard
    gain_grads = lax.dynamic_slice_in_dim(gain_grads, first, shard, 1)

    def finish(grad):
        if outer > 1:
            grad = lax.psum_scatter(grad, "g", scatter_dimension=0, tiled=True)
        return grad.astype(F32)

    def owner_rows(pair):
        near, far = pair[0], swap(pair[1], "y")
        both = ordered(near, far, y)
        return lax.all_gather(both, "x", axis=0, tiled=False)

    ff_all = owner_rows(grad_ff_w)
    ff_all = [
        jnp.concatenate(
            [
                ff_all[i, j, :, (2 * k + kind) * cols_f : (2 * k + kind + 1) * cols_f]
                for j in range(2)
                for k in range(2)
                for i in range(2)
            ],
            1,
        )
        for kind in range(2)
    ]
    qkv_all = owner_rows(grad_qkv_w)
    qkv_all = [
        jnp.concatenate(
            [
                qkv_all[i, j, :, kind * cols_h : (kind + 1) * cols_h]
                for j in range(2)
                for i in range(2)
            ],
            1,
        )
        for kind in range(3)
    ]
    down_all = lax.all_gather(grad_down, "x", axis=0, tiled=True)
    out_near = lax.all_gather(grad_out_half, "c", axis=1, tiled=True)
    out_far = lax.ppermute(out_near, ("x", "c"), [(0, 2), (3, 1)])
    out_all = jnp.where(c == x, out_near, out_far)

    return (
        output,
        grad_tokens,
        gain_grads[0],
        finish(qkv_all[0]),
        finish(qkv_all[1]),
        finish(qkv_all[2]),
        finish(out_all),
        gain_grads[1],
        finish(ff_all[0]),
        finish(ff_all[1]),
        finish(down_all),
    )


def solution(mesh):
    seq, fsdp, rep = (mesh.shape[a] for a in ("seq", "fsdp", "rep"))
    inner = Mesh(
        mesh.devices.reshape(seq, rep // 2, 2, fsdp // rep, rep), ("x", "y", "c", "g", "z")
    )
    owners = ("y", "c", "g")
    token_spec = P(owners, ("x", "z"), None)
    placed = (token_spec, P(owners, None), token_spec, P(owners)) + (P(owners, None),) * 4
    placed = placed + (P(owners),) + (P(owners, None),) * 3
    return jax.shard_map(
        on_device,
        mesh=inner,
        in_specs=placed,
        out_specs=(token_spec, token_spec, P(owners))
        + (P(owners, None),) * 4
        + (P(owners),)
        + (P(owners, None),) * 3,
        check_vma=False,
    )
```

time: 2920 us -> 1980 us (0.68)
  waiting for transfers between devices: 2260 us -> 609 us
  Pallas kernels: 0 us -> 446 us
  blocking collectives: 47.4 us -> 351 us
  matrix products: 346 us -> 195 us
  local copies, waits for them, and re-layouts: 82.5 us -> 141 us
  other arithmetic: 110 us -> 168 us
    psum x1 -> x0, waiting for transfers between devices: 833 us -> none  [on_device(): lax.psum(grad_w_query.astype(jnp.bfloat16), ('seq', 'rep'))]
    reduce_scatter x7 -> x6, waiting for transfers between devices: 682 us -> 67.3 us  [the longest x5 67.3 us: summed_z(): lax.psum_scatter(grad.astype(BF16), 'z', scatter_dimension=0, tiled=True)]
    pallas_call x0 -> x8, Pallas kernels: none -> 446 us  [the longest x3 187 us: scatter_rows(): pl.pallas_call(partial(scatter_kernel, cores), out_shape=jax.ShapeDtypeSt...]
    ppermute x16 -> x18, waiting for transfers between devices: 224 us -> 52.5 us  [the longest x5 40.3 us: turned(): return lax.ppermute(block, ('y', 'c', 'z'), turn_pairs)]
    dot_general x42 -> x16, matrix products: 346 us -> 195 us  [the longest x6 68.7 us: dot_tn(): lax.dot_general(left, right, (((0,), (0,)), ((), ())), preferred_element_...]
    all_gather x0 -> x1, blocking collectives: none -> 126 us  [on_device(): lax.all_gather(jnp.stack([joined(attn_gain), joined(mlp_gain)]), ('y', 'c...]
    psum x1, blocking collectives: 23.9 us -> 117 us  [on_device(): lax.psum(jnp.stack([gain_grad_one, gain_grad_two]), ('x', 'y', 'c', 'g',...]
    unnamed x2 -> x1, blocking collectives: 23.5 us -> 108 us
  transfers between devices with their start and end apart: 31 -> 36, of which waited for: 21 -> 14; matrix products, arithmetic and copies ran while one was open for 15% -> 24% of each run, Pallas kernels for 0% -> 15%
where the time goes in v1:
time: 1980 us; the launch traced here: 1970 us
  waiting for transfers between devices  609 us (31%)
  Pallas kernels  446 us (23%)
  blocking collectives  351 us (18%)
  matrix products  195 us (10%)
  other arithmetic  168 us (8%)
  local copies, waits for them, and re-layouts  141 us (7%)
  starting transfers between devices  44.5 us (2%)
    all_gather x6, waiting for transfers between devices, summed_z(): return lax.all_gather(part, 'z', axis=0, tiled=True)  307 us
    pallas_call x3, Pallas kernels, scatter_rows(): pl.pallas_call(partial(scatter_kernel, cores), out_shape=jax.ShapeDtypeSt...  187 us
    all_gather x2, waiting for transfers between devices, owner_rows(): return lax.all_gather(both, 'x', axis=0, tiled=False)  178 us
    pallas_call x3, Pallas kernels, gather_rows(): pl.pallas_call(partial(gather_kernel, cores), out_shape=jax.ShapeDtypeStr...  160 us
    all_gather x1, blocking collectives, on_device(): lax.all_gather(jnp.stack([joined(attn_gain), joined(mlp_gain)]), ('y', 'c...  126 us
    psum x1, blocking collectives, on_device(): lax.psum(jnp.stack([gain_grad_one, gain_grad_two]), ('x', 'y', 'c', 'g',...  117 us
    unnamed x1, blocking collectives  108 us
    dot_general x6, matrix products, dot_tn(): lax.dot_general(left, right, (((0,), (0,)), ((), ())), preferred_element_...  68.7 us
  transfers between devices with their start and end apart: 36, of which 14 were waited for; matrix products, arithmetic and copies ran while one was open for 24% of the time, Pallas kernels for 15%

profile of v1, /device:TPU:4, one launch (start us, length us, event | category | flops | bytes accessed | tf_op | source)
XLA Modules:
  0.0 1971.2 jit_solution(7441990280503876587)
XLA Ops:
  25.5 8.9 constant_dynamic-slice_fusion.8
  40.7 126.0 %all-gather = bf16[4,576,2]{1,2,0:T(2,128)(2,1)S(1)} all-gather(bf16[1,576,2]{1,2,0:T(2,128)(2,1)S(1)} %maximum_bitcast_fusion.1), channel_id=1, replica_groups=mesh['x'=2,'y'=2,'c'=2,'g'=1,'z'=4] {'y','c'}, dimensions={0}, use_global_device_ids=true | all-gather | bytes 11520 | tf_op jit(solution)/shard_map/all_gather | solution.py:505
  178.8 5.7 multiply_sine_fusion.1
  190.8 40.3 %collective-permute-done.9 = bf16[256,2304]{1,0:T(8,128)(2,1)} collective-permute-done((bf16[256,2304]{1,0:T(8,128)(2,1)}, bf16[256,2304]{1,0:T(8,128)(2,1)}, u32[]{:S(2)}, u32[]{:S(2)}) %collective-permute-start.9) | collective-permute-done | bytes 1179680 | tf_op jit(solution)/shard_map/ppermute | solution.py:503
  241.0 4.6 maximum_select_fusion.5
  247.4 73.4 %gather_rows.3 = bf16[4,2,256,2304]{3,2,1,0:T(8,128)(2,1)} custom-call(bf16[256,2304]{1,0:T(8,128)(2,1)} %fusion.23.block), custom_call_target="tpu_custom_call" | custom-call | tf_op jit(solution)/shard_map/gather_rows/pallas_call | solution.py:149
  320.9 4.8 constant_dynamic-slice_fusion.19
  338.5 7.9 maximum_select_fusion
  346.5 7.3 copy.85
  353.8 12.9 fusion.11.k_raw
  366.7 5.3 fusion.13.q_raw
  372.1 8.9 convolution_convert_fusion.6.v_ref
  381.0 42.9 %attend_forward.1 = (bf16[1024,576]{1,0:T(8,128)(2,1)}, bf16[2048,576]{1,0:T(8,128)(2,1)}, bf16[1024,576]{1,0:T(8,128)(2,1)}, f32[1024,576]{1,0:T(8,128)}) custom-call(f32[1024,576]{1,0:T(8,128)} %fusion.13.q_raw, f32[2048,576]{1,0:T(8,128)} %fusion.11.k_raw, bf16[2048,576]{1,0:T(8,128)(2,1)} %convolution_convert_fusion.6.v_ref, f32[1024,128]{1,0:T(8,128)} %bitcast.160, ...), custom_call_target="tpu_custom_call" | custom-call | tf_op jit(solution)/shard_map/attend_forward/pallas_call | solution.py:342
  423.9 8.2 convolution_convert_fusion.3
  432.1 46.6 %scatter_rows.3 = f32[256,2304]{1,0:T(8,128)} custom-call(bf16[4,1,256,2304]{3,2,1,0:T(8,128)(2,1)} %bitcast.168), custom_call_target="tpu_custom_call" | custom-call | tf_op jit(solution)/shard_map/scatter_rows/pallas_call | solution.py:245
  482.3 44.5 %gather_rows.4 = bf16[4,2,256,2304]{3,2,1,0:T(8,128)(2,1)} custom-call(bf16[256,2304]{1,0:T(8,128)(2,1)} %multiply_convert_fusion.4.block), custom_call_target="tpu_custom_call" | custom-call | tf_op jit(solution)/shard_map/gather_rows/pallas_call | solution.py:149
  526.8 20.1 %fusion.50 = f32[2048,1440]{0,1:T(8,128)} fusion(bf16[2048,2304]{1,0:T(8,128)(2,1)} %bitcast.145, bf16[2304,1440]{1,0:T(8,128)(2,1)} %bitcast.156), kind=kOutput, calls=%fused_computation.180 | convolution fusion | flops 13589544960 | bytes 27869184 | tf_op jit(solution)/shard_map/dot_general | solution.py:27
  546.9 16.8 multiply_convert_fusion.1
  563.7 21.2 %convolution_convert_fusion = bf16[2048,2304]{1,0:T(8,128)(2,1)} fusion(bf16[2304,1440]{1,0:T(8,128)(2,1)} %bitcast.157, bf16[2048,720]{0,1:T(8,128)(2,1)S(1)} %get-tuple-element.38, bf16[2048,720]{0,1:T(8,128)(2,1)S(1)} %get-tuple-element.37), kind=kOutput, calls=%fused_computation.1 | convolution fusion | flops 13606060032 | bytes 21970944 | tf_op jit(solution)/shard_map/dot_general | solution.py:35
  584.9 49.9 %scatter_rows.4 = f32[256,2304]{1,0:T(8,128)} custom-call(bf16[4,2,256,2304]{3,2,1,0:T(8,128)(2,1)} %bitcast.148), custom_call_target="tpu_custom_call" | custom-call | tf_op jit(solution)/shard_map/scatter_rows/pallas_call | solution.py:245
  641.0 42.0 %gather_rows.5 = bf16[4,1,256,2304]{3,2,1,0:T(8,128)(2,1)} custom-call(bf16[256,2304]{1,0:T(8,128)(2,1)} %multiply_convert_fusion.3.block), custom_call_target="tpu_custom_call" | custom-call | tf_op jit(solution)/shard_map/gather_rows/pallas_call | solution.py:149
  683.0 6.1 convolution_convert_fusion.9
  690.5 56.4 %attend_backward.1 = (bf16[1024,576]{1,0:T(8,128)(2,1)}, f32[2048,576]{1,0:T(8,128)}, f32[2048,576]{1,0:T(8,128)}) custom-call(bf16[1024,576]{1,0:T(8,128)(2,1)} %get-tuple-element.19.q_ref, bf16[2048,576]{1,0:T(8,128)(2,1)} %get-tuple-element.20.k_ref, bf16[2048,576]{1,0:T(8,128)(2,1)} %convolution_convert_fusion.6.v_ref, bf16[1024,576]{1,0:T(8,128)(2,1)} %copy.93.g_ref, ...), custom_call_target="tpu_custom_call" | custom-call | tf_op jit(solution)/shard_map/attend_backward/pallas_call | solution.py:431
  746.9 9.4 pad_maximum_fusion.1
  761.9 4.8 constant_dynamic-slice_fusion.1
  766.7 6.0 copy.106
  780.6 5.3 convolution_convert_fusion.5
  795.4 6.3 pad_maximum_fusion.4
  805.8 5.8 copy.109
  811.6 7.2 maximum_select_fusion.1
  821.8 8.2 convolution_convert_fusion.7
  830.2 10.4 convolution_convert_fusion.8
  840.7 12.5 broadcast_select_fusion.1
  853.2 16.2 fusion.5
  870.0 16.5 fusion.4
  886.5 12.1 convolution_convert_fusion.4
  898.7 107.9 %fusion = bf16[184,2304]{1,0:T(8,128)(2,1)S(1)} fusion(bf16[720,2304]{1,0:T(8,128)(2,1)} %convolution_convert_fusion.4), kind=kCustom, calls=%all-reduce-scatter | all-reduce-scatter fusion | flops 1695745 | bytes 4166144
  1006.6 14.5 collective-permute-start.18
  1029.1 67.2 %reduce-scatter.17.cloned.1.call-done = bf16[144,2880]{1,0:T(8,128)(2,1)} async-done(((bf16[576,2880]{1,0:T(8,128)(2,1)}), bf16[144,2880]{1,0:T(8,128)(2,1)}) %reduce-scatter.17.cloned.1.call-update) | async-done | bytes 829456 | tf_op jit(solution)/shard_map/reduce_scatter | solution.py:608
  1096.4 34.7 %all-gather.22.cloned.1.call-done = bf16[576,1152]{1,0:T(8,128)(2,1)} async-done(((bf16[144,1152]{1,0:T(8,128)(2,1)}), bf16[576,1152]{1,0:T(8,128)(2,1)}) %all-gather.22.cloned.1.call-update) | async-done | bytes 1327120 | tf_op jit(solution)/shard_map/all_gather | solution.py:609
  1131.1 12.0 convolution_convert_fusion.1
  1143.2 56.6 %all-gather.34.cloned.1.call-done = bf16[4,180,2304]{2,1,0:T(8,128)(2,1)} async-done(((bf16[1,180,2304]{2,1,0:T(8,128)(2,1)}), bf16[4,180,2304]{2,1,0:T(8,128)(2,1)}) %all-gather.34.cloned.1.call-update) | async-done | bytes 3317776 | tf_op jit(solution)/shard_map/all_gather | solution.py:609
  1203.3 41.9 %all-gather.18.cloned.1.call-done = bf16[576,1728]{1,0:T(8,128)(2,1)} async-done(((bf16[144,1728]{1,0:T(8,128)(2,1)}), bf16[576,1728]{1,0:T(8,128)(2,1)}) %all-gather.18.cloned.1.call-update) | async-done | bytes 1990672 | tf_op jit(solution)/shard_map/all_gather | solution.py:609
  1245.8 44.9 %all-gather.16.cloned.1.call-done = bf16[576,1728]{1,0:T(8,128)(2,1)} async-done(((bf16[144,1728]{1,0:T(8,128)(2,1)}), bf16[576,1728]{1,0:T(8,128)(2,1)}) %all-gather.16.cloned.1.call-update) | async-done | bytes 1990672 | tf_op jit(solution)/shard_map/all_gather | solution.py:609
  1296.7 61.9 %all-gather.28.cloned.1.call-done = bf16[576,2880]{1,0:T(8,128)(2,1)} async-done(((bf16[144,2880]{1,0:T(8,128)(2,1)}), bf16[576,2880]{1,0:T(8,128)(2,1)}) %all-gather.28.cloned.1.call-update) | async-done | bytes 3317776 | tf_op jit(solution)/shard_map/all_gather | solution.py:609
  1359.2 67.1 %all-gather.26.cloned.1.call-done = bf16[576,2880]{1,0:T(8,128)(2,1)} async-done(((bf16[144,2880]{1,0:T(8,128)(2,1)}), bf16[576,2880]{1,0:T(8,128)(2,1)}) %all-gather.26.cloned.1.call-update) | async-done | bytes 3317776 | tf_op jit(solution)/shard_map/all_gather | solution.py:609
  1426.3 7.6 collective-permute-done.17
  1433.9 7.7 maximum_select_fusion.3
  1443.0 4.8 collective-permute-start.15
  1447.8 15.2 convolution_convert_fusion.2
  1463.0 90.5 %scatter_rows.5 = f32[256,2304]{1,0:T(8,128)} custom-call(bf16[4,1,256,2304]{3,2,1,0:T(8,128)(2,1)} %bitcast.167), custom_call_target="tpu_custom_call" | custom-call | tf_op jit(solution)/shard_map/scatter_rows/pallas_call | solution.py:245
  1557.4 5.6 fusion.28
  1565.3 5.3 collective-permute-start.11
  1570.7 116.9 %psum.7 = f32[2,2304]{1,0:T(2,128)S(1)} all-reduce(f32[2,2304]{1,0:T(2,128)S(1)} %pad_maximum_fusion.15), channel_id=1, replica_groups=mesh['x'=2,'y'=2,'c'=2,'g'=1,'z'=4] {'x','y','c','g','z'}, use_global_device_ids=true, to_apply=%region_10.11 | all-reduce | flops 4608 | bytes 36864 | tf_op jit(solution)/shard_map/psum | solution.py:669
  1692.8 8.9 convert_element_type.169
  1701.7 41.5 %all-gather.20.cloned.1.call-done = bf16[2,2,576,1728]{3,2,1,0:T(8,128)(2,1)} async-done(((bf16[1,2,576,1728]{3,2,1,0:T(8,128)(2,1)}), bf16[2,2,576,1728]{3,2,1,0:T(8,128)(2,1)}) %all-gather.20.cloned.1.call-update) | async-done | bytes 7962640 | tf_op jit(solution)/shard_map/all_gather | solution.py:682
  1743.2 6.2 slice_bitcast_fusion.16
  1757.7 4.6 concatenate.143
  1772.1 136.4 %all-gather.30.cloned.1.call-done = bf16[2,2,576,2880]{3,2,1,0:T(8,128)(2,1)} async-done(((bf16[1,2,576,2880]{3,2,1,0:T(8,128)(2,1)}), bf16[2,2,576,2880]{3,2,1,0:T(8,128)(2,1)}) %all-gather.30.cloned.1.call-update) | async-done | bytes 13271056 | tf_op jit(solution)/shard_map/all_gather | solution.py:682
  1908.5 12.0 slice_bitcast_fusion
  1920.5 12.5 concatenate.146
  1932.9 8.8 convert_element_type.166
  1941.8 11.7 concatenate.147
  1953.4 9.0 convert_element_type.167
  (240 shorter events, 159.7 us)
Async XLA Ops:
  7.2 539.7 %all-gather.14.cloned.1.call-start = ((), (), s32[]{:S(2)}) async-start(), calls=%async_computation.7 | async-start | bytes 10616832 | tf_op jit(solution)/shard_map/all_gather | solution.py:572
  7.2 238.4 %collective-permute-start = (bf16[256,2304]{1,0:T(8,128)(2,1)}, bf16[256,2304]{1,0:T(8,128)(2,1)S(1)}, u32[]{:S(2)}, u32[]{:S(2)}) collective-permute-start(bf16[256,2304]{1,0:T(8,128)(2,1)} %bitcast.180), channel_id=1, source_target_pairs={{0,0},{1,4},{2,8},{3,12},{4,1},{5,5},{6,9},{7,13},{8,2},{9,6},{10,... | collective-permute-start | bytes 3538952 | tf_op jit(solution)/shard_map/ppermute | solution.py:503
  22.1 218.4 %collective-permute-start.1 = (bf16[576,1728]{1,0:T(8,128)(2,1)}, bf16[576,1728]{1,0:T(8,128)(2,1)}, u32[]{:S(2)}, u32[]{:S(2)}) collective-permute-start(bf16[576,1728]{1,0:T(8,128)(2,1)} %concatenate.130), channel_id=1, source_target_pairs={{0,8},{8,0},{1,9},{9,1},{2,10},{10,2},{3,11},{11,3},{4,12},{12,4},... | collective-permute-start | bytes 5971976 | tf_op jit(solution)/shard_map/ppermute | solution.py:39
  22.1 153.5 %collective-permute-start.3 = (s32[1,4]{1,0:T(1,128)S(1)}, s32[1,4]{1,0:T(1,128)S(1)}, u32[]{:S(2)}, u32[]{:S(2)}) collective-permute-start(s32[1,4]{1,0:T(1,128)S(1)} %copy-done.37), channel_id=1, source_target_pairs={{0,0},{1,4},{2,8},{3,12},{4,1},{5,5},{6,9},{7,13},{8,2},{9,6},{10,... | collective-permute-start | bytes 56 | tf_op jit(solution)/shard_map/ppermute | solution.py:503
  34.4 6.3 copy-start.33
  34.4 6.3 copy-start.34
  36.1 289.6 %collective-permute-start.7 = (bf16[576,1440]{1,0:T(8,128)(2,1)}, bf16[576,1440]{1,0:T(8,128)(2,1)}, u32[]{:S(2)}, u32[]{:S(2)}) collective-permute-start(bf16[576,1440]{1,0:T(8,128)(2,1)} %pad_maximum_fusion.12), channel_id=1, source_target_pairs={{0,12},{4,8},{8,4},{12,0},{1,13},{5,9},{9,5},{13,1},{2,14},{6,10},... | collective-permute-start | bytes 4976648 | tf_op jit(solution)/shard_map/ppermute | solution.py:538
  38.8 286.9 %collective-permute-start.6 = (bf16[576,1440]{1,0:T(8,128)(2,1)}, bf16[576,1440]{1,0:T(8,128)(2,1)}, u32[]{:S(2)}, u32[]{:S(2)}) collective-permute-start(bf16[576,1440]{1,0:T(8,128)(2,1)} %pad_maximum_fusion.11), channel_id=1, source_target_pairs={{0,8},{8,0},{1,9},{9,1},{2,10},{10,2},{3,11},{11,3},{4,12},{12,4},... | collective-permute-start | bytes 4976648 | tf_op jit(solution)/shard_map/ppermute | solution.py:39
  166.9 79.1 %copy-start.23 = (f32[2304]{0:T(1024)}, f32[2304]{0:T(1024)S(1)}, u32[]{:S(2)}) copy-start(f32[2304]{0:T(1024)S(1)} %get-tuple-element.32) | copy-start | bytes 27652
  166.9 471.0 %copy-start.21 = (f32[2304]{0:T(1024)}, f32[2304]{0:T(1024)S(1)}, u32[]{:S(2)}) copy-start(f32[2304]{0:T(1024)S(1)} %get-tuple-element.31) | copy-start | bytes 27652
  175.6 55.6 %collective-permute-start.9 = (bf16[256,2304]{1,0:T(8,128)(2,1)}, bf16[256,2304]{1,0:T(8,128)(2,1)}, u32[]{:S(2)}, u32[]{:S(2)}) collective-permute-start(bf16[256,2304]{1,0:T(8,128)(2,1)} %bitcast.179), channel_id=1, source_target_pairs={{0,0},{1,4},{2,8},{3,12},{4,1},{5,5},{6,9},{7,13},{8,2},{9,6},{10,... | collective-permute-start | bytes 3538952 | tf_op jit(solution)/shard_map/ppermute | solution.py:503
  231.2 98.2 %collective-permute-start.5 = (bf16[576,1440]{1,0:T(8,128)(2,1)}, bf16[576,1440]{1,0:T(8,128)(2,1)}, u32[]{:S(2)}, u32[]{:S(2)}) collective-permute-start(bf16[576,1440]{1,0:T(8,128)(2,1)} %pad_maximum_fusion.10), channel_id=1, source_target_pairs={{0,4},{4,0},{1,5},{5,1},{2,6},{6,2},{3,7},{7,3},{8,12},{12,8},{9,1... | collective-permute-start | bytes 4976648 | tf_op jit(solution)/shard_map/ppermute | solution.py:39
  233.7 664.9 %reduce-scatter.15.cloned.1.call-start = ((), (), s32[]{:S(2)}) async-start(), calls=%async_computation.13 | async-start | bytes 1658880 | tf_op jit(solution)/shard_map/reduce_scatter | solution.py:608
  240.5 183.4 %collective-permute-start.4 = (bf16[576,2304]{1,0:T(8,128)(2,1)}, bf16[576,2304]{1,0:T(8,128)(2,1)}, u32[]{:S(2)}, u32[]{:S(2)}) collective-permute-start(bf16[576,2304]{1,0:T(8,128)(2,1)} %param.19), channel_id=1, source_target_pairs={{0,4},{4,0},{1,5},{5,1},{2,6},{6,2},{3,7},{7,3},{8,12},{12,8},{9,1... | collective-permute-start | bytes 7962632 | tf_op jit(solution)/shard_map/ppermute | solution.py:39
  245.6 233.1 %copy-start.3 = (bf16[256,2304]{1,0:T(8,128)(2,1)}, bf16[256,2304]{1,0:T(8,128)(2,1)S(1)}, u32[]{:S(2)}) copy-start(bf16[256,2304]{1,0:T(8,128)(2,1)S(1)} %collective-permute-done) | copy-start | bytes 3538948
  245.6 92.9 %collective-permute-start.2 = (bf16[2,576,1728]{2,1,0:T(8,128)(2,1)}, bf16[2,576,1728]{2,1,0:T(8,128)(2,1)}, u32[]{:S(2)}, u32[]{:S(2)}) collective-permute-start(bf16[2,576,1728]{2,1,0:T(8,128)(2,1)} %maximum_select_fusion.5), channel_id=1, source_target_pairs={{0,4},{4,0},{1,5},{5,1},{2,6},{6,2},{3,7},{7,3},{8,12},{12,8},{9,1... | collective-permute-start | bytes 11943944 | tf_op jit(solution)/shard_map/ppermute | solution.py:39
  246.0 74.8 %copy-start.30 = (f32[256]{0:T(256)}, f32[256]{0:T(256)S(1)}, u32[]{:S(2)}) copy-start(f32[256]{0:T(256)S(1)} %add_rsqrt_fusion.1) | copy-start | bytes 3076
  346.5 20.2 %slice-start.3 = ((s8[4718592]{0:T(1024)(128)(4,1)}), s8[524288]{0:T(1024)(128)(4,1)S(1)}, s32[]{:S(2)}) async-start(s8[4718592]{0:T(1024)(128)(4,1)} %bitcast.164), calls=%async_computation.26 | async-start | bytes 1048576
  353.8 13.0 copy-start.10
  353.8 13.0 slice-start.4
  353.8 18.3 slice-start
  353.8 18.3 slice-start.1
  480.8 157.1 %copy-start = (f32[256,2304]{1,0:T(8,128)}, f32[256,2304]{1,0:T(8,128)S(1)}, u32[]{:S(2)}) copy-start(f32[256,2304]{1,0:T(8,128)S(1)} %get-tuple-element.34) | copy-start | bytes 7077892
  480.8 157.1 %copy-start.28 = (f32[256]{0:T(256)}, f32[256]{0:T(256)S(1)}, u32[]{:S(2)}) copy-start(f32[256]{0:T(256)S(1)} %add_rsqrt_fusion) | copy-start | bytes 3076
  563.7 21.2 %copy-start.5 = (bf16[2048,720]{0,1:T(8,128)(2,1)}, bf16[2048,720]{0,1:T(8,128)(2,1)S(1)}, u32[]{:S(2)}) copy-start(bf16[2048,720]{0,1:T(8,128)(2,1)S(1)} %get-tuple-element.37) | copy-start | bytes 8847364
  563.7 21.2 %copy-start.7 = (bf16[2048,720]{0,1:T(8,128)(2,1)}, bf16[2048,720]{0,1:T(8,128)(2,1)S(1)}, u32[]{:S(2)}) copy-start(bf16[2048,720]{0,1:T(8,128)(2,1)S(1)} %get-tuple-element.38) | copy-start | bytes 8847364
  761.8 13.2 collective-permute-start.10
  779.8 26.0 %collective-permute-start.12 = (bf16[1024,1728]{0,1:T(8,128)(2,1)S(1)}, bf16[1024,1728]{0,1:T(8,128)(2,1)}, u32[]{:S(2)}, u32[]{:S(2)}) collective-permute-start(bf16[1024,1728]{0,1:T(8,128)(2,1)S(1)} %pad_maximum_fusion.9), channel_id=1, source_target_pairs={{0,4},{4,0},{1,5},{5,1},{2,6},{6,2},{3,7},{7,3},{8,12},{12,8},{9,1... | collective-permute-start | bytes 10616840 | tf_op jit(solution)/shard_map/ppermute | solution.py:39
  788.6 3.5 collective-permute-start.14
  795.3 231.7 %reduce-scatter.13.cloned.1.call-start = ((), (), s32[]{:S(2)}) async-start(), calls=%async_computation.10 | async-start | bytes 2580480 | tf_op jit(solution)/shard_map/reduce_scatter | solution.py:608
  801.7 38.9 %collective-permute-start.16 = (bf16[2048,1440]{0,1:T(8,128)(2,1)}, bf16[2048,1440]{0,1:T(8,128)(2,1)}, u32[]{:S(2)}, u32[]{:S(2)}) collective-permute-start(bf16[2048,1440]{0,1:T(8,128)(2,1)} %pad_maximum_fusion.4), channel_id=1, source_target_pairs={{0,4},{4,0},{1,5},{5,1},{2,6},{6,2},{3,7},{7,3},{8,12},{12,8},{9,1... | collective-permute-start | bytes 17694728 | tf_op jit(solution)/shard_map/ppermute | solution.py:39
  830.1 197.7 %reduce-scatter.11.cloned.1.call-start = ((), (), s32[]{:S(2)}) async-start(), calls=%async_computation.8 | async-start | bytes 2580480 | tf_op jit(solution)/shard_map/reduce_scatter | solution.py:608
  830.2 10.5 copy-start.6
  840.6 187.7 %reduce-scatter.19.cloned.1.call-start = ((), (), s32[]{:S(2)}) async-start(), calls=%async_computation.18 | async-start | bytes 4239360 | tf_op jit(solution)/shard_map/reduce_scatter | solution.py:608
  869.4 17.1 copy-start.38
  869.5 226.8 %reduce-scatter.17.cloned.1.call-start = ((), (), s32[]{:S(2)}) async-start(), calls=%async_computation.16 | async-start | bytes 4239360 | tf_op jit(solution)/shard_map/reduce_scatter | solution.py:608
  886.5 244.6 %all-gather.22.cloned.1.call-start = ((), (), s32[]{:S(2)}) async-start(), calls=%async_computation.14 | async-start | bytes 1658880 | tf_op jit(solution)/shard_map/all_gather | solution.py:609
  898.6 122.5 %copy-start.35 = (u32[32]{0:T(128)S(1)}, u32[32]{0:T(128)}, u32[]{:S(2)}) copy-start(u32[32]{0:T(128)} %constant.95) | copy-start | bytes 388
  898.7 301.1 %all-gather.34.cloned.1.call-start = ((), (), s32[]{:S(2)}) async-start(), calls=%async_computation.22 | async-start | bytes 4239360 | tf_op jit(solution)/shard_map/all_gather | solution.py:609
  1006.6 18.1 collective-permute-start.18
  1026.9 104.2 %copy-start.39 = (bf16[2048,720]{0,1:T(8,128)(2,1)S(1)}, bf16[2048,720]{0,1:T(8,128)(2,1)}, u32[]{:S(2)}) copy-start(bf16[2048,720]{0,1:T(8,128)(2,1)} %get-tuple-element.57) | copy-start | bytes 8847364
  1027.0 218.3 %all-gather.18.cloned.1.call-start = ((), (), s32[]{:S(2)}) async-start(), calls=%async_computation.11 | async-start | bytes 2580480 | tf_op jit(solution)/shard_map/all_gather | solution.py:609
  1027.7 263.1 %all-gather.16.cloned.1.call-start = ((), (), s32[]{:S(2)}) async-start(), calls=%async_computation.9 | async-start | bytes 2580480 | tf_op jit(solution)/shard_map/all_gather | solution.py:609
  1028.3 330.4 %all-gather.28.cloned.1.call-start = ((), (), s32[]{:S(2)}) async-start(), calls=%async_computation.19 | async-start | bytes 4239360 | tf_op jit(solution)/shard_map/all_gather | solution.py:609
  1029.0 397.3 %all-gather.26.cloned.1.call-start = ((), (), s32[]{:S(2)}) async-start(), calls=%async_computation.17 | async-start | bytes 4239360 | tf_op jit(solution)/shard_map/all_gather | solution.py:609
  1096.3 346.7 %all-gather.24.cloned.1.call-start = ((), (), s32[]{:S(2)}) async-start(), calls=%async_computation.15 | async-start | bytes 3981312 | tf_op jit(solution)/shard_map/all_gather | solution.py:710
  1131.1 426.2 %reduce-scatter.9.cloned.1.call-start = ((), (), s32[]{:S(2)}) async-start(), calls=%async_computation.6 | async-start | bytes 10616832 | tf_op jit(solution)/shard_map/reduce_scatter | solution.py:594
  1143.1 549.6 %all-gather.32.cloned.1.call-start = ((), (), s32[]{:S(2)}) async-start(), calls=%async_computation.21 | async-start | bytes 9953280 | tf_op jit(solution)/shard_map/all_gather | solution.py:709
  1203.3 539.9 %all-gather.20.cloned.1.call-start = ((), (), s32[]{:S(2)}) async-start(), calls=%async_computation.12 | async-start | bytes 12386304 | tf_op jit(solution)/shard_map/all_gather | solution.py:682
  1245.3 46.9 %collective-permute-start.13 = (bf16[576,1728]{1,0:T(8,128)(2,1)}, bf16[576,1728]{1,0:T(8,128)(2,1)S(1)}, u32[]{:S(2)}, u32[]{:S(2)}) collective-permute-start(bf16[576,1728]{1,0:T(8,128)(2,1)} %all-gather.18.cloned.1.call-done), channel_id=1, source_target_pairs={{0,8},{8,0},{1,9},{9,1},{2,10},{10,2},{3,11},{11,3},{4,12},{12,4},... | collective-permute-start | bytes 5971976 | tf_op jit(solution)/shard_map/ppermute | solution.py:39
  1296.7 611.8 %all-gather.30.cloned.1.call-start = ((), (), s32[]{:S(2)}) async-start(), calls=%async_computation.20 | async-start | bytes 20348928 | tf_op jit(solution)/shard_map/all_gather | solution.py:682
  1358.6 75.3 %collective-permute-start.17 = (bf16[576,2880]{1,0:T(8,128)(2,1)}, bf16[576,2880]{1,0:T(8,128)(2,1)S(1)}, u32[]{:S(2)}, u32[]{:S(2)}) collective-permute-start(bf16[576,2880]{1,0:T(8,128)(2,1)} %all-gather.28.cloned.1.call-done), channel_id=1, source_target_pairs={{0,8},{8,0},{1,9},{9,1},{2,10},{10,2},{3,11},{11,3},{4,12},{12,4},... | collective-permute-start | bytes 9953288 | tf_op jit(solution)/shard_map/ppermute | solution.py:39
  1443.0 245.3 %collective-permute-start.15 = (bf16[576,2304]{1,0:T(8,128)(2,1)}, bf16[576,2304]{1,0:T(8,128)(2,1)}, u32[]{:S(2)}, u32[]{:S(2)}) collective-permute-start(bf16[576,2304]{1,0:T(8,128)(2,1)} %all-gather.24.cloned.1.call-done), channel_id=1, source_target_pairs={{0,16},{20,4},{1,17},{21,5},{2,18},{22,6},{3,19},{23,7},{8,24},{28... | collective-permute-start | bytes 7962632 | tf_op jit(solution)/shard_map/ppermute | solution.py:711
  1463.0 90.5 %copy-start.4 = (bf16[256,2304]{1,0:T(8,128)(2,1)S(1)}, bf16[256,2304]{1,0:T(8,128)(2,1)}, u32[]{:S(2)}) copy-start(bf16[256,2304]{1,0:T(8,128)(2,1)} %copy-done.3) | copy-start | bytes 3538948
  1463.0 90.6 %copy-start.24 = (f32[2304]{0:T(1024)S(1)}, f32[2304]{0:T(1024)}, u32[]{:S(2)}) copy-start(f32[2304]{0:T(1024)} %copy-done.23) | copy-start | bytes 27652
  1463.0 90.6 %copy-start.31 = (f32[256]{0:T(256)S(1)}, f32[256]{0:T(256)}, u32[]{:S(2)}) copy-start(f32[256]{0:T(256)} %copy-done.30) | copy-start | bytes 3076
  1557.3 13.3 copy-start.26
  1557.4 13.3 copy-start.27
  1563.0 138.7 %collective-permute-start.8 = (bf16[256,2304]{1,0:T(8,128)(2,1)}, bf16[256,2304]{1,0:T(8,128)(2,1)S(1)}, u32[]{:S(2)}, u32[]{:S(2)}) collective-permute-start(bf16[256,2304]{1,0:T(8,128)(2,1)} %get-tuple-element.85), channel_id=1, source_target_pairs={{0,0},{1,4},{2,8},{3,12},{4,1},{5,5},{6,9},{7,13},{8,2},{9,6},{10,... | collective-permute-start | bytes 3538952 | tf_op jit(solution)/shard_map/ppermute | solution.py:503
  1565.3 136.3 %collective-permute-start.11 = (bf16[256,2304]{1,0:T(8,128)(2,1)}, bf16[256,2304]{1,0:T(8,128)(2,1)S(1)}, u32[]{:S(2)}, u32[]{:S(2)}) collective-permute-start(bf16[256,2304]{1,0:T(8,128)(2,1)} %get-tuple-element.84), channel_id=1, source_target_pairs={{0,0},{1,4},{2,8},{3,12},{4,1},{5,5},{6,9},{7,13},{8,2},{9,6},{10,... | collective-permute-start | bytes 3538952 | tf_op jit(solution)/shard_map/ppermute | solution.py:503
  1701.7 47.7 %copy-start.16 = (bf16[256,2304]{1,0:T(8,128)(2,1)}, bf16[256,2304]{1,0:T(8,128)(2,1)S(1)}, u32[]{:S(2)}) copy-start(bf16[256,2304]{1,0:T(8,128)(2,1)S(1)} %collective-permute-done.8) | copy-start | bytes 3538948
  1701.7 47.7 %copy-start.18 = (bf16[256,2304]{1,0:T(8,128)(2,1)}, bf16[256,2304]{1,0:T(8,128)(2,1)S(1)}, u32[]{:S(2)}) copy-start(bf16[256,2304]{1,0:T(8,128)(2,1)S(1)} %collective-permute-done.11) | copy-start | bytes 3538948
  1953.4 9.0 copy-start.17
  1953.4 10.0 copy-start.19
  (17 other events, 57.0 us)
Sparse Core Ops, SparseCore 0:
  233.8 87.4 all-gather.13
  795.5 32.4 reduce-scatter.14
  830.3 43.8 reduce-scatter.12
  876.5 51.2 reduce-scatter.10
  930.5 96.9 reduce-scatter.18
  1030.2 66.0 reduce-scatter.16
  1097.9 33.1 all-gather.21
  1133.2 66.5 all-gather.33
  1201.4 43.8 all-gather.17
  1246.7 43.9 all-gather.15
  1292.3 66.2 all-gather.27
  1360.1 66.1 all-gather.25
  1427.8 10.2 all-gather.23
  1442.0 109.8 reduce-scatter.8
  1553.9 83.9 all-gather.31
  1639.9 103.2 all-gather.19
  1745.1 163.2 all-gather.29

commit v2 on v1

--- a/solution.py
+++ b/solution.py
@@ -85,25 +85,23 @@
     pl.semaphore_wait(barrier, len(devices))
 
 
-def gather_kernel(cores, block, out, send, recv, here):
+def gather_steps(cores, block, out, sems, base, here):
     x, y, c = (lax.axis_index(a) for a in PLANE)
     slot = c if cores == 2 else 0
     to_x, to_y, to_c = {"x": 1 - x}, {"y": 1 - y}, {"c": 1 - c}
-    sems = (send, recv)
     half = block.shape[0] // 2
     top, low = pl.ds(0, half), pl.ds(half, half)
     own, next_x = 2 * x + y, 2 * (1 - x) + y
     next_y, across = 2 * x + 1 - y, 2 * (1 - x) + 1 - y
-    meet([to_x, to_y] + ([to_c] if cores == 2 else []))
 
     def give(index, rows, device):
-        copy = remote(block.at[rows], out.at[own, slot, rows], sems, index, device)
+        copy = remote(block.at[rows], out.at[own, slot, rows], sems, base + index, device)
         copy.start()
         return copy
 
     def forward(index, chip, rows, device):
         place = out.at[chip, slot, rows]
-        copy = remote(place, place, sems, index, device)
+        copy = remote(place, place, sems, base + index, device)
         copy.start()
         return copy
 
@@ -144,6 +142,12 @@
         copy.wait_send()
 
 
+def gather_kernel(cores, block, out, send, recv, here):
+    x, y, c = (lax.axis_index(a) for a in PLANE)
+    meet([{"x": 1 - x}, {"y": 1 - y}] + ([{"c": 1 - c}] if cores == 2 else []))
+    gather_steps(cores, block, out, (send, recv), 0, here)
+
+
 def gather_rows(block, cores, ident):
     rows, cols = block.shape
     out = pl.pallas_call(
@@ -162,6 +166,158 @@
         name="gather_rows",
     )(block)
     return out.reshape(4 * cores * rows, cols)
+
+
+def front_kernel(
+    tokens, cotangent, lengths, gains, near, far, w_out,
+    rows_all, tok_out, cot_out, len_out, gain_out, qkv_out, side_out,
+    tok_in, len_in, gain_in, normed, send, recv, here,
+):
+    x, y, c = (lax.axis_index(a) for a in PLANE)
+    z = lax.axis_index("z")
+    to_x, to_y, to_c = {"x": 1 - x}, {"y": 1 - y}, {"c": 1 - c}
+    to_yc = {"y": 1 - y, "c": 1 - c}
+    own = 2 * y + c
+    goal = {"y": z // 2, "c": z % 2, "z": own}
+    sems = (send, recv)
+    moves = own != z
+    barrier = pltpu.get_barrier_semaphore()
+    for device in (to_x, to_y, to_c, to_yc):
+        pl.semaphore_signal(barrier, inc=1, device_id=device, device_id_type=MESH_ID)
+
+    @pl.when(moves)
+    def _():
+        pl.semaphore_signal(barrier, inc=1, device_id=goal, device_id_type=MESH_ID)
+        pl.semaphore_wait(barrier, 5)
+
+    @pl.when(~moves)
+    def _():
+        pl.semaphore_wait(barrier, 4)
+
+    gain_copies = [
+        remote(gains, gain_in.at[2 * y + c], sems, k, device)
+        for k, device in enumerate((to_y, to_c, to_yc))
+    ]
+    turn_copies = [
+        remote(src, dst, sems, 3 + k, goal)
+        for k, (src, dst) in enumerate(
+            ((lengths, len_in), (tokens, tok_in), (cotangent, cot_out))
+        )
+    ]
+    stay_copies = [
+        pltpu.make_async_copy(src, dst, here.at[k])
+        for k, (src, dst) in enumerate(
+            ((lengths, len_in), (tokens, tok_in), (cotangent, cot_out))
+        )
+    ]
+    for copy in gain_copies:
+        copy.start()
+    own_gain = pltpu.make_async_copy(gains, gain_in.at[2 * y + c], here.at[3])
+    own_gain.start()
+
+    @pl.when(moves)
+    def _():
+        for copy in turn_copies[:2]:
+            copy.start()
+
+    @pl.when(~moves)
+    def _():
+        for copy in stay_copies:
+            copy.start()
+
+    far_copy = remote(far, qkv_out.at[y, c], sems, 6, to_y)
+    near_copy = remote(near, qkv_out.at[y, c], sems, 7, to_c)
+    side_copy = remote(w_out, side_out, sems, 8, to_c)
+    far_copy.start()
+    near_copy.start()
+    side_copy.start()
+    own_near = pltpu.make_async_copy(near, qkv_out.at[y, c], here.at[4])
+    own_near.start()
+
+    @pl.when(moves)
+    def _():
+        for copy in turn_copies[:2]:
+            copy.wait_recv()
+        turn_copies[2].start()
+
+    @pl.when(~moves)
+    def _():
+        for copy in stay_copies[:2]:
+            copy.wait()
+
+    own_gain.wait()
+    for copy in gain_copies:
+        copy.wait_recv()
+    len_out[...] = len_in[...]
+    gain_out[...] = gain_in[0] + gain_in[1] + gain_in[2] + gain_in[3]
+    keep_tok = pltpu.make_async_copy(tok_in, tok_out, here.at[5])
+    keep_tok.start()
+    step = 16
+
+    @pl.loop(0, tok_in.shape[0] // step)
+    def _(i):
+        at = pl.ds(i * step, step)
+        rows = tok_in[at, :].astype(F32)
+        scale = lax.rsqrt(jnp.mean(rows * rows, -1, keepdims=True) + EPSILON)
+        normed[at, :] = (rows * scale * gain_out[0:1, :]).astype(BF16)
+
+    gather_steps(2, normed, rows_all, sems, 9, here.at[6])
+    far_copy.wait_recv()
+    from_far = qkv_out.at[1 - y, c]
+    pass_copy = remote(from_far, from_far, sems, 22, to_c)
+    pass_copy.start()
+    keep_tok.wait()
+    own_near.wait()
+    near_copy.wait_recv()
+    side_copy.wait_recv()
+    pass_copy.wait_recv()
+
+    @pl.when(moves)
+    def _():
+        turn_copies[2].wait_recv()
+        for copy in turn_copies:
+            copy.wait_send()
+
+    @pl.when(~moves)
+    def _():
+        stay_copies[2].wait()
+
+    for copy in gain_copies + [far_copy, near_copy, side_copy, pass_copy]:
+        copy.wait_send()
+
+
+def front(tokens, cotangent, lengths, gains, near, far, w_out, ident):
+    rows, cols = tokens.shape
+    shape = jax.ShapeDtypeStruct
+    dma = pltpu.SemaphoreType.DMA
+    outs = pl.pallas_call(
+        front_kernel,
+        out_shape=(
+            shape((4, 2, rows, cols), BF16),
+            shape((rows, cols), BF16),
+            shape((rows, cols), BF16),
+            shape(lengths.shape, lengths.dtype),
+            shape(gains.shape, F32),
+            shape((2, 2) + near.shape, BF16),
+            shape(w_out.shape, BF16),
+        ),
+        in_specs=[IN_VMEM] * 6 + [ANY],
+        out_specs=(ANY, ANY, ANY, IN_VMEM, IN_VMEM, ANY, ANY),
+        scratch_shapes=[
+            pltpu.VMEM((rows, cols), BF16),
+            pltpu.VMEM(lengths.shape, lengths.dtype),
+            pltpu.VMEM((4,) + gains.shape, F32),
+            pltpu.VMEM((rows, cols), BF16),
+            dma((23,)),
+            dma((23,)),
+            dma((7,)),
+        ],
+        compiler_params=pltpu.CompilerParams(
+            collective_id=ident, has_side_effects=True, vmem_limit_bytes=VMEM_LIMIT
+        ),
+        name="front",
+    )(tokens, cotangent, lengths, gains, near, far, w_out)
+    return (outs[0].reshape(8 * rows, cols),) + tuple(outs[1:])
 
 
 def add_rows(target, first, rows, terms):
@@ -262,6 +418,361 @@
         ),
         name="scatter_rows",
     )(part)
+
+
+PARTS = 3
+UNIT = 48 // PARTS
+OUT_AT, NEAR_AT, DOWN_AT, UNITS = 3 * PARTS, 4 * PARTS, 7 * PARTS, 9 * PARTS
+FAR_PLACE = 4 * 12 * PARTS
+DOWN_PLACE = FAR_PLACE + 12 * PARTS
+MINE_PLACE = DOWN_PLACE + 2 * 8 * PARTS
+OUT_PLACE = MINE_PLACE + 4 * PARTS
+PLACES = OUT_PLACE + 2 * 4 * PARTS
+
+
+def reduce_kernel(
+    grads, gain, out, gain_out,
+    inbox, final, gain_in, rs_send, rs_recv, ag_send, ag_recv, y_send, y_recv, x_send, x_recv,
+    o_send, o_recv, g_send, g_recv, here,
+):
+    x, y, c = (lax.axis_index(a) for a in PLANE)
+    z = lax.axis_index("z")
+    to_x, to_y, to_c = {"x": 1 - x}, {"y": 1 - y}, {"c": 1 - c}
+    to_xc = {"x": 1 - x, "c": 1 - c}
+    above, below = {"z": z + 1}, {"z": z - 1}
+    others = [{"z": (z + k) % 4} for k in (1, 2, 3)]
+    meet([to_x, to_y, to_c, to_xc] + others)
+
+    def add_unit(target, sources):
+        for first in range(0, UNIT, 16):
+            at = pl.ds(first, 16)
+            total = sources[0][at, :].astype(F32)
+            for ref in sources[1:]:
+                total = total + ref[at, :].astype(F32)
+            target[at, :] = total.astype(BF16)
+
+    def near_place(q, u):
+        return (2 * x + y) * 12 * PARTS + q * 3 * PARTS + u - NEAR_AT
+
+    def place(q, u):
+        far = FAR_PLACE + q * 3 * PARTS + u
+        mine = MINE_PLACE + q * PARTS + u - OUT_AT
+        down = DOWN_PLACE + x * 8 * PARTS + q * 2 * PARTS + u - DOWN_AT
+        return jnp.where(
+            u < OUT_AT,
+            far,
+            jnp.where(u < NEAR_AT, mine, jnp.where(u < DOWN_AT, near_place(q, u), down)),
+        )
+
+    def copy(src, dst, send, recv, device):
+        return pltpu.make_async_remote_copy(
+            src_ref=src, dst_ref=dst, send_sem=send, recv_sem=recv,
+            device_id=device, device_id_type=MESH_ID,
+        )
+
+    def rs_copy(src, q, u, slot, device):
+        return copy(src, inbox.at[slot, u], rs_send.at[q, u], rs_recv.at[slot, u], device)
+
+    def rs_arrived(slot, u):
+        rs_copy(inbox.at[slot, u], 0, u, slot, to_x).wait_recv()
+
+    def up(u):
+        for q in (3, 2, 1):
+            @pl.when(z == 0)
+            def _():
+                rs_copy(grads.at[q, u], q, u, q, above).start()
+
+            @pl.when((z > 0) & (z < q))
+            def _():
+                rs_arrived(q, u)
+                add_unit(inbox.at[q, u], [inbox.at[q, u], grads.at[q, u]])
+                rs_copy(inbox.at[q, u], q, u, q, above).start()
+
+    def down(u):
+        for q in (0, 1, 2):
+            @pl.when(z == 3)
+            def _():
+                rs_copy(grads.at[q, u], q, u, 4 if q == 2 else q, below).start()
+
+            for here_z in (1, 2):
+                if here_z > q:
+                    @pl.when(z == here_z)
+                    def _():
+                        rs_arrived(q, u)
+                        add_unit(inbox.at[q, u], [inbox.at[q, u], grads.at[q, u]])
+                        slot = 4 if here_z - 1 == q else q
+                        rs_copy(inbox.at[q, u], q, u, slot, below).start()
+
+    def ag_copy(src, q, u, way, device):
+        return copy(src, out.at[place(q, u)], ag_send.at[way, q, u], ag_recv.at[q, u], device)
+
+    def stay_copy(u):
+        return pltpu.make_async_copy(final.at[u], out.at[place(z, u)], here.at[u])
+
+    def x_copy(src, dst, q, u):
+        return copy(src, out.at[dst], x_send.at[q, u], x_recv.at[q, u], to_x)
+
+    def y_copy(src, q, u, owner_y):
+        dst = (2 * x + owner_y) * 12 * PARTS + q * 3 * PARTS + u
+        return copy(src, out.at[dst], y_send.at[q, u], y_recv.at[q, u], to_y)
+
+    def o_copy(src, q, k, half, way, device):
+        dst = OUT_PLACE + half * 4 * PARTS + q * PARTS + k
+        return copy(src, out.at[dst], o_send.at[way, q, k], o_recv.at[half, q, k], device)
+
+    def spread(src, q, u):
+        @pl.when(u < OUT_AT)
+        def _():
+            y_copy(src, q, u, y).start()
+
+        @pl.when((u >= OUT_AT) & (u < NEAR_AT) & (c == x))
+        def _():
+            o_copy(src, q, u - OUT_AT, c, 0, to_x).start()
+
+        @pl.when((u >= OUT_AT) & (u < NEAR_AT) & (c != x))
+        def _():
+            o_copy(src, q, u - OUT_AT, c, 0, to_xc).start()
+            o_copy(src, q, u - OUT_AT, c, 1, to_c).start()
+
+        @pl.when(u >= NEAR_AT)
+        def _():
+            x_copy(src, place(q, u), q, u).start()
+
+    def finish(u):
+        @pl.when(z == 0)
+        def _():
+            rs_arrived(4, u)
+            add_unit(final.at[u], [grads.at[0, u], inbox.at[4, u]])
+
+        for here_z in (1, 2):
+            @pl.when(z == here_z)
+            def _():
+                rs_arrived(here_z, u)
+                rs_arrived(4, u)
+                add_unit(
+                    final.at[u], [grads.at[here_z, u], inbox.at[here_z, u], inbox.at[4, u]]
+                )
+
+        @pl.when(z == 3)
+        def _():
+            rs_arrived(3, u)
+            add_unit(final.at[u], [grads.at[3, u], inbox.at[3, u]])
+
+        @pl.when(z < 3)
+        def _():
+            ag_copy(final.at[u], z, u, 0, above).start()
+
+        @pl.when(z > 0)
+        def _():
+            ag_copy(final.at[u], z, u, 1, below).start()
+
+        spread(final.at[u], z, u)
+        stay_copy(u).start()
+
+    def relay(u, far):
+        for q in range(4):
+            got = out.at[place(q, u)]
+
+            @pl.when(z == q + far)
+            def _():
+                ag_copy(got, q, u, 0, to_x).wait_recv()
+
+                @pl.when(z < 3)
+                def _():
+                    ag_copy(got, q, u, 0, above).start()
+
+                spread(got, q, u)
+
+            @pl.when(z == q - far)
+            def _():
+                ag_copy(got, q, u, 1, to_x).wait_recv()
+
+                @pl.when(z > 0)
+                def _():
+                    ag_copy(got, q, u, 1, below).start()
+
+                spread(got, q, u)
+
+    def cross(u, far):
+        for q in range(4):
+            @pl.when((z == q + far) | (z == q - far))
+            def _():
+                dst = (2 * x + 1 - y) * 12 * PARTS + q * 3 * PARTS + u
+                got = out.at[dst]
+                y_copy(got, q, u, 1 - y).wait_recv()
+                x_copy(got, dst, q, u).start()
+
+    def gain_copy(k, device):
+        return copy(gain_in.at[0], gain_in.at[1 + k], g_send.at[k], g_recv.at[k], device)
+
+    def gain_z(k, device):
+        return copy(gain_in.at[0], gain_in.at[4 + z], g_send.at[3 + k], g_recv.at[3 + z], device)
+
+    def gain_step(i):
+        for k, device in enumerate((to_c, to_x, to_y)):
+            @pl.when(i == k)
+            def _():
+                if k == 0:
+                    gain_in[0] = gain[...]
+                gain_copy(k, device).start()
+                gain_copy(k, device).wait()
+                gain_in[0] += gain_in[1 + k]
+
+        @pl.when(i == 3)
+        def _():
+            for k, device in enumerate(others):
+                gain_z(k, device).start()
+
+        @pl.when(i == 5)
+        def _():
+            for k in range(4):
+                @pl.when(z == k)
+                def _():
+                    gain_in[4 + k] = gain_in[0]
+
+                @pl.when(z != k)
+                def _():
+                    copy(
+                        gain_in.at[0], gain_in.at[4 + k], g_send.at[3], g_recv.at[3 + k], to_x
+                    ).wait_recv()
+
+            for k, device in enumerate(others):
+                gain_z(k, device).wait_send()
+            gain_out[...] = (gain_in[4] + gain_in[5]) + (gain_in[6] + gain_in[7])
+
+    def when_unit(u, last, work):
+        @pl.when((u >= 0) & (u < last))
+        def _():
+            work(u)
+
+    @pl.loop(0, UNITS + 8)
+    def _(i):
+        when_unit(i - z, UNITS, up)
+        when_unit(i - (3 - z), UNITS, down)
+        gain_step(i)
+        when_unit(i - 3, UNITS, finish)
+        for far in (1, 2, 3):
+            when_unit(i - 3 - far, UNITS, lambda u: relay(u, far))
+        for far in (0, 1, 2, 3):
+            when_unit(i - 4 - far, OUT_AT, lambda u: cross(u, far))
+
+    @pl.loop(0, UNITS)
+    def _(u):
+        stay_copy(u).wait()
+        for q in range(4):
+            src = grads.at[q, u]
+
+            @pl.when(z != q)
+            def _():
+                rs_copy(src, q, u, q, to_x).wait_send()
+
+            @pl.when((z < 3) & (q <= z))
+            def _():
+                ag_copy(src, q, u, 0, to_x).wait_send()
+
+            @pl.when((z > 0) & (q >= z))
+            def _():
+                ag_copy(src, q, u, 1, to_x).wait_send()
+
+            @pl.when(u < OUT_AT)
+            def _():
+                y_copy(src, q, u, y).wait_send()
+
+            @pl.when((u >= OUT_AT) & (u < NEAR_AT))
+            def _():
+                k = u - OUT_AT
+                o_copy(src, q, k, c, 0, to_x).wait_send()
+                o_copy(src, q, k, 1 - c, 0, to_x).wait_recv()
+
+                @pl.when(c != x)
+                def _():
+                    o_copy(src, q, k, c, 1, to_x).wait_send()
+                    o_copy(src, q, k, c, 0, to_x).wait_recv()
+
+            @pl.when((u < OUT_AT) | (u >= NEAR_AT))
+            def _():
+                x_copy(src, 0, q, u).wait()
+
+
+def reduce_grads(grads, gain, ident):
+    cols = grads.shape[3]
+    shape = jax.ShapeDtypeStruct
+    dma = pltpu.SemaphoreType.DMA
+    return pl.pallas_call(
+        reduce_kernel,
+        out_shape=(shape((PLACES, UNIT, cols), BF16), shape(gain.shape, F32)),
+        in_specs=[IN_VMEM] * 2,
+        out_specs=(ANY, IN_VMEM),
+        scratch_shapes=[
+            pltpu.VMEM((5, UNITS, UNIT, cols), BF16),
+            pltpu.VMEM((UNITS, UNIT, cols), BF16),
+            pltpu.VMEM((8,) + gain.shape, F32),
+            dma((4, UNITS)),
+            dma((5, UNITS)),
+            dma((2, 4, UNITS)),
+            dma((4, UNITS)),
+            dma((4, OUT_AT)),
+            dma((4, OUT_AT)),
+            dma((4, UNITS)),
+            dma((4, UNITS)),
+            dma((2, 4, PARTS)),
+            dma((2, 4, PARTS)),
+            dma((6,)),
+            dma((7,)),
+            dma((UNITS,)),
+        ],
+        compiler_params=pltpu.CompilerParams(
+            collective_id=ident, has_side_effects=True, vmem_limit_bytes=VMEM_LIMIT
+        ),
+        name="reduce_grads",
+    )(grads, gain)
+
+
+def rows_kernel(cols_f, cols_h, flags, *refs):
+    sources, outs = refs[:4], refs[4:]
+    core = flags[0]
+    rows = outs[0].shape[0]
+    cols = sources[0].shape[-1]
+    full = [[sources[2 * i + j][...].reshape(rows, cols) for j in range(2)] for i in range(2)]
+    for kind in range(3):
+        first = 4 * cols_f + kind * cols_h
+        outs[kind][...] = jnp.concatenate(
+            [full[i][j][:, first : first + cols_h] for j in range(2) for i in range(2)], 1
+        ).astype(F32)
+    for kind in range(2):
+        pieces = []
+        for j in range(2):
+            for k in range(2):
+                for i in range(2):
+                    own = full[i][j][:, kind * cols_f : (kind + 1) * cols_f]
+                    first = (2 + kind) * cols_f
+                    side = full[i][j][:, first : first + cols_f]
+                    pieces.append(jnp.where(core == k, own, side))
+        outs[3 + kind][...] = jnp.concatenate(pieces, 1).astype(F32)
+
+
+def place_rows(summed, c, rows_d, cols_f, cols_h):
+    cols = summed.shape[-1]
+    steps = rows_d // 48
+    shape = jax.ShapeDtypeStruct
+
+    def source(i, j):
+        return pl.BlockSpec((PARTS, UNIT, cols), lambda s: ((2 * i + j) * 12 + s, 0, 0))
+
+    def target(width):
+        return pl.BlockSpec((48, width), lambda s: (s, 0))
+
+    widths = (4 * cols_h,) * 3 + (8 * cols_f,) * 2
+    return pl.pallas_call(
+        partial(rows_kernel, cols_f, cols_h),
+        grid=(steps,),
+        out_shape=tuple(shape((rows_d, width), F32) for width in widths),
+        in_specs=[pl.BlockSpec(memory_space=pltpu.SMEM)]
+        + [source(i, j) for i in range(2) for j in range(2)],
+        out_specs=tuple(target(width) for width in widths),
+        compiler_params=pltpu.CompilerParams(vmem_limit_bytes=VMEM_LIMIT),
+        name="place_rows",
+    )(jnp.reshape(c, (1,)).astype(jnp.int32), summed, summed, summed, summed)
 
 
 def lanes(rows):
@@ -480,6 +991,13 @@
     x, y, c = (lax.axis_index(a) for a in PLANE)
     own = 2 * y + c
 
+    turn_pairs = [
+        (i * pieces_z + z, z * pieces_z + i) for i in range(pieces_z) for z in range(pieces_z)
+    ]
+
+    def turned(block):
+        return lax.ppermute(block, ("y", "c", "z"), turn_pairs)
+
     def joined(shard):
         if outer == 1:
             return shard
@@ -495,41 +1013,40 @@
     cols_h = model // 4
     cols_f = w_gate.shape[1] // 8
 
-    turn_pairs = [
-        (i * pieces_z + z, z * pieces_z + i) for i in range(pieces_z) for z in range(pieces_z)
-    ]
-
-    def turned(block):
-        return lax.ppermute(block, ("y", "c", "z"), turn_pairs)
-
-    gains = lax.all_gather(
-        jnp.stack([joined(attn_gain), joined(mlp_gain)]), ("y", "c"), axis=1, tiled=True
-    ).astype(F32)
-    gain_one, gain_two = gains[0:1], gains[1:2]
-    lengths = turned(doc_lengths)[0]
-    inputs = turned(tokens[0]).astype(F32)
-    upstream = turned(cotangent[0]).astype(F32)
-
     def head_cols(weight, group):
         return lax.dynamic_slice_in_dim(weight, group * cols_h, cols_h, 1)
 
     def qkv_cols(group):
         return jnp.concatenate([head_cols(w, group) for w in (w_query, w_key, w_value)], 1)
 
-    qkv_own = qkv_cols(2 * y + x)
-    qkv_far = swap(qkv_cols(2 * (1 - y) + x), "y")
-    qkv_pair = jnp.where(y == 0, jnp.stack([qkv_own, qkv_far]), jnp.stack([qkv_far, qkv_own]))
-    qkv_side = swap(qkv_pair, "c")
-    w_qkv = jnp.where(
-        c == 0, jnp.stack([qkv_pair, qkv_side], 1), jnp.stack([qkv_side, qkv_pair], 1)
-    ).reshape(4 * rows_d, 3 * cols_h)
-    out_side = swap(w_out, "c")
+    def spread(gain):
+        padded = jnp.zeros((model,), F32)
+        return lax.dynamic_update_slice_in_dim(padded, joined(gain).astype(F32), own * rows_d, 0)
+
+    gains = jnp.pad(jnp.stack([spread(attn_gain), spread(mlp_gain)]), ((0, 6), (0, 0)))
+    docs_in = jnp.pad(doc_lengths, ((0, 7), (0, LANES - doc_lengths.shape[1])))
+    normed_one, tok_low, cot_low, docs_turned, gains, w_qkv, out_side = front(
+        tokens[0],
+        cotangent[0],
+        docs_in,
+        gains,
+        qkv_cols(2 * y + x),
+        qkv_cols(2 * (1 - y) + x),
+        w_out,
+        1,
+    )
+    inputs, upstream = tok_low.astype(F32), cot_low.astype(F32)
+    lengths = docs_turned[0, : doc_lengths.shape[1]]
+    gain_one, gain_two = gains[0:1], gains[1:2]
+    w_qkv = w_qkv.reshape(4 * rows_d, 3 * cols_h)
     w_out_use = jnp.where(c == x, w_out, out_side)
+
+    gate_late, up_late, normed_one = lax.optimization_barrier((w_gate, w_up, normed_one))
 
     def ff_cols(dest):
         first = (2 * dest + x) * cols_f
         return jnp.concatenate(
-            [lax.dynamic_slice_in_dim(w, first, cols_f, 1) for w in (w_gate, w_up)], 1
+            [lax.dynamic_slice_in_dim(w, first, cols_f, 1) for w in (gate_late, up_late)], 1
         )
 
     ff_own = ff_cols(own)
@@ -573,7 +1090,6 @@
 
     rms_one = lax.rsqrt(jnp.mean(inputs * inputs, -1, keepdims=True) + EPSILON)
     unit_one = inputs * rms_one
-    normed_one = gather_rows((unit_one * gain_one).astype(BF16), 2, 1)
 
     query_raw = dot(own_rows(normed_one), w_qkv[:, :cols_h])
     key_raw = dot(normed_one, w_qkv[:, cols_h : 2 * cols_h])
@@ -604,29 +1120,12 @@
     grad_ff = jnp.concatenate([grad_gate, grad_up], 1)
     grad_normed_two = scatter_rows(dot_nt(grad_ff, w_ff), 2, 4)
 
-    def summed_z(grad):
-        part = lax.psum_scatter(grad.astype(BF16), "z", scatter_dimension=0, tiled=True)
-        return lax.all_gather(part, "z", axis=0, tiled=True)
-
-    grad_down = summed_z(dot_tn(activation, grad_mlp))
+    padded = jnp.pad(activation, ((0, 0), (0, 768 - cols_f)))
+    grad_down = dot_tn(padded, grad_mlp).astype(BF16)
     grad_ff_side = swap(grad_ff, "c")
-    grad_ff_chip = jnp.concatenate(
-        [
-            jnp.where(c == 0, grad_ff, grad_ff_side),
-            jnp.where(c == 0, grad_ff_side, grad_ff),
-        ],
-        1,
-    )
 
     def row_block(normed, y_of):
         return lax.dynamic_slice_in_dim(normed, (2 * y_of + c) * rows_d, rows_d, 1)
-
-    def row_grads(normed, grads):
-        near = dot_tn(row_block(normed, y), grads).astype(BF16)
-        far = dot_tn(row_block(normed, 1 - y), grads).astype(BF16)
-        return (near, far)
-
-    grad_ff_w = [summed_z(g) for g in row_grads(normed_two, grad_ff_chip)]
 
     gain_grad_two = jnp.sum(grad_normed_two * unit_two, 0)
     grad_hidden = upstream + norm_back(grad_normed_two, unit_two, rms_two, gain_two)
@@ -637,7 +1136,7 @@
     half = model // 2
     keep = lax.dynamic_slice_in_dim(grad_out_part, c * half, half, 1)
     give = lax.dynamic_slice_in_dim(grad_out_part, (1 - c) * half, half, 1)
-    grad_out_half = summed_z(keep.astype(F32) + swap(give, "c").astype(F32))
+    grad_out_half = (keep.astype(F32) + swap(give, "c").astype(F32)).astype(BF16)
 
     grad_query, grad_key, grad_value = attend_backward(
         query, key, value, grad_context, lse, tables, limits, pieces
@@ -660,56 +1159,69 @@
         .transpose(1, 0, 2, 3)
         .reshape(seq_len, 3 * cols_h)
     )
-    grad_qkv_w = [summed_z(g) for g in row_grads(normed_one, grad_qkv_all)]
-
+    def row_grads(y_of):
+        block_two, block_one = row_block(normed_two, y_of), row_block(normed_one, y_of)
+        return jnp.concatenate(
+            [
+                dot_tn(block_two, grad_ff).astype(BF16),
+                dot_tn(block_two, grad_ff_side).astype(BF16),
+                dot_tn(block_one, grad_qkv_all).astype(BF16),
+            ],
+            1,
+        )
+
+    wide = 2 * model
+    third = rows_d // 12
+    grads = jnp.concatenate(
+        [
+            row_grads(1 - y).reshape(4, 3 * PARTS, UNIT, wide),
+            jnp.pad(
+                jnp.concatenate(jnp.split(grad_out_half, 4, 0), 1), ((0, third), (0, 0))
+            ).reshape(4, PARTS, UNIT, wide),
+            row_grads(y).reshape(4, 3 * PARTS, UNIT, wide),
+            jnp.concatenate(jnp.split(grad_down, 2, 0), 1).reshape(4, 2 * PARTS, UNIT, wide),
+        ],
+        1,
+    )
     gain_grad_one = jnp.sum(grad_normed_one * unit_one, 0)
+    gain_part = jnp.pad(jnp.stack([gain_grad_one, gain_grad_two]), ((0, 6), (0, 0)))
+    summed, gain_grads = reduce_grads(grads, gain_part, 7)
+    if outer > 1:
+        gain_grads = lax.psum(gain_grads, "g")
+
     grad_inputs = grad_hidden + norm_back(grad_normed_one, unit_one, rms_one, gain_one)
     grad_tokens = turned(grad_inputs.astype(BF16))[None]
 
-    gain_grads = lax.psum(jnp.stack([gain_grad_one, gain_grad_two]), ("x", "y", "c", "g", "z"))
     shard = attn_gain.shape[0]
     first = own * rows_d + lax.axis_index("g") * shard
     gain_grads = lax.dynamic_slice_in_dim(gain_grads, first, shard, 1)
 
     def finish(grad):
         if outer > 1:
-            grad = lax.psum_scatter(grad, "g", scatter_dimension=0, tiled=True)
+            grad = lax.psum_scatter(grad.astype(BF16), "g", scatter_dimension=0, tiled=True)
         return grad.astype(F32)
 
-    def owner_rows(pair):
-        near, far = pair[0], swap(pair[1], "y")
-        both = ordered(near, far, y)
-        return lax.all_gather(both, "x", axis=0, tiled=False)
-
-    ff_all = owner_rows(grad_ff_w)
-    ff_all = [
-        jnp.concatenate(
-            [
-                ff_all[i, j, :, (2 * k + kind) * cols_f : (2 * k + kind + 1) * cols_f]
-                for j in range(2)
-                for k in range(2)
-                for i in range(2)
-            ],
-            1,
-        )
-        for kind in range(2)
+    *qkv_all, gate_all, up_all = place_rows(summed, c, rows_d, cols_f, cols_h)
+    ff_all = (gate_all, up_all)
+    down_sum = summed[DOWN_PLACE:MINE_PLACE].reshape(2, 384, wide)
+    out_mine = summed[MINE_PLACE:OUT_PLACE].reshape(4, third, wide)
+    out_got = summed[OUT_PLACE:].reshape(2, 4, third, wide)
+    down_all = jnp.concatenate(
+        [
+            part
+            for i in range(2)
+            for part in (down_sum[i, :, :model], down_sum[i, : cols_f - 384, model:])
+        ],
+        0,
+    )
+    out_halves = [
+        jnp.where((c == x) & (c == h), out_mine, out_got[h])[:3]
+        .reshape(3 * third, 4, half)
+        .transpose(1, 0, 2)
+        .reshape(rows_d, half)
+        for h in range(2)
     ]
-    qkv_all = owner_rows(grad_qkv_w)
-    qkv_all = [
-        jnp.concatenate(
-            [
-                qkv_all[i, j, :, kind * cols_h : (kind + 1) * cols_h]
-                for j in range(2)
-                for i in range(2)
-            ],
-            1,
-        )
-        for kind in range(3)
-    ]
-    down_all = lax.all_gather(grad_down, "x", axis=0, tiled=True)
-    out_near = lax.all_gather(grad_out_half, "c", axis=1, tiled=True)
-    out_far = lax.ppermute(out_near, ("x", "c"), [(0, 2), (3, 1)])
-    out_all = jnp.where(c == x, out_near, out_far)
+    out_all = jnp.concatenate(out_halves, 1)
 
     return (
         output,

time: 1980 us -> 1490 us (0.75)
  waiting for transfers between devices: 609 us -> 92.8 us
  Pallas kernels: 446 us -> 953 us
  blocking collectives: 351 us -> 0 us
  other arithmetic: 168 us -> 102 us
  starting transfers between devices: 44.5 us -> 10.9 us
  local copies, waits for them, and re-layouts: 141 us -> 114 us
    pallas_call x0 -> x3, Pallas kernels: none -> 593 us  [the longest x1 419 us: reduce_grads(): pl.pallas_call(reduce_kernel, out_shape=(shape((PLACES, UNIT, cols), BF16...]
    all_gather x10 -> x0, waiting for transfers between devices: 485 us -> none  [the longest x6 307 us: summed_z(): return lax.all_gather(part, 'z', axis=0, tiled=True)]
    all_gather x1 -> x0, blocking collectives: 126 us -> none  [on_device(): lax.all_gather(jnp.stack([joined(attn_gain), joined(mlp_gain)]), ('y', 'c...]
    psum x1 -> x0, blocking collectives: 117 us -> none  [on_device(): lax.psum(jnp.stack([gain_grad_one, gain_grad_two]), ('x', 'y', 'c', 'g',...]
    unnamed x1 -> x0, blocking collectives: 108 us -> none
    pallas_call x3 -> x2, Pallas kernels: 160 us -> 88.3 us  [gather_rows(): pl.pallas_call(partial(gather_kernel, cores), out_shape=jax.ShapeDtypeStr...]
    reduce_scatter x5 -> x0, waiting for transfers between devices: 67.3 us -> none  [summed_z(): lax.psum_scatter(grad.astype(BF16), 'z', scatter_dimension=0, tiled=True)]
    ppermute x5 -> x2, waiting for transfers between devices: 40.3 us -> 92.7 us  [turned(): return lax.ppermute(block, ('y', 'c', 'z'), turn_pairs)]
  transfers between devices with their start and end apart: 36 -> 11, of which waited for: 14 -> 2; matrix products, arithmetic and copies ran while one was open for 24% -> 18% of each run, Pallas kernels for 15% -> 44%
where the time goes in v2:
time: 1490 us; the launch traced here: 1480 us
  Pallas kernels  953 us (64%)
  matrix products  195 us (13%)
  local copies, waits for them, and re-layouts  114 us (8%)
  other arithmetic  102 us (7%)
  waiting for transfers between devices  92.8 us (6%)
  between operations  15.4 us (1%)
    pallas_call x1, Pallas kernels, reduce_grads(): pl.pallas_call(reduce_kernel, out_shape=(shape((PLACES, UNIT, cols), BF16...  419 us
    pallas_call x3, Pallas kernels, scatter_rows(): pl.pallas_call(partial(scatter_kernel, cores), out_shape=jax.ShapeDtypeSt...  173 us
    pallas_call x1, Pallas kernels, front(): pl.pallas_call(front_kernel, out_shape=(shape((4, 2, rows, cols), BF16),...  150 us
    ppermute x2, waiting for transfers between devices, turned(): return lax.ppermute(block, ('y', 'c', 'z'), turn_pairs)  92.7 us
    pallas_call x2, Pallas kernels, gather_rows(): pl.pallas_call(partial(gather_kernel, cores), out_shape=jax.ShapeDtypeStr...  88.3 us
    dot_general x8, matrix products, dot_tn(): lax.dot_general(left, right, (((0,), (0,)), ((), ())), preferred_element_...  79.8 us
    dot_general x6, matrix products, dot(): return jnp.dot(left, right, preferred_element_type=F32)  65.5 us
    pallas_call x1, Pallas kernels, attend_backward(): pl.pallas_call(partial(backward_kernel, spans, width), grid=(steps,), out...  56.4 us
  transfers between devices with their start and end apart: 11, of which 2 were waited for; matrix products, arithmetic and copies ran while one was open for 18% of the time, Pallas kernels for 44%

profile of v2, /device:TPU:4, one launch (start us, length us, event | category | flops | bytes accessed | tf_op | source)
XLA Modules:
  0.0 1483.7 jit_solution(11308400146078108197)
XLA Ops:
  10.9 3.4 constant_dynamic-slice_fusion.16
  14.3 3.0 constant_dynamic-slice_fusion.14
  17.3 4.3 concatenate.91.far
  21.6 4.3 concatenate.90.near
  25.8 150.4 %front.1 = (bf16[4,2,256,2304]{3,2,1,0:T(8,128)(2,1)}, bf16[256,2304]{1,0:T(8,128)(2,1)}, bf16[256,2304]{1,0:T(8,128)(2,1)}, s32[8,128]{1,0:T(8,128)}, f32[8,230...) custom-call(bf16[256,2304]{1,0:T(8,128)(2,1)} %bitcast.123, bf16[256,2304]{1,0:T(8,128)(2,1)} %bitcast.124, ...), custom_call_target="tpu_custom_call" | custom-call | tf_op jit(solution)/shard_map/front/pallas_call | solution.py:293
  179.0 5.1 constant_dynamic-slice_fusion.10
  184.1 5.3 constant_dynamic-slice_fusion.9
  200.3 3.7 multiply_sine_fusion.1
  206.6 4.2 fusion.41
  214.9 8.3 fusion.12.q_raw
  223.2 8.7 convolution_convert_fusion.6.v_ref
  232.0 9.4 fusion.10.k_raw
  241.4 42.9 %attend_forward.1 = (bf16[1024,576]{1,0:T(8,128)(2,1)}, bf16[2048,576]{1,0:T(8,128)(2,1)}, bf16[1024,576]{1,0:T(8,128)(2,1)}, f32[1024,576]{1,0:T(8,128)}) custom-call(f32[1024,576]{1,0:T(8,128)} %fusion.12.q_raw, f32[2048,576]{1,0:T(8,128)} %fusion.10.k_raw, bf16[2048,576]{1,0:T(8,128)(2,1)} %convolution_convert_fusion.6.v_ref, f32[1024,128]{1,0:T(8,128)} %bitcast.108, ...), custom_call_target="tpu_custom_call" | custom-call | tf_op jit(solution)/shard_map/attend_forward/pallas_call | solution.py:853
  284.2 7.3 convolution_convert_fusion.3
  291.6 51.2 %scatter_rows.3 = f32[256,2304]{1,0:T(8,128)} custom-call(bf16[4,1,256,2304]{3,2,1,0:T(8,128)(2,1)} %bitcast.116), custom_call_target="tpu_custom_call" | custom-call | tf_op jit(solution)/shard_map/scatter_rows/pallas_call | solution.py:401
  348.1 46.2 %gather_rows.2 = bf16[4,2,256,2304]{3,2,1,0:T(8,128)(2,1)} custom-call(bf16[256,2304]{1,0:T(8,128)(2,1)} %multiply_convert_fusion.4.block), custom_call_target="tpu_custom_call" | custom-call | tf_op jit(solution)/shard_map/gather_rows/pallas_call | solution.py:153
  396.5 2.9 maximum_select_fusion.2
  399.5 3.7 maximum_select_fusion.3
  403.3 3.7 maximum_select_fusion.1
  407.0 19.7 %fusion.57 = f32[2048,1440]{0,1:T(8,128)} fusion(bf16[2048,2304]{1,0:T(8,128)(2,1)S(1)} %bitcast.94, bf16[2304,1440]{1,0:T(8,128)(2,1)} %bitcast.101), kind=kOutput, calls=%fused_computation.166 | convolution fusion | flops 13589544960 | bytes 27869184 | tf_op jit(solution)/shard_map/dot_general | solution.py:27
  426.7 16.8 %multiply_convert_fusion.1 = (bf16[2048,720]{0,1:T(8,128)(2,1)S(1)}, bf16[2048,720]{0,1:T(8,128)(2,1)S(1)}, bf16[2048,720]{0,1:T(8,128)(2,1)}) fusion(f32[2048,1440]{0,1:T(8,128)} %fusion.57, bf16[2048,2304]{1,0:T(8,128)(2,1)} %all-gather.2.cloned.1.call-done, bf16[1440,2304]{1,0:T(8,128)(2,1)} %param.23, s32[]{:T(128)S(6)} %select_n.160), kind=kOutput, calls=%fused_computation.9 | convolution fusion | flops 6816890880 | bytes 33398788 | tf_op jit(solution)/shard_map/dot_general | solution.py:35
  443.6 13.7 convolution_convert_fusion.8
  457.2 17.1 %convolution_convert_fusion = bf16[2048,2304]{1,0:T(8,128)(2,1)} fusion(bf16[2304,1440]{1,0:T(8,128)(2,1)S(1)} %bitcast.102, bf16[2048,720]{0,1:T(8,128)(2,1)S(1)} %get-tuple-element.75, bf16[2048,720]{0,1:T(8,128)(2,1)S(1)} %get-tuple-element.74), kind=kOutput, calls=%fused_computation.1 | convolution fusion | flops 13606060032 | bytes 21970944 | tf_op jit(solution)/shard_map/dot_general | solution.py:35
  474.4 3.1 pad_maximum_fusion.2
  477.5 50.1 %scatter_rows.4 = f32[256,2304]{1,0:T(8,128)} custom-call(bf16[4,2,256,2304]{3,2,1,0:T(8,128)(2,1)} %bitcast.95), custom_call_target="tpu_custom_call" | custom-call | tf_op jit(solution)/shard_map/scatter_rows/pallas_call | solution.py:401
  532.0 42.1 %gather_rows.3 = bf16[4,1,256,2304]{3,2,1,0:T(8,128)(2,1)} custom-call(bf16[256,2304]{1,0:T(8,128)(2,1)} %multiply_convert_fusion.3.block), custom_call_target="tpu_custom_call" | custom-call | tf_op jit(solution)/shard_map/gather_rows/pallas_call | solution.py:153
  574.2 5.4 convolution_convert_fusion.13
  579.6 4.7 convolution_convert_fusion.5
  584.3 12.0 convolution_convert_fusion.1
  596.3 11.7 convolution_convert_fusion.4
  611.6 56.4 %attend_backward.1 = (bf16[1024,576]{1,0:T(8,128)(2,1)}, f32[2048,576]{1,0:T(8,128)}, f32[2048,576]{1,0:T(8,128)}) custom-call(bf16[1024,576]{1,0:T(8,128)(2,1)} %get-tuple-element.46.q_ref, bf16[2048,576]{1,0:T(8,128)(2,1)} %get-tuple-element.47.k_ref, bf16[2048,576]{1,0:T(8,128)(2,1)} %convolution_convert_fusion.6.v_ref, bf16[1024,576]{1,0:T(8,128)(2,1)} %copy.83.g_ref, ...), custom_call_target="tpu_custom_call" | custom-call | tf_op jit(solution)/shard_map/attend_backward/pallas_call | solution.py:942
  668.0 2.8 copy.88
  670.7 9.4 pad_maximum_fusion.1
  680.1 4.8 constant_dynamic-slice_fusion.2
  685.0 2.6 dynamic-slice_convert_fusion
  693.1 6.2 copy.98
  701.5 10.9 convolution_convert_fusion.10
  714.3 2.9 add_convert_fusion
  719.7 10.7 convolution_convert_fusion.2
  730.4 3.6 copy.100
  734.0 71.3 %scatter_rows.5 = f32[256,2304]{1,0:T(8,128)} custom-call(bf16[4,1,256,2304]{3,2,1,0:T(8,128)(2,1)} %bitcast.114), custom_call_target="tpu_custom_call" | custom-call | tf_op jit(solution)/shard_map/scatter_rows/pallas_call | solution.py:401
  805.3 2.7 fusion.25
  809.2 5.8 copy.101
  815.0 7.3 maximum_select_fusion
  822.3 12.6 convolution_convert_fusion.7
  834.9 8.1 convolution_convert_fusion.11
  843.0 10.7 concatenate.105
  853.7 10.1 convolution_convert_fusion.9
  863.8 8.0 convolution_convert_fusion.12
  871.8 10.5 concatenate.103
  882.3 12.2 pad_maximum_fusion.grads
  894.5 419.0 %reduce_grads.1 = (bf16[264,16,4608]{2,1,0:T(8,128)(2,1)}, f32[8,2304]{1,0:T(8,128)}) custom-call(bf16[4,27,16,4608]{3,2,1,0:T(8,128)(2,1)} %pad_maximum_fusion.grads, f32[8,2304]{1,0:T(8,128)} %select_maximum_fusion.gain), custom_call_target="tpu_custom_call" | custom-call | tf_op jit(solution)/shard_map/reduce_grads/pallas_call | solution.py:701
  1313.5 6.4 slice.92
  1320.0 2.9 fusion.54
  1324.1 2.7 reshape.430
  1328.6 23.7 %place_rows.1 = (f32[576,2304]{1,0:T(8,128)}, f32[576,2304]{1,0:T(8,128)}, f32[576,2304]{1,0:T(8,128)}, f32[576,5760]{1,0:T(8,128)}, f32[576,5760]{1,0:T(8,128)}) custom-call(s32[1]{0:T(128)} %bitcast.36.flags, bf16[264,16,4608]{2,1,0:T(8,128)(2,1)} %get-tuple-element.53.refs_0_.refs_1_.refs_2_.refs_3_, ...), custom_call_target="tpu_custom_call" | custom-call | tf_op jit(solution)/shard_map/place_rows/pallas_call | solution.py:766
  1353.8 2.8 maximum_convert_fusion.1
  1356.6 3.7 slice_bitcast_fusion.3
  1360.3 4.1 slice_bitcast_fusion.1
  1364.5 4.2 fusion.24
  1368.8 5.3 collective-permute-start.5
  1376.5 5.2 maximum_convert_fusion
  1381.7 67.5 %collective-permute-done.5 = bf16[256,2304]{1,0:T(8,128)(2,1)S(1)} collective-permute-done((bf16[256,2304]{1,0:T(8,128)(2,1)S(1)}, bf16[256,2304]{1,0:T(8,128)(2,1)S(1)}, u32[]{:S(2)}, u32[]{:S(2)}) %collective-permute-start.5) | collective-permute-done | bytes 1179680 | tf_op jit(solution)/shard_map/ppermute | solution.py:999
  1449.2 25.3 %collective-permute-done.3 = bf16[256,2304]{1,0:T(8,128)(2,1)S(1)} collective-permute-done((bf16[256,2304]{1,0:T(8,128)(2,1)S(1)}, bf16[256,2304]{1,0:T(8,128)(2,1)S(1)}, u32[]{:S(2)}, u32[]{:S(2)}) %collective-permute-start.3) | collective-permute-done | bytes 1179680 | tf_op jit(solution)/shard_map/ppermute | solution.py:999
  (183 shorter events, 61.6 us)
Async XLA Ops:
  7.2 419.5 %all-gather.2.cloned.1.call-start = ((), (), s32[]{:S(2)}) async-start(), calls=%async_computation.2 | async-start | bytes 10616832 | tf_op jit(solution)/shard_map/all_gather | solution.py:1089
  10.2 4.0 copy-start.24
  178.7 1185.7 %reduce-scatter.2.cloned.1.call-start = ((), (), s32[]{:S(2)}) async-start(), calls=%async_computation.1 | async-start | bytes 10616832 | tf_op jit(solution)/shard_map/reduce_scatter | solution.py:1110
  191.1 205.5 %collective-permute-start = (bf16[576,1440]{1,0:T(8,128)(2,1)}, bf16[576,1440]{1,0:T(8,128)(2,1)}, u32[]{:S(2)}, u32[]{:S(2)}) collective-permute-start(bf16[576,1440]{1,0:T(8,128)(2,1)} %pad_maximum_fusion.5), channel_id=1, source_target_pairs={{0,4},{4,0},{1,5},{5,1},{2,6},{6,2},{3,7},{7,3},{8,12},{12,8},{9,1... | collective-permute-start | bytes 4976648 | tf_op jit(solution)/shard_map/ppermute | solution.py:39
  192.9 206.6 %collective-permute-start.1 = (bf16[576,1440]{1,0:T(8,128)(2,1)}, bf16[576,1440]{1,0:T(8,128)(2,1)}, u32[]{:S(2)}, u32[]{:S(2)}) collective-permute-start(bf16[576,1440]{1,0:T(8,128)(2,1)} %pad_maximum_fusion.6), channel_id=1, source_target_pairs={{0,8},{8,0},{1,9},{9,1},{2,10},{10,2},{3,11},{11,3},{4,12},{12,4},... | collective-permute-start | bytes 4976648 | tf_op jit(solution)/shard_map/ppermute | solution.py:39
  192.9 21.7 %slice-start.7 = ((s8[9437184]{0:T(1024)(128)(4,1)}), s8[1048576]{0:T(1024)(128)(4,1)S(1)}, s32[]{:S(2)}) async-start(s8[9437184]{0:T(1024)(128)(4,1)} %bitcast.119), calls=%async_computation.10 | async-start | bytes 2097152
  194.6 204.9 %collective-permute-start.2 = (bf16[576,1440]{1,0:T(8,128)(2,1)}, bf16[576,1440]{1,0:T(8,128)(2,1)}, u32[]{:S(2)}, u32[]{:S(2)}) collective-permute-start(bf16[576,1440]{1,0:T(8,128)(2,1)} %pad_maximum_fusion.7), channel_id=1, source_target_pairs={{0,12},{4,8},{8,4},{12,0},{1,13},{5,9},{9,5},{13,1},{2,14},{6,10},... | collective-permute-start | bytes 4976648 | tf_op jit(solution)/shard_map/ppermute | solution.py:1055
  200.3 14.3 slice-start.8
  206.6 8.0 slice-start.9
  214.6 8.6 slice-start.10
  214.9 8.3 slice-start.11
  241.4 42.9 %copy-start.21 = (bf16[576,2304]{1,0:T(8,128)(2,1)S(1)}, bf16[576,2304]{1,0:T(8,128)(2,1)}, u32[]{:S(2)}) copy-start(bf16[576,2304]{1,0:T(8,128)(2,1)} %w_out.1) | copy-start | bytes 7962628
  291.6 51.2 %copy-start.4 = (bf16[256,2304]{1,0:T(8,128)(2,1)S(1)}, bf16[256,2304]{1,0:T(8,128)(2,1)}, u32[]{:S(2)}) copy-start(bf16[256,2304]{1,0:T(8,128)(2,1)} %get-tuple-element.35) | copy-start | bytes 3538948
  345.0 185.0 %copy-start = (f32[256,2304]{1,0:T(8,128)}, f32[256,2304]{1,0:T(8,128)S(1)}, u32[]{:S(2)}) copy-start(f32[256,2304]{1,0:T(8,128)S(1)} %get-tuple-element.68) | copy-start | bytes 7077892
  346.8 183.3 %copy-start.25 = (f32[2304]{0:T(1024)}, f32[2304]{0:T(1024)S(1)}, u32[]{:S(2)}) copy-start(f32[2304]{0:T(1024)S(1)} %get-tuple-element.66) | copy-start | bytes 27652
  346.8 183.3 %copy-start.28 = (f32[256]{0:T(256)}, f32[256]{0:T(256)S(1)}, u32[]{:S(2)}) copy-start(f32[256]{0:T(256)S(1)} %add_rsqrt_fusion.1) | copy-start | bytes 3076
  348.1 46.8 %copy-start.18 = (bf16[576,720]{1,0:T(8,128)(2,1)S(1)}, bf16[576,720]{1,0:T(8,128)(2,1)}, u32[]{:S(2)}) copy-start(bf16[576,720]{1,0:T(8,128)(2,1)} %get-tuple-element.81) | copy-start | bytes 2488324
  396.5 10.4 slice-start.2
  399.5 7.5 slice-start.3
  403.3 3.7 slice-start.4
  443.5 30.8 %copy-start.19 = (bf16[2048,720]{0,1:T(8,128)(2,1)}, bf16[2048,720]{0,1:T(8,128)(2,1)S(1)}, u32[]{:S(2)}) copy-start(bf16[2048,720]{0,1:T(8,128)(2,1)S(1)} %get-tuple-element.74) | copy-start | bytes 8847364
  443.5 30.8 %copy-start.20 = (bf16[2048,720]{0,1:T(8,128)(2,1)}, bf16[2048,720]{0,1:T(8,128)(2,1)S(1)}, u32[]{:S(2)}) copy-start(bf16[2048,720]{0,1:T(8,128)(2,1)S(1)} %get-tuple-element.75) | copy-start | bytes 8847364
  443.5 13.7 copy-start.10
  527.6 2.5 copy-start.2
  527.6 2.7 copy-start.6
  530.3 1.8 copy-start.31
  532.0 42.1 %copy-start.22 = (bf16[576,2304]{1,0:T(8,128)(2,1)S(1)}, bf16[576,2304]{1,0:T(8,128)(2,1)}, u32[]{:S(2)}) copy-start(bf16[576,2304]{1,0:T(8,128)(2,1)} %w_out.1) | copy-start | bytes 7962628
  574.1 5.5 copy-start.17
  574.1 5.5 copy-start.32
  579.6 4.7 copy-start.33
  690.0 24.2 %collective-permute-start.4 = (bf16[1024,1152]{0,1:T(8,128)(2,1)}, bf16[1024,1152]{0,1:T(8,128)(2,1)}, u32[]{:S(2)}, u32[]{:S(2)}) collective-permute-start(bf16[1024,1152]{0,1:T(8,128)(2,1)} %copy.99), channel_id=1, source_target_pairs={{0,4},{4,0},{1,5},{5,1},{2,6},{6,2},{3,7},{7,3},{8,12},{12,8},{9,1... | collective-permute-start | bytes 7077896 | tf_op jit(solution)/shard_map/ppermute | solution.py:39
  692.6 19.8 %collective-permute-start.8 = (bf16[576,1152]{1,0:T(8,128)(2,1)}, bf16[576,1152]{1,0:T(8,128)(2,1)}, u32[]{:S(2)}, u32[]{:S(2)}) collective-permute-start(bf16[576,1152]{1,0:T(8,128)(2,1)} %constant_dynamic-slice_fusion.1), channel_id=1, source_target_pairs={{0,4},{4,0},{1,5},{5,1},{2,6},{6,2},{3,7},{7,3},{8,12},{12,8},{9,1... | collective-permute-start | bytes 3981320 | tf_op jit(solution)/shard_map/ppermute | solution.py:39
  693.1 129.2 %collective-permute-start.6 = (bf16[2048,1440]{0,1:T(8,128)(2,1)}, bf16[2048,1440]{0,1:T(8,128)(2,1)}, u32[]{:S(2)}, u32[]{:S(2)}) collective-permute-start(bf16[2048,1440]{0,1:T(8,128)(2,1)} %pad_maximum_fusion.2), channel_id=1, source_target_pairs={{0,4},{4,0},{1,5},{5,1},{2,6},{6,2},{3,7},{7,3},{8,12},{12,8},{9,1... | collective-permute-start | bytes 17694728 | tf_op jit(solution)/shard_map/ppermute | solution.py:39
  693.1 6.2 copy-start.8
  693.1 6.2 copy-start.9
  699.3 14.9 %slice-start = ((s8[4718592]{0:T(1024)(128)(4,1)}), s8[4194304]{0:T(1024)(128)(4,1)S(1)}, s32[]{:S(2)}) async-start(s8[4718592]{0:T(1024)(128)(4,1)} %bitcast.83), calls=%async_computation.3 | async-start | bytes 8388608
  701.5 10.9 copy-start.23
  701.5 12.8 slice-start.1
  714.2 3.0 copy-start.16
  714.3 5.4 slice-start.12
  717.3 2.4 slice-start.13
  717.6 91.6 %collective-permute-start.7 = (bf16[1024,1728]{0,1:T(8,128)(2,1)S(1)}, bf16[1024,1728]{0,1:T(8,128)(2,1)}, u32[]{:S(2)}, u32[]{:S(2)}) collective-permute-start(bf16[1024,1728]{0,1:T(8,128)(2,1)S(1)} %pad_maximum_fusion.3), channel_id=1, source_target_pairs={{0,4},{4,0},{1,5},{5,1},{2,6},{6,2},{3,7},{7,3},{8,12},{12,8},{9,1... | collective-permute-start | bytes 10616840 | tf_op jit(solution)/shard_map/ppermute | solution.py:39
  734.0 71.3 %copy-start.27 = (f32[2304]{0:T(1024)S(1)}, f32[2304]{0:T(1024)}, u32[]{:S(2)}) copy-start(f32[2304]{0:T(1024)} %get-tuple-element.65) | copy-start | bytes 27652
  734.0 71.3 %copy-start.30 = (f32[256]{0:T(256)S(1)}, f32[256]{0:T(256)}, u32[]{:S(2)}) copy-start(f32[256]{0:T(256)} %add_rsqrt_fusion) | copy-start | bytes 3076
  822.3 12.6 copy-start.7
  843.0 20.8 %slice-start.5 = ((s8[7340032]{0:T(1024)(128)(4,1)}), s8[3145728]{0:T(1024)(128)(4,1)S(1)}, s32[]{:S(2)}) async-start(s8[7340032]{0:T(1024)(128)(4,1)} %bitcast.98), calls=%async_computation.8 | async-start | bytes 6291456
  853.7 10.1 slice-start.6
  871.8 10.5 copy-start.3
  1328.6 25.2 %copy-start.15 = (bf16[4,144,1152]{2,1,0:T(8,128)(2,1)S(1)}, bf16[4,144,1152]{2,1,0:T(8,128)(2,1)}, u32[]{:S(2)}) copy-start(bf16[4,144,1152]{2,1,0:T(8,128)(2,1)} %copy.93) | copy-start | bytes 3981316
  1360.3 4.2 copy-start.1
  1360.3 4.2 copy-start.5
  1360.3 4.2 copy-start.26
  1360.3 4.2 copy-start.29
  1364.5 11.9 copy-start.11
  1364.5 11.9 copy-start.12
  1364.5 11.9 copy-start.13
  1364.5 11.9 copy-start.14
  1368.8 80.4 %collective-permute-start.5 = (bf16[256,2304]{1,0:T(8,128)(2,1)S(1)}, bf16[256,2304]{1,0:T(8,128)(2,1)S(1)}, u32[]{:S(2)}, u32[]{:S(2)}) collective-permute-start(bf16[256,2304]{1,0:T(8,128)(2,1)S(1)} %get-tuple-element.97), channel_id=1, source_target_pairs={{0,0},{1,4},{2,8},{3,12},{4,1},{5,5},{6,9},{7,13},{8,2},{9,6},{10,... | collective-permute-start | bytes 3538952 | tf_op jit(solution)/shard_map/ppermute | solution.py:999
  1374.1 100.4 %collective-permute-start.3 = (bf16[256,2304]{1,0:T(8,128)(2,1)S(1)}, bf16[256,2304]{1,0:T(8,128)(2,1)S(1)}, u32[]{:S(2)}, u32[]{:S(2)}) collective-permute-start(bf16[256,2304]{1,0:T(8,128)(2,1)S(1)} %get-tuple-element.98), channel_id=1, source_target_pairs={{0,0},{1,4},{2,8},{3,12},{4,1},{5,5},{6,9},{7,13},{8,2},{9,6},{10,... | collective-permute-start | bytes 3538952 | tf_op jit(solution)/shard_map/ppermute | solution.py:999
Sparse Core Ops, SparseCore 0:
  178.8 90.2 all-gather.1
  693.2 107.1 reduce-scatter.1

commit v3 on v2

--- a/solution.py
+++ b/solution.py
@@ -39,32 +39,13 @@
     return lax.ppermute(array, axis, [(0, 1), (1, 0)])
 
 
-def layout(lengths, position):
-    doc_ends = jnp.cumsum(lengths)
-    doc_ids = jnp.sum((position[:, None] >= doc_ends[None, :]).astype(jnp.int32), axis=1)
-    doc_starts = doc_ends - lengths
-    choose = doc_ids[:, None] == jnp.arange(lengths.shape[0], dtype=jnp.int32)[None, :]
-    doc_first = jnp.sum(jnp.where(choose, doc_starts[None, :], 0), axis=1)
-    return (doc_ids, position - doc_first)
-
-
-def rope_tables(offset):
-    half_dim = HEAD_DIM // 2
-    frequency = jnp.exp(
-        jnp.arange(half_dim, dtype=F32) * (-2.0 * math.log(10000.0) / HEAD_DIM)
-    )
-    angles = offset.astype(F32)[:, None] * frequency[None, :]
-    cosine = jnp.cos(angles)
-    sine_table = jnp.sin(angles)
-    return (
-        jnp.concatenate([cosine, cosine] * 2, 1),
-        jnp.concatenate([-sine_table, sine_table] * 2, 1),
-    )
-
-
 MESH_ID = pl.DeviceIdType.MESH
 ANY = pl.BlockSpec(memory_space=pl.ANY)
 IN_VMEM = pl.BlockSpec(memory_space=pltpu.VMEM)
+
+
+def cost(micros):
+    return pl.CostEstimate(flops=int(micros * 1.0e9), bytes_accessed=0, transcendentals=0)
 
 
 def remote(src, dst, sems, index, device):
@@ -85,7 +66,7 @@
     pl.semaphore_wait(barrier, len(devices))
 
 
-def gather_steps(cores, block, out, sems, base, here):
+def gather_steps(cores, block, out, sems, base, here, meanwhile=None):
     x, y, c = (lax.axis_index(a) for a in PLANE)
     slot = c if cores == 2 else 0
     to_x, to_y, to_c = {"x": 1 - x}, {"y": 1 - y}, {"c": 1 - c}
@@ -115,6 +96,8 @@
     passed = []
     if cores == 2:
         passed.append(give(4, pl.ds(0, 2 * half), to_c))
+    if meanwhile is not None:
+        meanwhile()
     x_top.wait_recv()
     y_across = forward(5, next_x, top, to_y)
     if cores == 2:
@@ -163,14 +146,15 @@
         compiler_params=pltpu.CompilerParams(
             collective_id=ident, has_side_effects=True, vmem_limit_bytes=VMEM_LIMIT
         ),
+        cost_estimate=cost(45),
         name="gather_rows",
     )(block)
     return out.reshape(4 * cores * rows, cols)
 
 
 def front_kernel(
-    tokens, cotangent, lengths, gains, near, far, w_out,
-    rows_all, tok_out, cot_out, len_out, gain_out, qkv_out, side_out,
+    docs, tokens, lengths, gains, near, far, w_out,
+    rows_all, tok_out, gain_out, qkv_out, side_out, cos_q, sin_q, cos_k, sin_k, first_q,
     tok_in, len_in, gain_in, normed, send, recv, here,
 ):
     x, y, c = (lax.axis_index(a) for a in PLANE)
@@ -200,15 +184,11 @@
     ]
     turn_copies = [
         remote(src, dst, sems, 3 + k, goal)
-        for k, (src, dst) in enumerate(
-            ((lengths, len_in), (tokens, tok_in), (cotangent, cot_out))
-        )
+        for k, (src, dst) in enumerate(((lengths, len_in), (tokens, tok_in)))
     ]
     stay_copies = [
         pltpu.make_async_copy(src, dst, here.at[k])
-        for k, (src, dst) in enumerate(
-            ((lengths, len_in), (tokens, tok_in), (cotangent, cot_out))
-        )
+        for k, (src, dst) in enumerate(((lengths, len_in), (tokens, tok_in)))
     ]
     for copy in gain_copies:
         copy.start()
@@ -217,7 +197,7 @@
 
     @pl.when(moves)
     def _():
-        for copy in turn_copies[:2]:
+        for copy in turn_copies:
             copy.start()
 
     @pl.when(~moves)
@@ -236,19 +216,17 @@
 
     @pl.when(moves)
     def _():
-        for copy in turn_copies[:2]:
+        for copy in turn_copies:
             copy.wait_recv()
-        turn_copies[2].start()
 
     @pl.when(~moves)
     def _():
-        for copy in stay_copies[:2]:
+        for copy in stay_copies:
             copy.wait()
 
     own_gain.wait()
     for copy in gain_copies:
         copy.wait_recv()
-    len_out[...] = len_in[...]
     gain_out[...] = gain_in[0] + gain_in[1] + gain_in[2] + gain_in[3]
     keep_tok = pltpu.make_async_copy(tok_in, tok_out, here.at[5])
     keep_tok.start()
@@ -261,7 +239,40 @@
         scale = lax.rsqrt(jnp.mean(rows * rows, -1, keepdims=True) + EPSILON)
         normed[at, :] = (rows * scale * gain_out[0:1, :]).astype(BF16)
 
-    gather_steps(2, normed, rows_all, sems, 9, here.at[6])
+    step = 64
+    piece = tok_in.shape[0]
+
+    def table_rows(place, at, cosine, sine):
+        first = jnp.zeros((step, 1), jnp.int32)
+        end = jnp.zeros((1, 1), jnp.int32)
+        for k in range(docs):
+            length = len_in[0:1, k : k + 1]
+            end = end + length
+            first = first + jnp.where(place >= end, length, 0)
+        lane = lax.broadcasted_iota(jnp.int32, (step, LANES), 1) % HEAD_DIM
+        half = HEAD_DIM // 2
+        frequency = jnp.exp((lane % half).astype(F32) * (-2.0 * math.log(10000.0) / HEAD_DIM))
+        angles = (place - first).astype(F32) * frequency
+        cosine[at, :] = jnp.cos(angles)
+        turned = jnp.sin(angles)
+        sine[at, :] = jnp.where(lane < half, -turned, turned)
+        return jnp.maximum(first, place - (WINDOW - 1))
+
+    def tables():
+        @pl.loop(0, cos_k.shape[0] // step)
+        def _(i):
+            place = i * step + lax.broadcasted_iota(jnp.int32, (step, 1), 0)
+            table_rows(place, pl.ds(i * step, step), cos_k, sin_k)
+
+        @pl.loop(0, cos_q.shape[0] // step)
+        def _(i):
+            row = i * step + lax.broadcasted_iota(jnp.int32, (step, 1), 0)
+            whole_pieces = i // (piece // step)
+            place = row + (whole_pieces + c) * piece
+            at = pl.ds(i * step, step)
+            first_q[at, :] = table_rows(place, at, cos_q, sin_q)
+
+    gather_steps(2, normed, rows_all, sems, 9, here.at[6], tables)
     far_copy.wait_recv()
     from_far = qkv_out.at[1 - y, c]
     pass_copy = remote(from_far, from_far, sems, 22, to_c)
@@ -274,35 +285,35 @@
 
     @pl.when(moves)
     def _():
-        turn_copies[2].wait_recv()
         for copy in turn_copies:
             copy.wait_send()
 
-    @pl.when(~moves)
-    def _():
-        stay_copies[2].wait()
-
     for copy in gain_copies + [far_copy, near_copy, side_copy, pass_copy]:
         copy.wait_send()
 
 
-def front(tokens, cotangent, lengths, gains, near, far, w_out, ident):
+def front(tokens, doc_lengths, gains, near, far, w_out, seq_len, ident):
     rows, cols = tokens.shape
+    docs = doc_lengths.shape[1]
+    lengths = jnp.pad(doc_lengths, ((0, 7), (0, LANES - docs)))
     shape = jax.ShapeDtypeStruct
     dma = pltpu.SemaphoreType.DMA
     outs = pl.pallas_call(
-        front_kernel,
+        partial(front_kernel, docs),
         out_shape=(
             shape((4, 2, rows, cols), BF16),
             shape((rows, cols), BF16),
-            shape((rows, cols), BF16),
-            shape(lengths.shape, lengths.dtype),
             shape(gains.shape, F32),
             shape((2, 2) + near.shape, BF16),
             shape(w_out.shape, BF16),
+            shape((seq_len // 2, LANES), F32),
+            shape((seq_len // 2, LANES), F32),
+            shape((seq_len, LANES), F32),
+            shape((seq_len, LANES), F32),
+            shape((seq_len // 2, 1), jnp.int32),
         ),
-        in_specs=[IN_VMEM] * 6 + [ANY],
-        out_specs=(ANY, ANY, ANY, IN_VMEM, IN_VMEM, ANY, ANY),
+        in_specs=[IN_VMEM] * 5 + [ANY],
+        out_specs=(ANY, ANY, IN_VMEM, ANY, ANY) + (IN_VMEM,) * 5,
         scratch_shapes=[
             pltpu.VMEM((rows, cols), BF16),
             pltpu.VMEM(lengths.shape, lengths.dtype),
@@ -315,8 +326,9 @@
         compiler_params=pltpu.CompilerParams(
             collective_id=ident, has_side_effects=True, vmem_limit_bytes=VMEM_LIMIT
         ),
+        cost_estimate=cost(110),
         name="front",
-    )(tokens, cotangent, lengths, gains, near, far, w_out)
+    )(tokens, lengths, gains, near, far, w_out)
     return (outs[0].reshape(8 * rows, cols),) + tuple(outs[1:])
 
 
@@ -416,22 +428,18 @@
         compiler_params=pltpu.CompilerParams(
             collective_id=ident, has_side_effects=True, vmem_limit_bytes=VMEM_LIMIT
         ),
+        cost_estimate=cost(50),
         name="scatter_rows",
     )(part)
 
 
 PARTS = 3
 UNIT = 48 // PARTS
-OUT_AT, NEAR_AT, DOWN_AT, UNITS = 3 * PARTS, 4 * PARTS, 7 * PARTS, 9 * PARTS
-FAR_PLACE = 4 * 12 * PARTS
-DOWN_PLACE = FAR_PLACE + 12 * PARTS
-MINE_PLACE = DOWN_PLACE + 2 * 8 * PARTS
-OUT_PLACE = MINE_PLACE + 4 * PARTS
-PLACES = OUT_PLACE + 2 * 4 * PARTS
+OUT_AT, UNITS = 3 * PARTS, 4 * PARTS
 
 
 def reduce_kernel(
-    grads, gain, out, gain_out,
+    grads, gain, out, rows_out, out_out, gain_out,
     inbox, final, gain_in, rs_send, rs_recv, ag_send, ag_recv, y_send, y_recv, x_send, x_recv,
     o_send, o_recv, g_send, g_recv, here,
 ):
@@ -451,18 +459,14 @@
                 total = total + ref[at, :].astype(F32)
             target[at, :] = total.astype(BF16)
 
-    def near_place(q, u):
-        return (2 * x + y) * 12 * PARTS + q * 3 * PARTS + u - NEAR_AT
+    width = grads.shape[3] // 2
+    near_half, far_half = pl.ds(0, width), pl.ds(width, width)
 
     def place(q, u):
-        far = FAR_PLACE + q * 3 * PARTS + u
-        mine = MINE_PLACE + q * PARTS + u - OUT_AT
-        down = DOWN_PLACE + x * 8 * PARTS + q * 2 * PARTS + u - DOWN_AT
-        return jnp.where(
-            u < OUT_AT,
-            far,
-            jnp.where(u < NEAR_AT, mine, jnp.where(u < DOWN_AT, near_place(q, u), down)),
-        )
+        return q * UNITS + u
+
+    def rows_place(owner_x, owner_y, q, u):
+        return ((2 * owner_x + owner_y) * 4 + q) * OUT_AT + u
 
     def copy(src, dst, send, recv, device):
         return pltpu.make_async_remote_copy(
@@ -509,34 +513,32 @@
     def stay_copy(u):
         return pltpu.make_async_copy(final.at[u], out.at[place(z, u)], here.at[u])
 
-    def x_copy(src, dst, q, u):
-        return copy(src, out.at[dst], x_send.at[q, u], x_recv.at[q, u], to_x)
+    def x_copy(src, q, u, far):
+        dst = rows_place(x, y, q, u) if far == 0 else rows_place(x, 1 - y, q, u)
+        return copy(src, rows_out.at[dst], x_send.at[far, q, u], x_recv.at[far, q, u], to_x)
 
     def y_copy(src, q, u, owner_y):
-        dst = (2 * x + owner_y) * 12 * PARTS + q * 3 * PARTS + u
-        return copy(src, out.at[dst], y_send.at[q, u], y_recv.at[q, u], to_y)
+        dst = rows_out.at[rows_place(x, owner_y, q, u)]
+        return copy(src, dst, y_send.at[q, u], y_recv.at[q, u], to_y)
 
     def o_copy(src, q, k, half, way, device):
-        dst = OUT_PLACE + half * 4 * PARTS + q * PARTS + k
-        return copy(src, out.at[dst], o_send.at[way, q, k], o_recv.at[half, q, k], device)
+        dst = half * 4 * PARTS + q * PARTS + k
+        return copy(src, out_out.at[dst], o_send.at[way, q, k], o_recv.at[half, q, k], device)
 
     def spread(src, q, u):
         @pl.when(u < OUT_AT)
         def _():
-            y_copy(src, q, u, y).start()
-
-        @pl.when((u >= OUT_AT) & (u < NEAR_AT) & (c == x))
+            y_copy(src.at[:, far_half], q, u, y).start()
+            x_copy(src.at[:, near_half], q, u, 0).start()
+
+        @pl.when((u >= OUT_AT) & (c == x))
         def _():
             o_copy(src, q, u - OUT_AT, c, 0, to_x).start()
 
-        @pl.when((u >= OUT_AT) & (u < NEAR_AT) & (c != x))
+        @pl.when((u >= OUT_AT) & (c != x))
         def _():
             o_copy(src, q, u - OUT_AT, c, 0, to_xc).start()
             o_copy(src, q, u - OUT_AT, c, 1, to_c).start()
-
-        @pl.when(u >= NEAR_AT)
-        def _():
-            x_copy(src, place(q, u), q, u).start()
 
     def finish(u):
         @pl.when(z == 0)
@@ -597,10 +599,9 @@
         for q in range(4):
             @pl.when((z == q + far) | (z == q - far))
             def _():
-                dst = (2 * x + 1 - y) * 12 * PARTS + q * 3 * PARTS + u
-                got = out.at[dst]
+                got = rows_out.at[rows_place(x, 1 - y, q, u)]
                 y_copy(got, q, u, 1 - y).wait_recv()
-                x_copy(got, dst, q, u).start()
+                x_copy(got, q, u, 1).start()
 
     def gain_copy(k, device):
         return copy(gain_in.at[0], gain_in.at[1 + k], g_send.at[k], g_recv.at[k], device)
@@ -676,9 +677,12 @@
 
             @pl.when(u < OUT_AT)
             def _():
-                y_copy(src, q, u, y).wait_send()
-
-            @pl.when((u >= OUT_AT) & (u < NEAR_AT))
+                half = rows_out.at[0]
+                y_copy(half, q, u, y).wait_send()
+                x_copy(half, q, u, 0).wait()
+                x_copy(half, q, u, 1).wait()
+
+            @pl.when(u >= OUT_AT)
             def _():
                 k = u - OUT_AT
                 o_copy(src, q, k, c, 0, to_x).wait_send()
@@ -688,10 +692,6 @@
                 def _():
                     o_copy(src, q, k, c, 1, to_x).wait_send()
                     o_copy(src, q, k, c, 0, to_x).wait_recv()
-
-            @pl.when((u < OUT_AT) | (u >= NEAR_AT))
-            def _():
-                x_copy(src, 0, q, u).wait()
 
 
 def reduce_grads(grads, gain, ident):
@@ -700,9 +700,14 @@
     dma = pltpu.SemaphoreType.DMA
     return pl.pallas_call(
         reduce_kernel,
-        out_shape=(shape((PLACES, UNIT, cols), BF16), shape(gain.shape, F32)),
+        out_shape=(
+            shape((4 * UNITS, UNIT, cols), BF16),
+            shape((16 * OUT_AT, UNIT, cols // 2), BF16),
+            shape((8 * PARTS, UNIT, cols), BF16),
+            shape(gain.shape, F32),
+        ),
         in_specs=[IN_VMEM] * 2,
-        out_specs=(ANY, IN_VMEM),
+        out_specs=(ANY, ANY, ANY, IN_VMEM),
         scratch_shapes=[
             pltpu.VMEM((5, UNITS, UNIT, cols), BF16),
             pltpu.VMEM((UNITS, UNIT, cols), BF16),
@@ -713,8 +718,8 @@
             dma((4, UNITS)),
             dma((4, OUT_AT)),
             dma((4, OUT_AT)),
-            dma((4, UNITS)),
-            dma((4, UNITS)),
+            dma((2, 4, OUT_AT)),
+            dma((2, 4, OUT_AT)),
             dma((2, 4, PARTS)),
             dma((2, 4, PARTS)),
             dma((6,)),
@@ -724,21 +729,42 @@
         compiler_params=pltpu.CompilerParams(
             collective_id=ident, has_side_effects=True, vmem_limit_bytes=VMEM_LIMIT
         ),
+        cost_estimate=cost(180),
         name="reduce_grads",
     )(grads, gain)
 
 
-def rows_kernel(cols_f, cols_h, flags, *refs):
+def rows_kernel(cols_f, cols_h, flags, mine, near, far, near_x, far_x, *refs):
     sources, outs = refs[:4], refs[4:]
-    core = flags[0]
-    rows = outs[0].shape[0]
-    cols = sources[0].shape[-1]
-    full = [[sources[2 * i + j][...].reshape(rows, cols) for j in range(2)] for i in range(2)]
+    here_x, here_y, core = flags[0], flags[1], flags[2]
+    rows, cols = outs[0].shape[0], mine.shape[-1]
+    own = mine[...].reshape(rows, cols)
+    full = [
+        [
+            jnp.where(
+                (here_x == i) & (here_y == j), own, sources[2 * i + j][...].reshape(rows, cols)
+            )
+            for j in range(2)
+        ]
+        for i in range(2)
+    ]
     for kind in range(3):
-        first = 4 * cols_f + kind * cols_h
+        first = kind * cols_h
         outs[kind][...] = jnp.concatenate(
             [full[i][j][:, first : first + cols_h] for j in range(2) for i in range(2)], 1
         ).astype(F32)
+    by_x = [(near[...], far[...]), (near_x[...], far_x[...])]
+    full = [
+        [
+            jnp.where(
+                here_x == i,
+                jnp.where(here_y == j, *by_x[0]),
+                jnp.where(here_y == j, *by_x[1]),
+            )
+            for j in range(2)
+        ]
+        for i in range(2)
+    ]
     for kind in range(2):
         pieces = []
         for j in range(2):
@@ -751,9 +777,8 @@
         outs[3 + kind][...] = jnp.concatenate(pieces, 1).astype(F32)
 
 
-def place_rows(summed, c, rows_d, cols_f, cols_h):
+def place_rows(flags, mine, summed, near, far, near_x, far_x, rows_d, cols_f, cols_h):
     cols = summed.shape[-1]
-    steps = rows_d // 48
     shape = jax.ShapeDtypeStruct
 
     def source(i, j):
@@ -762,17 +787,20 @@
     def target(width):
         return pl.BlockSpec((48, width), lambda s: (s, 0))
 
+    own = pl.BlockSpec((PARTS, UNIT, cols), lambda s: (s + s // 3, 0, 0))
+    ff = pl.BlockSpec((48, 4 * cols_f), lambda s: (s, 0))
     widths = (4 * cols_h,) * 3 + (8 * cols_f,) * 2
     return pl.pallas_call(
         partial(rows_kernel, cols_f, cols_h),
-        grid=(steps,),
+        grid=(rows_d // 48,),
         out_shape=tuple(shape((rows_d, width), F32) for width in widths),
-        in_specs=[pl.BlockSpec(memory_space=pltpu.SMEM)]
+        in_specs=[pl.BlockSpec(memory_space=pltpu.SMEM), own] + [ff] * 4
         + [source(i, j) for i in range(2) for j in range(2)],
         out_specs=tuple(target(width) for width in widths),
         compiler_params=pltpu.CompilerParams(vmem_limit_bytes=VMEM_LIMIT),
+        cost_estimate=cost(25),
         name="place_rows",
-    )(jnp.reshape(c, (1,)).astype(jnp.int32), summed, summed, summed, summed)
+    )(flags, mine, near, far, near_x, far_x, summed, summed, summed, summed)
 
 
 def lanes(rows):
@@ -878,11 +906,62 @@
         ),
         scratch_shapes=[pltpu.VMEM((k_rows, LANES), BF16)],
         compiler_params=pltpu.CompilerParams(vmem_limit_bytes=VMEM_LIMIT),
+        cost_estimate=cost(43),
         name="attend_forward",
     )(q_raw, k_raw, value, *tables, *limits)
 
 
 def backward_kernel(
+    spans, width, q_ref, k_ref, v_ref, g_ref, lse, cos_q, sin_q, cos_k, sin_k, first, place,
+    dq_out, dk_done, dv_done, k_keep, v_keep, dk_out, dv_out, give, got, send, recv,
+):
+    step = pl.program_id(0)
+    c = lax.axis_index("c")
+    rows_j = q_ref.shape[0] // len(spans)
+    pair = [("dk", dk_out, dk_done), ("dv", dv_out, dv_done)]
+
+    def to_side(at):
+        return pltpu.make_async_remote_copy(
+            src_ref=give.at[at],
+            dst_ref=got.at[at],
+            send_sem=send.at[at],
+            recv_sem=recv.at[at],
+            device_id={"c": 1 - c},
+            device_id_type=MESH_ID,
+        )
+
+    @pl.when(step == 0)
+    def _():
+        meet([{"c": 1 - c}])
+
+    @pl.when(step > 0)
+    def _():
+        to_side(step - 1).wait_recv()
+        for k, (_, whole_sum, done) in enumerate(pair):
+            for j in range(len(spans)):
+                rows = pl.ds(j * rows_j, rows_j)
+                own = whole_sum[pl.ds(pl.multiple_of((2 * j + c) * rows_j, rows_j), rows_j), :]
+                done[rows, :] = (own + got[step - 1, k, rows, :].astype(F32)).astype(BF16)
+
+    @pl.when(step < pl.num_programs(0) - 1)
+    def _():
+        backward_step(
+            spans, width, q_ref, k_ref, v_ref, g_ref, lse, cos_q, sin_q, cos_k, sin_k,
+            first, place, dq_out, dk_out, dv_out, k_keep, v_keep,
+        )
+        for k, (_, whole_sum, _) in enumerate(pair):
+            for j in range(len(spans)):
+                other = pl.ds(pl.multiple_of((2 * j + 1 - c) * rows_j, rows_j), rows_j)
+                give[step, k, pl.ds(j * rows_j, rows_j), :] = whole_sum[other, :].astype(BF16)
+        to_side(step).start()
+
+    @pl.when(step == pl.num_programs(0) - 1)
+    def _():
+        for k in range(give.shape[0]):
+            to_side(k).wait_send()
+
+
+def backward_step(
     spans, width, q_ref, k_ref, v_ref, g_ref, lse, cos_q, sin_q, cos_k, sin_k, first, place,
     dq_out, dk_out, dv_out, k_keep, v_keep,
 ):
@@ -933,26 +1012,29 @@
     dk_out[...] = rotated(dk_out[...], cos_k[...], -sin_k[...])
 
 
-def attend_backward(query, key, value, grad, lse, tables, limits, pieces):
+def attend_backward(query, key, value, grad, lse, tables, limits, pieces, ident):
     q_rows, width = query.shape
     k_rows = key.shape[0]
     spans = key_spans(pieces, k_rows // pieces)
     steps = -(-width // LANES)
     shape = jax.ShapeDtypeStruct
+
+    def this(rows):
+        return pl.BlockSpec((rows, LANES), lambda p: (0, jnp.minimum(p, steps - 1)))
+
+    def last(rows):
+        return pl.BlockSpec((rows, LANES), lambda p: (0, jnp.maximum(p - 1, 0)))
+
     return pl.pallas_call(
         partial(backward_kernel, spans, width),
-        grid=(steps,),
-        out_shape=(
-            shape((q_rows, width), BF16),
-            shape((k_rows, width), F32),
-            shape((k_rows, width), F32),
-        ),
+        grid=(steps + 1,),
+        out_shape=(shape((q_rows, width), BF16),) * 3,
         in_specs=[
-            lane_block(q_rows),
-            lane_block(k_rows),
-            lane_block(k_rows),
-            lane_block(q_rows),
-            lane_block(q_rows),
+            this(q_rows),
+            this(k_rows),
+            this(k_rows),
+            this(q_rows),
+            this(q_rows),
             whole(q_rows, LANES),
             whole(q_rows, LANES),
             whole(k_rows, LANES),
@@ -960,9 +1042,15 @@
             whole(q_rows, 1),
             whole(q_rows, 1),
         ],
-        out_specs=(lane_block(q_rows), lane_block(k_rows), lane_block(k_rows)),
-        scratch_shapes=[pltpu.VMEM((k_rows, LANES), BF16)] * 2,
-        compiler_params=pltpu.CompilerParams(vmem_limit_bytes=VMEM_LIMIT),
+        out_specs=(this(q_rows), last(q_rows), last(q_rows)),
+        scratch_shapes=[pltpu.VMEM((k_rows, LANES), BF16)] * 2
+        + [pltpu.VMEM((k_rows, LANES), F32)] * 2
+        + [pltpu.VMEM((steps, 2, q_rows, LANES), BF16)] * 2
+        + [pltpu.SemaphoreType.DMA((steps,))] * 2,
+        compiler_params=pltpu.CompilerParams(
+            collective_id=ident, has_side_effects=True, vmem_limit_bytes=VMEM_LIMIT
+        ),
+        cost_estimate=cost(57),
         name="attend_backward",
     )(query, key, value, grad, lse, *tables, *limits)
 
@@ -1024,19 +1112,19 @@
         return lax.dynamic_update_slice_in_dim(padded, joined(gain).astype(F32), own * rows_d, 0)
 
     gains = jnp.pad(jnp.stack([spread(attn_gain), spread(mlp_gain)]), ((0, 6), (0, 0)))
-    docs_in = jnp.pad(doc_lengths, ((0, 7), (0, LANES - doc_lengths.shape[1])))
-    normed_one, tok_low, cot_low, docs_turned, gains, w_qkv, out_side = front(
+    normed_one, tok_low, gains, w_qkv, out_side, *tables, first_query = front(
         tokens[0],
-        cotangent[0],
-        docs_in,
+        doc_lengths,
         gains,
         qkv_cols(2 * y + x),
         qkv_cols(2 * (1 - y) + x),
         w_out,
+        seq_len,
         1,
     )
+    cot_late, _ = lax.optimization_barrier((cotangent[0], tok_low))
+    cot_low = turned(cot_late)
     inputs, upstream = tok_low.astype(F32), cot_low.astype(F32)
-    lengths = docs_turned[0, : doc_lengths.shape[1]]
     gain_one, gain_two = gains[0:1], gains[1:2]
     w_qkv = w_qkv.reshape(4 * rows_d, 3 * cols_h)
     w_out_use = jnp.where(c == x, w_out, out_side)
@@ -1064,10 +1152,6 @@
     w_ff = ordered(ff_near, ff_far, y).reshape(4 * rows_d, 2 * cols_f)
     down_use = lax.dynamic_slice_in_dim(w_down, x * cols_f, cols_f, 0)
 
-    place = jnp.arange(seq_len, dtype=jnp.int32)
-    docs, offset = layout(lengths, place)
-    cosine, sine_table = rope_tables(offset)
-
     def own_rows(array):
         cols = array.shape[1:]
         split = array.reshape((pieces // 2, 2, tok_rows) + cols)
@@ -1075,16 +1159,8 @@
             (seq_len // 2,) + cols
         )
 
-    def other_rows(array):
-        cols = array.shape[1:]
-        split = array.reshape((pieces // 2, 2, tok_rows) + cols)
-        return lax.dynamic_index_in_dim(split, 1 - c, 1, keepdims=False).reshape(
-            (seq_len // 2,) + cols
-        )
-
-    tables = (own_rows(cosine), own_rows(sine_table), cosine, sine_table)
-    first_key = jnp.maximum(place - offset, place - (WINDOW - 1))
-    limits = (own_rows(first_key)[:, None], own_rows(place)[:, None])
+    place = own_rows(jnp.arange(seq_len, dtype=jnp.int32))
+    limits = (first_query, place[:, None])
 
     grad_mlp = lax.all_gather((BETA * upstream).astype(BF16), PLANE, axis=0, tiled=True)
 
@@ -1118,14 +1194,34 @@
         grad_activation * up * (sigmoid_gate * (1.0 + gate * (1.0 - sigmoid_gate)))
     ).astype(BF16)
     grad_ff = jnp.concatenate([grad_gate, grad_up], 1)
-    grad_normed_two = scatter_rows(dot_nt(grad_ff, w_ff), 2, 4)
-
     padded = jnp.pad(activation, ((0, 0), (0, 768 - cols_f)))
-    grad_down = dot_tn(padded, grad_mlp).astype(BF16)
     grad_ff_side = swap(grad_ff, "c")
 
     def row_block(normed, y_of):
         return lax.dynamic_slice_in_dim(normed, (2 * y_of + c) * rows_d, rows_d, 1)
+
+    def ff_rows(y_of):
+        block = row_block(normed_two, y_of)
+        return jnp.concatenate(
+            [dot_tn(block, grad_ff).astype(BF16), dot_tn(block, grad_ff_side).astype(BF16)], 1
+        )
+
+    grad_down = dot_tn(padded, grad_mlp).astype(BF16)
+    ff_near, ff_far = ff_rows(y), ff_rows(1 - y)
+    back_part = dot_nt(grad_ff, w_ff).astype(BF16)
+    back_part, grad_down, ff_near, ff_far = lax.optimization_barrier(
+        (back_part, grad_down, ff_near, ff_far)
+    )
+
+    def sum_z(grad):
+        return lax.psum_scatter(grad, "z", scatter_dimension=0, tiled=True)
+
+    def gather_z(part, after):
+        part = lax.optimization_barrier((part, after))[0]
+        return lax.all_gather(part, "z", axis=0, tiled=True)
+
+    ff_far, ff_near, grad_down = sum_z(ff_far), sum_z(ff_near), sum_z(grad_down)
+    grad_normed_two = scatter_rows(back_part, 2, 4)
 
     gain_grad_two = jnp.sum(grad_normed_two * unit_two, 0)
     grad_hidden = upstream + norm_back(grad_normed_two, unit_two, rms_two, gain_two)
@@ -1139,12 +1235,10 @@
     grad_out_half = (keep.astype(F32) + swap(give, "c").astype(F32)).astype(BF16)
 
     grad_query, grad_key, grad_value = attend_backward(
-        query, key, value, grad_context, lse, tables, limits, pieces
+        query, key, value, grad_context, lse, tables, limits, pieces, 8
     )
-    grad_kv = jnp.concatenate([grad_key, grad_value], 1)
-    grad_kv = own_rows(grad_kv) + swap(other_rows(grad_kv).astype(BF16), "c").astype(F32)
-    grad_key = grad_kv[:, :cols_h].astype(BF16)
-    grad_value = grad_kv[:, cols_h:].astype(BF16)
+    ff_far = swap(gather_z(ff_far, grad_query), "y")
+    ff_near = gather_z(ff_near, grad_query)
     grad_qkv = jnp.concatenate([grad_query, grad_key, grad_value], 1)
 
     grad_normed_one = scatter_rows(dot_nt(grad_qkv, w_qkv), 1, 6)
@@ -1159,33 +1253,29 @@
         .transpose(1, 0, 2, 3)
         .reshape(seq_len, 3 * cols_h)
     )
-    def row_grads(y_of):
-        block_two, block_one = row_block(normed_two, y_of), row_block(normed_one, y_of)
-        return jnp.concatenate(
-            [
-                dot_tn(block_two, grad_ff).astype(BF16),
-                dot_tn(block_two, grad_ff_side).astype(BF16),
-                dot_tn(block_one, grad_qkv_all).astype(BF16),
-            ],
-            1,
-        )
-
-    wide = 2 * model
+    grad_down = gather_z(grad_down, grad_normed_one)
     third = rows_d // 12
+    width = -(-3 * cols_h // LANES) * LANES
+
+    def qkv_rows(y_of):
+        part = dot_tn(row_block(normed_one, y_of), grad_qkv_all).astype(BF16)
+        return jnp.pad(part, ((0, 0), (0, width - 3 * cols_h)))
+
     grads = jnp.concatenate(
         [
-            row_grads(1 - y).reshape(4, 3 * PARTS, UNIT, wide),
+            jnp.concatenate([qkv_rows(y), qkv_rows(1 - y)], 1).reshape(
+                4, OUT_AT, UNIT, 2 * width
+            ),
             jnp.pad(
-                jnp.concatenate(jnp.split(grad_out_half, 4, 0), 1), ((0, third), (0, 0))
-            ).reshape(4, PARTS, UNIT, wide),
-            row_grads(y).reshape(4, 3 * PARTS, UNIT, wide),
-            jnp.concatenate(jnp.split(grad_down, 2, 0), 1).reshape(4, 2 * PARTS, UNIT, wide),
+                jnp.concatenate(jnp.split(grad_out_half, 3, 0), 1),
+                ((0, 0), (0, 2 * width - 3 * half)),
+            ).reshape(4, PARTS, UNIT, 2 * width),
         ],
         1,
     )
     gain_grad_one = jnp.sum(grad_normed_one * unit_one, 0)
     gain_part = jnp.pad(jnp.stack([gain_grad_one, gain_grad_two]), ((0, 6), (0, 0)))
-    summed, gain_grads = reduce_grads(grads, gain_part, 7)
+    mine, summed, out_got, gain_grads = reduce_grads(grads, gain_part, 7)
     if outer > 1:
         gain_grads = lax.psum(gain_grads, "g")
 
@@ -1201,24 +1291,23 @@
             grad = lax.psum_scatter(grad.astype(BF16), "g", scatter_dimension=0, tiled=True)
         return grad.astype(F32)
 
-    *qkv_all, gate_all, up_all = place_rows(summed, c, rows_d, cols_f, cols_h)
+    flags = jnp.stack([x, y, c]).astype(jnp.int32)
+    *qkv_all, gate_all, up_all = place_rows(
+        flags, mine, summed, ff_near, ff_far, swap(ff_near, "x"), swap(ff_far, "x"),
+        rows_d, cols_f, cols_h,
+    )
     ff_all = (gate_all, up_all)
-    down_sum = summed[DOWN_PLACE:MINE_PLACE].reshape(2, 384, wide)
-    out_mine = summed[MINE_PLACE:OUT_PLACE].reshape(4, third, wide)
-    out_got = summed[OUT_PLACE:].reshape(2, 4, third, wide)
+    down_own, down_side = grad_down[:cols_f], swap(grad_down, "x")[:cols_f]
     down_all = jnp.concatenate(
-        [
-            part
-            for i in range(2)
-            for part in (down_sum[i, :, :model], down_sum[i, : cols_f - 384, model:])
-        ],
-        0,
+        [jnp.where(x == 0, down_own, down_side), jnp.where(x == 0, down_side, down_own)], 0
     )
+    out_mine = mine.reshape(4, UNITS, UNIT, 2 * width)[:, OUT_AT:, :, : 3 * half]
+    out_mine = out_mine.reshape(4 * third, 3 * half)
+    out_got = out_got[:, :, : 3 * half].reshape(2, 4 * third, 3 * half)
     out_halves = [
-        jnp.where((c == x) & (c == h), out_mine, out_got[h])[:3]
-        .reshape(3 * third, 4, half)
-        .transpose(1, 0, 2)
-        .reshape(rows_d, half)
+        jnp.concatenate(
+            jnp.split(jnp.where((c == x) & (c == h), out_mine, out_got[h]), 3, 1), 0
+        )
         for h in range(2)
     ]
     out_all = jnp.concatenate(out_halves, 1)

time: 1490 us -> 1340 us (0.90)
  Pallas kernels: 953 us -> 754 us
  waiting for transfers between devices: 92.8 us -> 179 us
  local copies, waits for them, and re-layouts: 114 us -> 74.8 us
  other arithmetic: 102 us -> 82.9 us
    pallas_call x4, Pallas kernels: 649 us -> 451 us  [the longest x1 235 us: reduce_grads(): pl.pallas_call(reduce_kernel, out_shape=(shape((4 * UNITS, UNIT, cols), B...]
    ppermute x6 -> x9, waiting for transfers between devices: 0.02 us -> 178 us  [swap(): return lax.ppermute(array, axis, [(0, 1), (1, 0)])]
    ppermute x2 -> x3, waiting for transfers between devices: 92.7 us -> 0.01 us  [turned(): return lax.ppermute(block, ('y', 'c', 'z'), turn_pairs)]
    concatenate x9 -> x5, other arithmetic: 31.8 us -> 8.65 us  [the longest x2 5.29 us: ff_rows(): jnp.concatenate([dot_tn(block, grad_ff).astype(BF16), dot_tn(block, grad_...]
  transfers between devices with their start and end apart: 11 -> 21, of which waited for: 2 -> 3; matrix products, arithmetic and copies ran while one was open for 18% -> 20% of each run, Pallas kernels for 44% -> 46%
where the time goes in v3:
time: 1340 us; the launch traced here: 1320 us
  Pallas kernels  754 us (56%)
  matrix products  193 us (14%)
  waiting for transfers between devices  179 us (13%)
  other arithmetic  82.9 us (6%)
  local copies, waits for them, and re-layouts  74.8 us (6%)
  starting transfers between devices  21.3 us (2%)
  between operations  15.1 us (1%)
    pallas_call x1, Pallas kernels, reduce_grads(): pl.pallas_call(reduce_kernel, out_shape=(shape((4 * UNITS, UNIT, cols), B...  235 us
    ppermute x9, waiting for transfers between devices, swap(): return lax.ppermute(array, axis, [(0, 1), (1, 0)])  178 us
    pallas_call x3, Pallas kernels, scatter_rows(): pl.pallas_call(partial(scatter_kernel, cores), out_shape=jax.ShapeDtypeSt...  174 us
    pallas_call x1, Pallas kernels, front(): pl.pallas_call(partial(front_kernel, docs), out_shape=(shape((4, 2, rows,...  126 us
    pallas_call x2, Pallas kernels, gather_rows(): pl.pallas_call(partial(gather_kernel, cores), out_shape=jax.ShapeDtypeStr...  86.9 us
    dot_general x6, matrix products, dot(): return jnp.dot(left, right, preferred_element_type=F32)  68.5 us
    dot_general x8, matrix products, dot_tn(): lax.dot_general(left, right, (((0,), (0,)), ((), ())), preferred_element_...  68.2 us
    pallas_call x1, Pallas kernels, attend_backward(): pl.pallas_call(partial(backward_kernel, spans, width), grid=(steps + 1,),...  65.1 us
  transfers between devices with their start and end apart: 21, of which 3 were waited for; matrix products, arithmetic and copies ran while one was open for 20% of the time, Pallas kernels for 46%

profile of v3, /device:TPU:4, one launch (start us, length us, event | category | flops | bytes accessed | tf_op | source)
XLA Modules:
  0.0 1320.9 jit_solution(16843539642240360793)
XLA Ops:
  10.9 3.4 constant_dynamic-slice_fusion.13
  14.3 3.0 constant_dynamic-slice_fusion.11
  17.3 4.3 concatenate.81.near
  21.6 4.3 concatenate.82.far
  25.9 126.0 %front.1 = (bf16[4,2,256,2304]{3,2,1,0:T(8,128)(2,1)}, bf16[256,2304]{1,0:T(8,128)(2,1)}, f32[8,2304]{1,0:T(8,128)}, bf16[2,2,576,1728]{3,2,1,0:T(8,128)(2,1)}, ...) custom-call(bf16[256,2304]{1,0:T(8,128)(2,1)} %bitcast.83, ...), custom_call_target="tpu_custom_call" | custom-call | flops 109999996928 | tf_op jit(solution)/shard_map/front/pallas_call | solution.py:301
  151.8 5.0 constant_dynamic-slice_fusion.8
  156.9 5.0 constant_dynamic-slice_fusion.9
  168.9 5.7 collective-permute-start.4
  174.6 12.8 fusion.9.k_raw
  187.4 12.0 convolution_convert_fusion.6.v_ref
  199.4 2.6 constant_dynamic-slice_fusion.10
  202.0 7.2 fusion.11.q_raw
  210.2 42.8 %attend_forward.1 = (bf16[1024,576]{1,0:T(8,128)(2,1)}, bf16[2048,576]{1,0:T(8,128)(2,1)}, bf16[1024,576]{1,0:T(8,128)(2,1)}, f32[1024,576]{1,0:T(8,128)}) custom-call(f32[1024,576]{1,0:T(8,128)} %fusion.11.q_raw, f32[2048,576]{1,0:T(8,128)} %fusion.9.k_raw, bf16[2048,576]{1,0:T(8,128)(2,1)} %convolution_convert_fusion.6.v_ref, ...), custom_call_target="tpu_custom_call" | custom-call | flops 43000000512 | tf_op jit(solution)/shard_map/attend_forward/pallas_call | solution.py:881
  256.8 7.5 convolution_convert_fusion.3
  264.3 78.0 %scatter_rows.3 = f32[256,2304]{1,0:T(8,128)} custom-call(bf16[4,1,256,2304]{3,2,1,0:T(8,128)(2,1)} %bitcast.100), custom_call_target="tpu_custom_call" | custom-call | flops 49999998976 | tf_op jit(solution)/shard_map/scatter_rows/pallas_call | solution.py:413
  342.3 2.8 multiply_reduce_fusion.2
  347.9 44.4 %gather_rows.2 = bf16[4,2,256,2304]{3,2,1,0:T(8,128)(2,1)} custom-call(bf16[256,2304]{1,0:T(8,128)(2,1)} %multiply_convert_fusion.4.block), custom_call_target="tpu_custom_call" | custom-call | flops 44999999488 | tf_op jit(solution)/shard_map/gather_rows/pallas_call | solution.py:136
  392.9 3.7 maximum_select_fusion.3
  396.6 2.7 maximum_select_fusion.2
  400.8 3.0 copy-done.9
  403.8 17.1 %fusion.51 = f32[2048,1440]{0,1:T(8,128)} fusion(bf16[2048,2304]{1,0:T(8,128)(2,1)S(1)} %bitcast.91, bf16[2304,1440]{1,0:T(8,128)(2,1)S(1)} %bitcast.69), kind=kOutput, calls=%fused_computation.134 | convolution fusion | flops 13589544960 | bytes 27869184 | tf_op jit(solution)/shard_map/dot_general | solution.py:27
  420.9 15.9 %multiply_convert_fusion.1 = (bf16[2048,720]{0,1:T(8,128)(2,1)S(1)}, bf16[2048,720]{0,1:T(8,128)(2,1)S(1)}, bf16[2048,720]{0,1:T(8,128)(2,1)S(1)}) fusion(f32[2048,1440]{0,1:T(8,128)} %fusion.51, bf16[2048,2304]{1,0:T(8,128)(2,1)} %all-gather.5.cloned.1.call-done, bf16[1440,2304]{1,0:T(8,128)(2,1)} %param.23, s32[]{:T(128)S(6)} %select_n.156), kind=kOutput, calls=%fused_computation.11 | convolution fusion | flops 6816890880 | bytes 33398788 | tf_op jit(solution)/shard_map/dot_general | solution.py:35
  436.8 3.4 pad_maximum_fusion
  440.7 10.8 convolution_convert_fusion.10
  451.5 11.2 convolution_convert_fusion.8
  462.7 8.9 convolution_convert_fusion.4
  471.6 20.1 %convolution_convert_fusion = bf16[2048,2304]{1,0:T(8,128)(2,1)} fusion(bf16[2304,1440]{1,0:T(8,128)(2,1)} %bitcast.70, bf16[2048,720]{0,1:T(8,128)(2,1)} %copy-done.15, bf16[2048,720]{0,1:T(8,128)(2,1)S(1)} %get-tuple-element.95), kind=kOutput, calls=%fused_computation | convolution fusion | flops 13606060032 | bytes 21970944 | tf_op jit(solution)/shard_map/dot_general | solution.py:35
  491.7 8.8 convolution_convert_fusion.9
  500.6 2.6 pad_maximum_fusion.2
  503.2 8.8 convolution_convert_fusion.7
  512.1 2.6 pad_maximum_fusion.3
  515.6 50.4 %scatter_rows.4 = f32[256,2304]{1,0:T(8,128)} custom-call(bf16[4,2,256,2304]{3,2,1,0:T(8,128)(2,1)} %bitcast.92), custom_call_target="tpu_custom_call" | custom-call | flops 49999998976 | tf_op jit(solution)/shard_map/scatter_rows/pallas_call | solution.py:413
  566.0 3.0 multiply_reduce_fusion
  569.7 3.5 multiply_convert_fusion.3.block
  573.2 42.5 %gather_rows.3 = bf16[4,1,256,2304]{3,2,1,0:T(8,128)(2,1)} custom-call(bf16[256,2304]{1,0:T(8,128)(2,1)} %multiply_convert_fusion.3.block), custom_call_target="tpu_custom_call" | custom-call | flops 44999999488 | tf_op jit(solution)/shard_map/gather_rows/pallas_call | solution.py:136
  615.7 6.2 convolution_convert_fusion.13
  623.3 65.1 %attend_backward.1 = (bf16[1024,576]{1,0:T(8,128)(2,1)}, bf16[1024,576]{1,0:T(8,128)(2,1)}, bf16[1024,576]{1,0:T(8,128)(2,1)}) custom-call(bf16[1024,576]{1,0:T(8,128)(2,1)} %get-tuple-element.64.q_ref, bf16[2048,576]{1,0:T(8,128)(2,1)} %get-tuple-element.65.k_ref, bf16[2048,576]{1,0:T(8,128)(2,1)} %convolution_convert_fusion.6.v_ref, ...), custom_call_target="tpu_custom_call" | custom-call | flops 57000001536 | tf_op jit(solution)/shard_map/attend_backward/pallas_call | solution.py:1028
  688.4 7.0 concatenate.90
  695.5 14.4 %convolution_convert_fusion.2 = bf16[1024,2304]{1,0:T(8,128)(2,1)} fusion(bf16[1024,1728]{1,0:T(8,128)(2,1)} %concatenate.90, bf16[2304,1728]{1,0:T(8,128)(2,1)} %bitcast.96), kind=kOutput, calls=%fused_computation.15 | convolution fusion | flops 8156086272 | bytes 16220160 | tf_op jit(solution)/shard_map/dot_general | solution.py:35
  710.0 45.3 %scatter_rows.5 = f32[256,2304]{1,0:T(8,128)} custom-call(bf16[4,1,256,2304]{3,2,1,0:T(8,128)(2,1)} %bitcast.99), custom_call_target="tpu_custom_call" | custom-call | flops 49999998976 | tf_op jit(solution)/shard_map/scatter_rows/pallas_call | solution.py:413
  755.5 12.0 convolution_convert_fusion.1
  767.5 5.9 copy.54
  773.4 5.8 convolution_convert_fusion.5
  787.8 5.8 copy.62
  793.6 7.5 maximum_select_fusion
  801.2 6.9 convolution_convert_fusion.11
  808.1 6.9 convolution_convert_fusion.12
  815.4 2.9 pad_maximum_fusion.1.grads
  818.3 235.1 %reduce_grads.1 = (bf16[48,16,3584]{2,1,0:T(8,128)(2,1)}, bf16[144,16,1792]{2,1,0:T(8,128)(2,1)}, bf16[24,16,3584]{2,1,0:T(8,128)(2,1)}, f32[8,2304]{1,0:T(8,128)}) custom-call(bf16[4,12,16,3584]{3,2,1,0:T(8,128)(2,1)} %pad_maximum_fusion.1.grads, f32[8,2304]{1,0:T(8,128)} %select_maximum_fusion.gain), custom_call_target="tpu_custom_call" | custom-call | flops 179999997952 | tf_op jit(solution)/shard_map/reduce_grads/pallas_call | solution.py:701
  1053.4 2.5 slice.66
  1056.2 3.4 fusion.47
  1059.6 2.5 collective-permute-start.12
  1062.1 4.0 bitcast_select_fusion.1
  1066.1 5.0 fusion.26
  1071.1 7.0 collective-permute-start.3
  1081.7 100.2 %collective-permute-done.9.far = bf16[576,2880]{1,0:T(8,128)(2,1)} collective-permute-done((bf16[576,2880]{1,0:T(8,128)(2,1)}, bf16[576,2880]{1,0:T(8,128)(2,1)}, u32[]{:S(2)}, u32[]{:S(2)}) %collective-permute-start.9) | collective-permute-done | bytes 3317792 | tf_op jit(solution)/shard_map/ppermute | solution.py:39
  1182.8 15.3 %maximum_convert_fusion.1 = f32[576,2304]{1,0:T(8,128)} fusion(bf16[192,1152]{1,0:T(8,128)(2,1)S(1)} %get-tuple-element.124, bf16[192,1152]{1,0:T(8,128)(2,1)S(1)} %get-tuple-element.125, bf16[192,1152]{1,0:T(8,128)(2,1)S(1)} %get-tuple-element.123, bf16[192,1152]{1,0:T(8,128)(2,1)S(1)} %get-tuple-element.119, bf16[192,1152]{1,0:T(8,128)(2,1)S(1)} %get-tuple-element.120, ...), kind=kLoop, calls=%fused_computation.55 | loop fusion | flops 15925248 | bytes 7962624 | tf_op jit(solution)/shard_map/convert_element_type | solution.py:1292
  1198.2 2.2 broadcast_select_fusion.1
  1200.4 6.0 maximum_convert_fusion
  1206.4 5.6 collective-permute-done.10.near_x
  1212.0 72.6 %collective-permute-done.11.far_x = bf16[576,2880]{1,0:T(8,128)(2,1)} collective-permute-done((bf16[576,2880]{1,0:T(8,128)(2,1)}, bf16[576,2880]{1,0:T(8,128)(2,1)}, u32[]{:S(2)}, u32[]{:S(2)}) %collective-permute-start.11) | collective-permute-done | bytes 3317792 | tf_op jit(solution)/shard_map/ppermute | solution.py:39
  1284.6 24.5 %place_rows.1 = (f32[576,2304]{1,0:T(8,128)}, f32[576,2304]{1,0:T(8,128)}, f32[576,2304]{1,0:T(8,128)}, f32[576,5760]{1,0:T(8,128)}, f32[576,5760]{1,0:T(8,128)}) custom-call(s32[3]{0:T(128)} %pad_add_fusion.flags, bf16[48,16,3584]{2,1,0:T(8,128)(2,1)} %get-tuple-element.71.mine, bf16[576,2880]{1,0:T(8,128)(2,1)} %all-gather.7.cloned.1.call-done.near, ...), custom_call_target="tpu_custom_call" | custom-call | flops 24999999488 | tf_op jit(solution)/shard_map/place_rows/pallas_call | solution.py:793
  1309.1 2.4 copy.69
  1311.5 2.4 copy.70
  (162 shorter events, 37.4 us)
Async XLA Ops:
  7.2 413.7 %all-gather.5.cloned.1.call-start = ((), (), s32[]{:S(2)}) async-start(), calls=%async_computation.5 | async-start | bytes 10616832 | tf_op jit(solution)/shard_map/all_gather | solution.py:1165
  10.9 3.4 copy-start.20
  163.6 229.2 %collective-permute-start.2 = (bf16[576,1440]{1,0:T(8,128)(2,1)}, bf16[576,1440]{1,0:T(8,128)(2,1)}, u32[]{:S(2)}, u32[]{:S(2)}) collective-permute-start(bf16[576,1440]{1,0:T(8,128)(2,1)} %pad_maximum_fusion.6), channel_id=1, source_target_pairs={{0,12},{4,8},{8,4},{12,0},{1,13},{5,9},{9,5},{13,1},{2,14},{6,10},... | collective-permute-start | bytes 4976648 | tf_op jit(solution)/shard_map/ppermute | solution.py:1143
  163.6 5.3 copy-start.30
  165.3 227.5 %collective-permute-start.1 = (bf16[576,1440]{1,0:T(8,128)(2,1)}, bf16[576,1440]{1,0:T(8,128)(2,1)}, u32[]{:S(2)}, u32[]{:S(2)}) collective-permute-start(bf16[576,1440]{1,0:T(8,128)(2,1)} %pad_maximum_fusion.5), channel_id=1, source_target_pairs={{0,8},{8,0},{1,9},{9,1},{2,10},{10,2},{3,11},{11,3},{4,12},{12,4},... | collective-permute-start | bytes 4976648 | tf_op jit(solution)/shard_map/ppermute | solution.py:39
  168.8 227.8 %collective-permute-start = (bf16[576,1440]{1,0:T(8,128)(2,1)}, bf16[576,1440]{1,0:T(8,128)(2,1)}, u32[]{:S(2)}, u32[]{:S(2)}) collective-permute-start(bf16[576,1440]{1,0:T(8,128)(2,1)} %pad_maximum_fusion.4), channel_id=1, source_target_pairs={{0,4},{4,0},{1,5},{5,1},{2,6},{6,2},{3,7},{7,3},{8,12},{12,8},{9,1... | collective-permute-start | bytes 4976648 | tf_op jit(solution)/shard_map/ppermute | solution.py:39
  168.9 85.7 %collective-permute-start.4 = (bf16[256,2304]{1,0:T(8,128)(2,1)S(1)}, bf16[256,2304]{1,0:T(8,128)(2,1)S(1)}, u32[]{:S(2)}, u32[]{:S(2)}) collective-permute-start(bf16[256,2304]{1,0:T(8,128)(2,1)S(1)} %bitcast.84), channel_id=1, source_target_pairs={{0,0},{1,4},{2,8},{3,12},{4,1},{5,5},{6,9},{7,13},{8,2},{9,6},{10,... | collective-permute-start | bytes 3538952 | tf_op jit(solution)/shard_map/ppermute | solution.py:1087
  254.6 90.5 %copy-start.21 = (f32[2304]{0:T(1024)}, f32[2304]{0:T(1024)S(1)}, u32[]{:S(2)}) copy-start(f32[2304]{0:T(1024)S(1)} %get-tuple-element.92) | copy-start | bytes 27652
  254.6 9.7 copy-start.6
  254.6 2.2 copy-start.31
  255.9 439.6 %reduce-scatter.9.cloned.1.call-start = ((), (), s32[]{:S(2)}) async-start(), calls=%async_computation.8 | async-start | bytes 4239360 | tf_op jit(solution)/shard_map/reduce_scatter | solution.py:1217
  264.3 78.0 %copy-start.3 = (bf16[256,2304]{1,0:T(8,128)(2,1)S(1)}, bf16[256,2304]{1,0:T(8,128)(2,1)}, u32[]{:S(2)}) copy-start(bf16[256,2304]{1,0:T(8,128)(2,1)} %get-tuple-element.48) | copy-start | bytes 3538948
  345.2 1.5 copy-start
  345.2 1.5 copy-start.25
  347.9 44.4 %copy-start.12 = (bf16[576,720]{1,0:T(8,128)(2,1)S(1)}, bf16[576,720]{1,0:T(8,128)(2,1)}, u32[]{:S(2)}) copy-start(bf16[576,720]{1,0:T(8,128)(2,1)} %get-tuple-element.104) | copy-start | bytes 2488324
  347.9 44.4 %copy-start.13 = (bf16[576,720]{1,0:T(8,128)(2,1)S(1)}, bf16[576,720]{1,0:T(8,128)(2,1)}, u32[]{:S(2)}) copy-start(bf16[576,720]{1,0:T(8,128)(2,1)} %get-tuple-element.100) | copy-start | bytes 2488324
  392.9 10.9 slice-start.3
  396.6 7.1 slice-start.4
  399.3 4.4 slice-start.5
  400.8 3.0 copy-start.9
  436.8 14.7 %copy-start.15 = (bf16[2048,720]{0,1:T(8,128)(2,1)}, bf16[2048,720]{0,1:T(8,128)(2,1)S(1)}, u32[]{:S(2)}) copy-start(bf16[2048,720]{0,1:T(8,128)(2,1)S(1)} %get-tuple-element.96) | copy-start | bytes 8847364
  436.8 25.9 %copy-start.32 = (bf16[2048,720]{0,1:T(8,128)(2,1)}, bf16[2048,720]{0,1:T(8,128)(2,1)S(1)}, u32[]{:S(2)}) copy-start(bf16[2048,720]{0,1:T(8,128)(2,1)S(1)} %get-tuple-element.97) | copy-start | bytes 8847364
  440.3 51.4 %collective-permute-start.5 = (bf16[2048,1440]{0,1:T(8,128)(2,1)}, bf16[2048,1440]{0,1:T(8,128)(2,1)}, u32[]{:S(2)}, u32[]{:S(2)}) collective-permute-start(bf16[2048,1440]{0,1:T(8,128)(2,1)} %pad_maximum_fusion), channel_id=1, source_target_pairs={{0,4},{4,0},{1,5},{5,1},{2,6},{6,2},{3,7},{7,3},{8,12},{12,8},{9,1... | collective-permute-start | bytes 17694728 | tf_op jit(solution)/shard_map/ppermute | solution.py:39
  440.7 22.0 %slice-start = ((s8[9437184]{0:T(1024)(128)(4,1)}), s8[4194304]{0:T(1024)(128)(4,1)S(1)}, s32[]{:S(2)}) async-start(s8[9437184]{0:T(1024)(128)(4,1)} %bitcast.81), calls=%async_computation.12 | async-start | bytes 8388608
  440.7 22.0 %slice-start.1 = ((s8[9437184]{0:T(1024)(128)(4,1)}), s8[4194304]{0:T(1024)(128)(4,1)S(1)}, s32[]{:S(2)}) async-start(s8[9437184]{0:T(1024)(128)(4,1)} %bitcast.81), calls=%async_computation.13 | async-start | bytes 8388608
  451.5 11.2 slice-start.2
  491.7 8.9 copy-start.19
  503.2 8.9 copy-start.18
  514.8 240.6 %reduce-scatter.11.cloned.1.call-start = ((), (), s32[]{:S(2)}) async-start(), calls=%async_computation.10 | async-start | bytes 4423680 | tf_op jit(solution)/shard_map/reduce_scatter | solution.py:1217
  515.5 302.8 %reduce-scatter.7.cloned.1.call-start = ((), (), s32[]{:S(2)}) async-start(), calls=%async_computation.6 | async-start | bytes 4239360 | tf_op jit(solution)/shard_map/reduce_scatter | solution.py:1217
  515.6 50.4 %copy-start.1 = (f32[256,2304]{1,0:T(8,128)S(1)}, f32[256,2304]{1,0:T(8,128)}, u32[]{:S(2)}) copy-start(f32[256,2304]{1,0:T(8,128)} %copy-done) | copy-start | bytes 7077892
  515.6 50.4 %copy-start.22 = (f32[2304]{0:T(1024)S(1)}, f32[2304]{0:T(1024)}, u32[]{:S(2)}) copy-start(f32[2304]{0:T(1024)} %copy-done.21) | copy-start | bytes 27652
  515.6 50.4 %copy-start.26 = (f32[256]{0:T(256)S(1)}, f32[256]{0:T(256)}, u32[]{:S(2)}) copy-start(f32[256]{0:T(256)} %copy-done.25) | copy-start | bytes 3076
  566.0 3.6 copy-start.7
  569.6 486.2 %all-gather.9.cloned.1.call-start = ((), (), s32[]{:S(2)}) async-start(), calls=%async_computation.9 | async-start | bytes 4239360 | tf_op jit(solution)/shard_map/all_gather | solution.py:1221
  695.5 364.1 %all-gather.11.cloned.1.call-start = ((), (), s32[]{:S(2)}) async-start(), calls=%async_computation.11 | async-start | bytes 4423680 | tf_op jit(solution)/shard_map/all_gather | solution.py:1221
  710.0 45.4 %copy-start.33 = (bf16[2048,720]{0,1:T(8,128)(2,1)S(1)}, bf16[2048,720]{0,1:T(8,128)(2,1)}, u32[]{:S(2)}) copy-start(bf16[2048,720]{0,1:T(8,128)(2,1)} %copy-done.32) | copy-start | bytes 8847364
  755.4 310.7 %reduce-scatter.5.cloned.1.call-start = ((), (), s32[]{:S(2)}) async-start(), calls=%async_computation.4 | async-start | bytes 10616832 | tf_op jit(solution)/shard_map/reduce_scatter | solution.py:1186
  767.4 314.3 %all-gather.7.cloned.1.call-start = ((), (), s32[]{:S(2)}) async-start(), calls=%async_computation.7 | async-start | bytes 4239360 | tf_op jit(solution)/shard_map/all_gather | solution.py:1221
  773.4 9.6 copy-start.29
  773.4 10.5 copy-start.24
  773.4 14.4 %collective-permute-start.7 = (bf16[1024,1728]{0,1:T(8,128)(2,1)}, bf16[1024,1728]{0,1:T(8,128)(2,1)}, u32[]{:S(2)}, u32[]{:S(2)}) collective-permute-start(bf16[1024,1728]{0,1:T(8,128)(2,1)} %copy.54), channel_id=1, source_target_pairs={{0,4},{4,0},{1,5},{5,1},{2,6},{6,2},{3,7},{7,3},{8,12},{12,8},{9,1... | collective-permute-start | bytes 10616840 | tf_op jit(solution)/shard_map/ppermute | solution.py:39
  773.4 10.5 copy-start.8
  779.3 1.5 copy-start.16
  780.8 3.2 copy-start.4
  781.9 4.0 collective-permute-start.8
  782.4 3.5 copy-start.17
  783.1 1.6 copy-start.28
  1055.8 126.1 %collective-permute-start.9 = (bf16[576,2880]{1,0:T(8,128)(2,1)}, bf16[576,2880]{1,0:T(8,128)(2,1)}, u32[]{:S(2)}, u32[]{:S(2)}) collective-permute-start(bf16[576,2880]{1,0:T(8,128)(2,1)} %all-gather.9.cloned.1.call-done), channel_id=1, source_target_pairs={{0,8},{8,0},{1,9},{9,1},{2,10},{10,2},{3,11},{11,3},{4,12},{12,4},... | collective-permute-start | bytes 9953288 | tf_op jit(solution)/shard_map/ppermute | solution.py:39
  1059.6 138.6 %collective-permute-start.12 = (bf16[768,2304]{1,0:T(8,128)(2,1)}, bf16[768,2304]{1,0:T(8,128)(2,1)}, u32[]{:S(2)}, u32[]{:S(2)}) collective-permute-start(bf16[768,2304]{1,0:T(8,128)(2,1)} %all-gather.11.cloned.1.call-done), channel_id=1, source_target_pairs={{0,16},{16,0},{1,17},{17,1},{2,18},{18,2},{3,19},{19,3},{4,20},{20... | collective-permute-start | bytes 10616840 | tf_op jit(solution)/shard_map/ppermute | solution.py:39
  1062.0 4.0 copy-start.2
  1062.0 4.0 copy-start.5
  1062.0 4.0 copy-start.23
  1062.0 4.0 copy-start.27
  1066.1 14.0 %copy-start.11 = (bf16[192,3456]{1,0:T(8,128)(2,1)S(1)}, bf16[192,3456]{1,0:T(8,128)(2,1)}, u32[]{:S(2)}) copy-start(bf16[192,3456]{1,0:T(8,128)(2,1)} %get-tuple-element.122) | copy-start | bytes 3981316
  1071.1 111.6 %copy-start.10 = (bf16[192,3456]{1,0:T(8,128)(2,1)S(1)}, bf16[192,3456]{1,0:T(8,128)(2,1)}, u32[]{:S(2)}) copy-start(bf16[192,3456]{1,0:T(8,128)(2,1)} %get-tuple-element.121) | copy-start | bytes 3981316
  1071.1 127.1 %collective-permute-start.3 = (bf16[256,2304]{1,0:T(8,128)(2,1)}, bf16[256,2304]{1,0:T(8,128)(2,1)}, u32[]{:S(2)}, u32[]{:S(2)}) collective-permute-start(bf16[256,2304]{1,0:T(8,128)(2,1)} %get-tuple-element.117), channel_id=1, source_target_pairs={{0,0},{1,4},{2,8},{3,12},{4,1},{5,5},{6,9},{7,13},{8,2},{9,6},{10,... | collective-permute-start | bytes 3538952 | tf_op jit(solution)/shard_map/ppermute | solution.py:1087
  1078.1 120.1 %collective-permute-start.6 = (bf16[256,2304]{1,0:T(8,128)(2,1)}, bf16[256,2304]{1,0:T(8,128)(2,1)}, u32[]{:S(2)}, u32[]{:S(2)}) collective-permute-start(bf16[256,2304]{1,0:T(8,128)(2,1)} %get-tuple-element.116), channel_id=1, source_target_pairs={{0,0},{1,4},{2,8},{3,12},{4,1},{5,5},{6,9},{7,13},{8,2},{9,6},{10,... | collective-permute-start | bytes 3538952 | tf_op jit(solution)/shard_map/ppermute | solution.py:1087
  1081.7 130.3 %collective-permute-start.10 = (bf16[576,2880]{1,0:T(8,128)(2,1)}, bf16[576,2880]{1,0:T(8,128)(2,1)}, u32[]{:S(2)}, u32[]{:S(2)}) collective-permute-start(bf16[576,2880]{1,0:T(8,128)(2,1)} %all-gather.7.cloned.1.call-done.near), channel_id=1, source_target_pairs={{0,16},{16,0},{1,17},{17,1},{2,18},{18,2},{3,19},{19,3},{4,20},{20... | collective-permute-start | bytes 9953288 | tf_op jit(solution)/shard_map/ppermute | solution.py:39
  1181.9 102.7 %collective-permute-start.11 = (bf16[576,2880]{1,0:T(8,128)(2,1)}, bf16[576,2880]{1,0:T(8,128)(2,1)}, u32[]{:S(2)}, u32[]{:S(2)}) collective-permute-start(bf16[576,2880]{1,0:T(8,128)(2,1)} %collective-permute-done.9.far), channel_id=1, source_target_pairs={{0,16},{16,0},{1,17},{17,1},{2,18},{18,2},{3,19},{19,3},{4,20},{20... | collective-permute-start | bytes 9953288 | tf_op jit(solution)/shard_map/ppermute | solution.py:39
  1182.8 15.4 %copy-start.14 = (bf16[768,2304]{1,0:T(8,128)(2,1)S(1)}, bf16[768,2304]{1,0:T(8,128)(2,1)}, u32[]{:S(2)}) copy-start(bf16[768,2304]{1,0:T(8,128)(2,1)} %all-gather.11.cloned.1.call-done) | copy-start | bytes 10616836
Sparse Core Ops, SparseCore 0:
  256.0 89.7 all-gather.4
  514.9 64.6 reduce-scatter.8
  582.5 66.5 reduce-scatter.10
  651.8 64.5 reduce-scatter.6
  717.8 67.7 all-gather.8
  787.0 91.6 all-gather.10
  882.7 118.1 reduce-scatter.4
  1002.5 67.5 all-gather.6

commit v4 on v3

--- a/solution.py
+++ b/solution.py
@@ -345,24 +345,20 @@
         target[at, :] = total.astype(target.dtype)
 
 
-def scatter_kernel(cores, part, out, side, ready, got_x, got_y, pass_x, pass_y, send, recv):
+def scatter_stages(cores, part, out, side, ready, got_x, got_y, pass_x, pass_y, sems):
     x, y, c = (lax.axis_index(a) for a in PLANE)
     slot = c if cores == 2 else 0
     to_x, to_y, to_c = {"x": 1 - x}, {"y": 1 - y}, {"c": 1 - c}
-    sems = (send, recv)
     rows = part.shape[2]
     half = rows // 2
     top, low = pl.ds(0, half), pl.ds(half, half)
     own, next_x = 2 * x + y, 2 * (1 - x) + y
     next_y, across = 2 * x + 1 - y, 2 * (1 - x) + 1 - y
     order = [across, next_x, next_y, own]
-    meet([to_x, to_y] + ([to_c] if cores == 2 else []))
     from_side = []
     if cores == 2:
         for k, chip in enumerate(order):
-            copy = remote(part.at[chip, 1 - c], side.at[k], sems, k, to_c)
-            copy.start()
-            from_side.append(copy)
+            from_side.append(remote(part.at[chip, 1 - c], side.at[k], sems, k, to_c))
 
     def terms(k, first):
         out_terms = [(part.at[order[k], slot], first)]
@@ -374,36 +370,69 @@
         if cores == 2:
             from_side[k].wait_recv()
 
-    def launch(index, src, dst, device):
-        copy = remote(src, dst, sems, index, device)
-        copy.start()
-        return copy
-
-    arrived(0)
-    add_rows(ready.at[0], 0, half, terms(0, 0))
-    a_x = launch(4, ready.at[0, top], pass_x, to_x)
-    add_rows(ready.at[0], half, half, terms(0, half))
-    a_y = launch(5, ready.at[0, low], pass_y, to_y)
-    arrived(1)
-    add_rows(ready.at[1], 0, half, terms(1, 0))
-    x_top = launch(6, ready.at[1, top], got_x.at[top], to_x)
-    arrived(2)
-    add_rows(ready.at[2], half, half, terms(2, half))
-    y_low = launch(7, ready.at[2, low], got_y.at[low], to_y)
-    a_y.wait_recv()
-    add_rows(ready.at[1], half, half, terms(1, half) + [(pass_y, 0)])
-    x_low = launch(8, ready.at[1, low], got_x.at[low], to_x)
-    a_x.wait_recv()
-    add_rows(ready.at[2], 0, half, terms(2, 0) + [(pass_x, 0)])
-    y_top = launch(9, ready.at[2, top], got_y.at[top], to_y)
-    arrived(3)
-    x_top.wait_recv()
-    y_low.wait_recv()
-    x_low.wait_recv()
-    y_top.wait_recv()
-    add_rows(out, 0, rows, terms(3, 0) + [(got_x, 0), (got_y, 0)])
-    for copy in from_side + [a_x, a_y, x_top, y_low, x_low, y_top]:
-        copy.wait_send()
+    a_x = remote(ready.at[0, top], pass_x, sems, 4, to_x)
+    a_y = remote(ready.at[0, low], pass_y, sems, 5, to_y)
+    x_top = remote(ready.at[1, top], got_x.at[top], sems, 6, to_x)
+    y_low = remote(ready.at[2, low], got_y.at[low], sems, 7, to_y)
+    x_low = remote(ready.at[1, low], got_x.at[low], sems, 8, to_x)
+    y_top = remote(ready.at[2, top], got_y.at[top], sems, 9, to_y)
+
+    def begin():
+        for copy in from_side:
+            copy.start()
+
+    def first_hop():
+        arrived(0)
+        add_rows(ready.at[0], 0, half, terms(0, 0))
+        a_x.start()
+        add_rows(ready.at[0], half, half, terms(0, half))
+        a_y.start()
+        arrived(1)
+        add_rows(ready.at[1], 0, half, terms(1, 0))
+        x_top.start()
+        arrived(2)
+        add_rows(ready.at[2], half, half, terms(2, half))
+        y_low.start()
+
+    def second_hop():
+        a_y.wait_recv()
+        add_rows(ready.at[1], half, half, terms(1, half) + [(pass_y, 0)])
+        x_low.start()
+        a_x.wait_recv()
+        add_rows(ready.at[2], 0, half, terms(2, 0) + [(pass_x, 0)])
+        y_top.start()
+
+    def end():
+        arrived(3)
+        x_top.wait_recv()
+        y_low.wait_recv()
+        x_low.wait_recv()
+        y_top.wait_recv()
+        add_rows(out, 0, rows, terms(3, 0) + [(got_x, 0), (got_y, 0)])
+        for copy in from_side + [a_x, a_y, x_top, y_low, x_low, y_top]:
+            copy.wait_send()
+
+    return begin, first_hop, second_hop, end
+
+
+def scatter_kernel(cores, part, out, *scratch):
+    x, y, c = (lax.axis_index(a) for a in PLANE)
+    meet([{"x": 1 - x}, {"y": 1 - y}] + ([{"c": 1 - c}] if cores == 2 else []))
+    for stage in scatter_stages(cores, part, out, *scratch[:-2], scratch[-2:]):
+        stage()
+
+
+def scatter_scratch(cores, rows, cols):
+    return [
+        pltpu.VMEM((4, rows if cores == 2 else 16, cols), BF16),
+        pltpu.VMEM((3, rows, cols), BF16),
+        pltpu.VMEM((rows, cols), BF16),
+        pltpu.VMEM((rows, cols), BF16),
+        pltpu.VMEM((rows // 2, cols), BF16),
+        pltpu.VMEM((rows // 2, cols), BF16),
+        pltpu.SemaphoreType.DMA((10,)),
+        pltpu.SemaphoreType.DMA((10,)),
+    ]
 
 
 def scatter_rows(partial_rows, cores, ident):
@@ -415,16 +444,7 @@
         out_shape=jax.ShapeDtypeStruct((rows, cols), F32),
         in_specs=[IN_VMEM],
         out_specs=IN_VMEM,
-        scratch_shapes=[
-            pltpu.VMEM((4, rows if cores == 2 else 16, cols), BF16),
-            pltpu.VMEM((3, rows, cols), BF16),
-            pltpu.VMEM((rows, cols), BF16),
-            pltpu.VMEM((rows, cols), BF16),
-            pltpu.VMEM((rows // 2, cols), BF16),
-            pltpu.VMEM((rows // 2, cols), BF16),
-            pltpu.SemaphoreType.DMA((10,)),
-            pltpu.SemaphoreType.DMA((10,)),
-        ],
+        scratch_shapes=scatter_scratch(cores, rows, cols),
         compiler_params=pltpu.CompilerParams(
             collective_id=ident, has_side_effects=True, vmem_limit_bytes=VMEM_LIMIT
         ),
@@ -436,12 +456,16 @@
 PARTS = 3
 UNIT = 48 // PARTS
 OUT_AT, UNITS = 3 * PARTS, 4 * PARTS
+PIECE = 48
 
 
 def reduce_kernel(
-    grads, gain, out, rows_out, out_out, gain_out,
+    grads, gain, far_part, down_part,
+    out, rows_out, out_out, gain_out,
+    far_all, down_all, far_y, far_x, down_x,
     inbox, final, gain_in, rs_send, rs_recv, ag_send, ag_recv, y_send, y_recv, x_send, x_recv,
-    o_send, o_recv, g_send, g_recv, here,
+    o_send, o_recv, g_send, g_recv,
+    ma_send, ma_recv, mx_send, mx_recv, my_send, my_recv, m_here, here,
 ):
     x, y, c = (lax.axis_index(a) for a in PLANE)
     z = lax.axis_index("z")
@@ -640,6 +664,114 @@
             for k, device in enumerate(others):
                 gain_z(k, device).wait_send()
             gain_out[...] = (gain_in[4] + gain_in[5]) + (gain_in[6] + gain_in[7])
+
+    ready = [
+        (far_part, far_all, far_x, 0),
+        (down_part, down_all, down_x, 3),
+    ]
+    counts = [part.shape[0] // PIECE for part, _, _, _ in ready]
+
+    def piece(ref, q, p):
+        return ref.at[q, pl.ds(pl.multiple_of(p * PIECE, 16), PIECE)]
+
+    def own_piece(kind, p):
+        return ready[kind][0].at[pl.ds(pl.multiple_of(p * PIECE, 16), PIECE)]
+
+    def ma_copy(kind, src, q, p, way, device):
+        dst = piece(ready[kind][1], q, p)
+        return copy(src, dst, ma_send.at[kind, way, q, p], ma_recv.at[kind, q, p], device)
+
+    def mx_copy(kind, src, q, p):
+        dst = piece(ready[kind][2], q, p)
+        return copy(src, dst, mx_send.at[kind, q, p], mx_recv.at[kind, q, p], to_x)
+
+    def my_copy(src, q, p):
+        return copy(src, piece(far_y, q, p), my_send.at[q, p], my_recv.at[q, p], to_y)
+
+    def m_stay(kind, p):
+        return pltpu.make_async_copy(
+            own_piece(kind, p), piece(ready[kind][1], z, p), m_here.at[kind, p]
+        )
+
+    def m_spread(kind, src, q, p):
+        if kind == 0:
+            my_copy(src, q, p).start()
+        else:
+            mx_copy(kind, src, q, p).start()
+
+    def m_begin(kind, p):
+        src = own_piece(kind, p)
+
+        @pl.when(z < 3)
+        def _():
+            ma_copy(kind, src, z, p, 0, above).start()
+
+        @pl.when(z > 0)
+        def _():
+            ma_copy(kind, src, z, p, 1, below).start()
+
+        m_spread(kind, src, z, p)
+        m_stay(kind, p).start()
+
+    def m_relay(kind, p, hops):
+        for q in range(4):
+            got = piece(ready[kind][1], q, p)
+
+            @pl.when(z == q + hops)
+            def _():
+                ma_copy(kind, got, q, p, 0, to_x).wait_recv()
+
+                @pl.when(z < 3)
+                def _():
+                    ma_copy(kind, got, q, p, 0, above).start()
+
+                m_spread(kind, got, q, p)
+
+            @pl.when(z == q - hops)
+            def _():
+                ma_copy(kind, got, q, p, 1, to_x).wait_recv()
+
+                @pl.when(z > 0)
+                def _():
+                    ma_copy(kind, got, q, p, 1, below).start()
+
+                m_spread(kind, got, q, p)
+
+    def m_cross(p, hops):
+        for q in range(4):
+            @pl.when((z == q + hops) | (z == q - hops))
+            def _():
+                got = piece(far_y, q, p)
+                my_copy(got, q, p).wait_recv()
+                mx_copy(0, got, q, p).start()
+
+    def m_step(i):
+        for kind, count in enumerate(counts):
+            first = i - ready[kind][3]
+            when_unit(first, count, partial(m_begin, kind))
+            for hops in (1, 2, 3):
+                when_unit(first - hops, count, lambda p: m_relay(kind, p, hops))
+        for hops in (0, 1, 2, 3):
+            when_unit(i - ready[0][3] - 1 - hops, counts[0], lambda p: m_cross(p, hops))
+
+    def m_end():
+        for kind, count in enumerate(counts):
+            @pl.loop(0, count)
+            def _(p):
+                src = own_piece(kind, p)
+                m_stay(kind, p).wait()
+                for q in range(4):
+                    @pl.when((z < 3) & (q <= z))
+                    def _():
+                        ma_copy(kind, src, q, p, 0, to_x).wait_send()
+
+                    @pl.when((z > 0) & (q >= z))
+                    def _():
+                        ma_copy(kind, src, q, p, 1, to_x).wait_send()
+
+                    mx_copy(kind, src, q, p).wait()
+                    if kind == 0:
+                        my_copy(src, q, p).wait_send()
 
     def when_unit(u, last, work):
         @pl.when((u >= 0) & (u < last))
@@ -656,6 +788,9 @@
             when_unit(i - 3 - far, UNITS, lambda u: relay(u, far))
         for far in (0, 1, 2, 3):
             when_unit(i - 4 - far, OUT_AT, lambda u: cross(u, far))
+        m_step(i)
+
+    m_end()
 
     @pl.loop(0, UNITS)
     def _(u):
@@ -694,7 +829,7 @@
                     o_copy(src, q, k, c, 0, to_x).wait_recv()
 
 
-def reduce_grads(grads, gain, ident):
+def reduce_grads(grads, gain, far, down, ident):
     cols = grads.shape[3]
     shape = jax.ShapeDtypeStruct
     dma = pltpu.SemaphoreType.DMA
@@ -705,9 +840,14 @@
             shape((16 * OUT_AT, UNIT, cols // 2), BF16),
             shape((8 * PARTS, UNIT, cols), BF16),
             shape(gain.shape, F32),
+            shape((4,) + far.shape, BF16),
+            shape((4,) + down.shape, BF16),
+            shape((4,) + far.shape, BF16),
+            shape((4,) + far.shape, BF16),
+            shape((4,) + down.shape, BF16),
         ),
-        in_specs=[IN_VMEM] * 2,
-        out_specs=(ANY, ANY, ANY, IN_VMEM),
+        in_specs=[IN_VMEM] * 4,
+        out_specs=(ANY, ANY, ANY, IN_VMEM) + (ANY,) * 5,
         scratch_shapes=[
             pltpu.VMEM((5, UNITS, UNIT, cols), BF16),
             pltpu.VMEM((UNITS, UNIT, cols), BF16),
@@ -724,14 +864,21 @@
             dma((2, 4, PARTS)),
             dma((6,)),
             dma((7,)),
+            dma((2, 2, 4, down.shape[0] // PIECE)),
+            dma((2, 4, down.shape[0] // PIECE)),
+            dma((2, 4, down.shape[0] // PIECE)),
+            dma((2, 4, down.shape[0] // PIECE)),
+            dma((4, far.shape[0] // PIECE)),
+            dma((4, far.shape[0] // PIECE)),
+            dma((2, down.shape[0] // PIECE)),
             dma((UNITS,)),
         ],
         compiler_params=pltpu.CompilerParams(
             collective_id=ident, has_side_effects=True, vmem_limit_bytes=VMEM_LIMIT
         ),
-        cost_estimate=cost(180),
+        cost_estimate=cost(300),
         name="reduce_grads",
-    )(grads, gain)
+    )(grads, gain, far, down)
 
 
 def rows_kernel(cols_f, cols_h, flags, mine, near, far, near_x, far_x, *refs):
@@ -803,6 +950,27 @@
     )(flags, mine, near, far, near_x, far_x, summed, summed, summed, summed)
 
 
+def down_kernel(per_x, flags, own, side, out):
+    mine = flags[0] == pl.program_id(0) // per_x
+    out[...] = jnp.where(mine, own[...].astype(F32), side[...].astype(F32))
+
+
+def place_down(flags, own, side, rows):
+    cols = own.shape[1]
+    per_x = rows // 144
+    source = pl.BlockSpec((144, cols), lambda s: (s % per_x, 0))
+    return pl.pallas_call(
+        partial(down_kernel, per_x),
+        grid=(2 * per_x,),
+        out_shape=jax.ShapeDtypeStruct((2 * rows, cols), F32),
+        in_specs=[pl.BlockSpec(memory_space=pltpu.SMEM), source, source],
+        out_specs=pl.BlockSpec((144, cols), lambda s: (s, 0)),
+        compiler_params=pltpu.CompilerParams(vmem_limit_bytes=VMEM_LIMIT),
+        cost_estimate=cost(8),
+        name="place_down",
+    )(flags, own, side)
+
+
 def lanes(rows):
     return lax.broadcasted_iota(jnp.int32, (rows, LANES), 1)
 
@@ -913,7 +1081,8 @@
 
 def backward_kernel(
     spans, width, q_ref, k_ref, v_ref, g_ref, lse, cos_q, sin_q, cos_k, sin_k, first, place,
-    dq_out, dk_done, dv_done, k_keep, v_keep, dk_out, dv_out, give, got, send, recv,
+    part, dq_out, dk_done, dv_done, rows_out,
+    k_keep, v_keep, dk_out, dv_out, give, got, send, recv, *scatter,
 ):
     step = pl.program_id(0)
     c = lax.axis_index("c")
@@ -930,9 +1099,16 @@
             device_id_type=MESH_ID,
         )
 
+    stages = scatter_stages(2, part, rows_out, *scatter[:-2], scatter[-2:])
+    x, y = lax.axis_index("x"), lax.axis_index("y")
+
     @pl.when(step == 0)
     def _():
-        meet([{"c": 1 - c}])
+        meet([{"x": 1 - x}, {"y": 1 - y}, {"c": 1 - c}])
+
+    last = pl.num_programs(0) - 1
+    for at, stage in zip((0, 1, last - 2, last), stages):
+        pl.when(step == at)(stage)
 
     @pl.when(step > 0)
     def _():
@@ -1012,10 +1188,11 @@
     dk_out[...] = rotated(dk_out[...], cos_k[...], -sin_k[...])
 
 
-def attend_backward(query, key, value, grad, lse, tables, limits, pieces, ident):
+def attend_backward(query, key, value, grad, lse, tables, limits, partial_rows, pieces, ident):
     q_rows, width = query.shape
     k_rows = key.shape[0]
     spans = key_spans(pieces, k_rows // pieces)
+    rows, cols = partial_rows.shape[0] // 8, partial_rows.shape[1]
     steps = -(-width // LANES)
     shape = jax.ShapeDtypeStruct
 
@@ -1028,7 +1205,7 @@
     return pl.pallas_call(
         partial(backward_kernel, spans, width),
         grid=(steps + 1,),
-        out_shape=(shape((q_rows, width), BF16),) * 3,
+        out_shape=(shape((q_rows, width), BF16),) * 3 + (shape((rows, cols), F32),),
         in_specs=[
             this(q_rows),
             this(k_rows),
@@ -1041,18 +1218,23 @@
             whole(k_rows, LANES),
             whole(q_rows, 1),
             whole(q_rows, 1),
+            IN_VMEM,
         ],
-        out_specs=(this(q_rows), last(q_rows), last(q_rows)),
+        out_specs=(this(q_rows), last(q_rows), last(q_rows), IN_VMEM),
         scratch_shapes=[pltpu.VMEM((k_rows, LANES), BF16)] * 2
         + [pltpu.VMEM((k_rows, LANES), F32)] * 2
         + [pltpu.VMEM((steps, 2, q_rows, LANES), BF16)] * 2
-        + [pltpu.SemaphoreType.DMA((steps,))] * 2,
+        + [pltpu.SemaphoreType.DMA((steps,))] * 2
+        + scatter_scratch(2, rows, cols),
         compiler_params=pltpu.CompilerParams(
             collective_id=ident, has_side_effects=True, vmem_limit_bytes=VMEM_LIMIT
         ),
         cost_estimate=cost(57),
         name="attend_backward",
-    )(query, key, value, grad, lse, *tables, *limits)
+    )(
+        query, key, value, grad, lse, *tables, *limits,
+        partial_rows.reshape(4, 2, rows, cols),
+    )
 
 
 def norm_back(grad_normed, unit_rows, rms_rows, gain_rows):
@@ -1147,9 +1329,6 @@
     def ordered(a, b, flag):
         return jnp.where(flag == 0, jnp.stack([a, b]), jnp.stack([b, a]))
 
-    ff_near = ordered(ff_own, ff_c, c)
-    ff_far = ordered(ff_y, ff_yc, c)
-    w_ff = ordered(ff_near, ff_far, y).reshape(4 * rows_d, 2 * cols_f)
     down_use = lax.dynamic_slice_in_dim(w_down, x * cols_f, cols_f, 0)
 
     def own_rows(array):
@@ -1162,8 +1341,6 @@
     place = own_rows(jnp.arange(seq_len, dtype=jnp.int32))
     limits = (first_query, place[:, None])
 
-    grad_mlp = lax.all_gather((BETA * upstream).astype(BF16), PLANE, axis=0, tiled=True)
-
     rms_one = lax.rsqrt(jnp.mean(inputs * inputs, -1, keepdims=True) + EPSILON)
     unit_one = inputs * rms_one
 
@@ -1176,17 +1353,22 @@
     hidden_res = inputs + BETA * attn_out
     rms_two = lax.rsqrt(jnp.mean(hidden_res * hidden_res, -1, keepdims=True) + EPSILON)
     unit_two = hidden_res * rms_two
-    normed_two = gather_rows((unit_two * gain_two).astype(BF16), 2, 3)
+    normed_rows = (unit_two * gain_two).astype(BF16)
+    normed_rows, ff_c, ff_y, ff_yc = lax.optimization_barrier((normed_rows, ff_c, ff_y, ff_yc))
+    normed_two = gather_rows(normed_rows, 2, 3)
+    cot_rows = lax.optimization_barrier(((BETA * upstream).astype(BF16), normed_two))[0]
+    grad_mlp = lax.all_gather(cot_rows, PLANE, axis=0, tiled=True)
+    ff_near = ordered(ff_own, ff_c, c)
+    ff_far = ordered(ff_y, ff_yc, c)
+    w_ff = ordered(ff_near, ff_far, y).reshape(4 * rows_d, 2 * cols_f)
 
     gate_up = dot(normed_two, w_ff)
     gate, up = gate_up[:, :cols_f], gate_up[:, cols_f:]
     sigmoid_gate = jax.nn.sigmoid(gate)
     silu_gate = gate * sigmoid_gate
     activation = (silu_gate * up).astype(BF16)
-    mlp_out = lax.psum_scatter(
-        dot(activation, down_use).astype(BF16), PLANE, scatter_dimension=0, tiled=True
-    ).astype(F32)
-    output = turned((hidden_res + BETA * mlp_out).astype(BF16))[None]
+    mlp_part = dot(activation, down_use).astype(BF16)
+    mlp_part, grad_mlp = lax.optimization_barrier((mlp_part, grad_mlp))
 
     grad_activation = dot_nt(grad_mlp, down_use)
     grad_up = (grad_activation * silu_gate).astype(BF16)
@@ -1216,10 +1398,6 @@
     def sum_z(grad):
         return lax.psum_scatter(grad, "z", scatter_dimension=0, tiled=True)
 
-    def gather_z(part, after):
-        part = lax.optimization_barrier((part, after))[0]
-        return lax.all_gather(part, "z", axis=0, tiled=True)
-
     ff_far, ff_near, grad_down = sum_z(ff_far), sum_z(ff_near), sum_z(grad_down)
     grad_normed_two = scatter_rows(back_part, 2, 4)
 
@@ -1234,14 +1412,16 @@
     give = lax.dynamic_slice_in_dim(grad_out_part, (1 - c) * half, half, 1)
     grad_out_half = (keep.astype(F32) + swap(give, "c").astype(F32)).astype(BF16)
 
-    grad_query, grad_key, grad_value = attend_backward(
-        query, key, value, grad_context, lse, tables, limits, pieces, 8
+    grad_context, ff_far = lax.optimization_barrier((grad_context, ff_far))
+    grad_query, grad_key, grad_value, mlp_out = attend_backward(
+        query, key, value, grad_context, lse, tables, limits, mlp_part, pieces, 8
     )
-    ff_far = swap(gather_z(ff_far, grad_query), "y")
-    ff_near = gather_z(ff_near, grad_query)
     grad_qkv = jnp.concatenate([grad_query, grad_key, grad_value], 1)
 
-    grad_normed_one = scatter_rows(dot_nt(grad_qkv, w_qkv), 1, 6)
+    query_part = dot_nt(grad_qkv, w_qkv).astype(BF16)
+    ff_near = lax.optimization_barrier((ff_near, grad_query))[0]
+    ff_near = lax.all_gather(ff_near, "z", axis=0, tiled=True)
+    grad_normed_one = scatter_rows(query_part, 1, 6)
     grad_qkv_side = swap(grad_qkv, "c")
     grad_qkv_all = (
         jnp.where(
@@ -1253,7 +1433,6 @@
         .transpose(1, 0, 2, 3)
         .reshape(seq_len, 3 * cols_h)
     )
-    grad_down = gather_z(grad_down, grad_normed_one)
     third = rows_d // 12
     width = -(-3 * cols_h // LANES) * LANES
 
@@ -1275,12 +1454,24 @@
     )
     gain_grad_one = jnp.sum(grad_normed_one * unit_one, 0)
     gain_part = jnp.pad(jnp.stack([gain_grad_one, gain_grad_two]), ((0, 6), (0, 0)))
-    mine, summed, out_got, gain_grads = reduce_grads(grads, gain_part, 7)
+    grads, ff_near = lax.optimization_barrier((grads, ff_near))
+    near_x = swap(ff_near, "x")
+    mine, summed, out_got, gain_grads, _, *ff_sums = reduce_grads(
+        grads, gain_part, ff_far, grad_down, 7
+    )
+    down_own, far_y, far_x, down_side = (
+        part.reshape(-1, part.shape[-1]) for part in ff_sums
+    )
+    grad_inputs = grad_hidden + norm_back(grad_normed_one, unit_one, rms_one, gain_one)
+
+    def later(array):
+        return lax.optimization_barrier((array, gain_grads))[0]
+
+    grad_tokens = turned(later(grad_inputs.astype(BF16)))[None]
+    output = turned(later((hidden_res + BETA * mlp_out).astype(BF16)))[None]
     if outer > 1:
         gain_grads = lax.psum(gain_grads, "g")
 
-    grad_inputs = grad_hidden + norm_back(grad_normed_one, unit_one, rms_one, gain_one)
-    grad_tokens = turned(grad_inputs.astype(BF16))[None]
 
     shard = attn_gain.shape[0]
     first = own * rows_d + lax.axis_index("g") * shard
@@ -1293,14 +1484,11 @@
 
     flags = jnp.stack([x, y, c]).astype(jnp.int32)
     *qkv_all, gate_all, up_all = place_rows(
-        flags, mine, summed, ff_near, ff_far, swap(ff_near, "x"), swap(ff_far, "x"),
+        flags, mine, summed, ff_near, far_y, near_x, far_x,
         rows_d, cols_f, cols_h,
     )
     ff_all = (gate_all, up_all)
-    down_own, down_side = grad_down[:cols_f], swap(grad_down, "x")[:cols_f]
-    down_all = jnp.concatenate(
-        [jnp.where(x == 0, down_own, down_side), jnp.where(x == 0, down_side, down_own)], 0
-    )
+    down_all = place_down(flags, down_own, down_side, cols_f)
     out_mine = mine.reshape(4, UNITS, UNIT, 2 * width)[:, OUT_AT:, :, : 3 * half]
     out_mine = out_mine.reshape(4 * third, 3 * half)
     out_got = out_got[:, :, : 3 * half].reshape(2, 4 * third, 3 * half)

time: 1340 us -> 1290 us (0.963)
  waiting for transfers between devices: 179 us -> 84.5 us
  Pallas kernels: 754 us -> 815 us
    ppermute x9 -> x6, waiting for transfers between devices: 178 us -> 2.38 us  [swap(): return lax.ppermute(array, axis, [(0, 1), (1, 0)])]
    pallas_call x1, Pallas kernels: 235 us -> 307 us  [reduce_grads(): pl.pallas_call(reduce_kernel, out_shape=(shape((4 * UNITS, UNIT, cols), B...]
    ppermute x3, waiting for transfers between devices: 0.01 us -> 59.9 us  [turned(): return lax.ppermute(block, ('y', 'c', 'z'), turn_pairs)]
    pallas_call x3, Pallas kernels: 174 us -> 145 us  [scatter_rows(): pl.pallas_call(partial(scatter_kernel, cores), out_shape=jax.ShapeDtypeSt...]
  transfers between devices with their start and end apart: 21 -> 15, of which waited for: 3 -> 5; matrix products, arithmetic and copies ran while one was open for 20% -> 20% of each run, Pallas kernels for 46% -> 24%
where the time goes in v4:
time: 1290 us; the launch traced here: 1280 us
  Pallas kernels  815 us (63%)
  matrix products  201 us (16%)
  waiting for transfers between devices  84.5 us (7%)
  other arithmetic  75 us (6%)
  local copies, waits for them, and re-layouts  68.4 us (5%)
  starting transfers between devices  19.2 us (1%)
  between operations  14.7 us (1%)
    pallas_call x1, Pallas kernels, reduce_grads(): pl.pallas_call(reduce_kernel, out_shape=(shape((4 * UNITS, UNIT, cols), B...  307 us
    pallas_call x3, Pallas kernels, scatter_rows(): pl.pallas_call(partial(scatter_kernel, cores), out_shape=jax.ShapeDtypeSt...  145 us
    pallas_call x1, Pallas kernels, front(): pl.pallas_call(partial(front_kernel, docs), out_shape=(shape((4, 2, rows,...  126 us
    pallas_call x2, Pallas kernels, gather_rows(): pl.pallas_call(partial(gather_kernel, cores), out_shape=jax.ShapeDtypeStr...  87.3 us
    dot_general x6, matrix products, dot(): return jnp.dot(left, right, preferred_element_type=F32)  72.1 us
    dot_general x8, matrix products, dot_tn(): lax.dot_general(left, right, (((0,), (0,)), ((), ())), preferred_element_...  72 us
    pallas_call x1, Pallas kernels, attend_backward(): pl.pallas_call(partial(backward_kernel, spans, width), grid=(steps + 1,),...  69.9 us
    ppermute x3, waiting for transfers between devices, turned(): return lax.ppermute(block, ('y', 'c', 'z'), turn_pairs)  59.9 us
  transfers between devices with their start and end apart: 15, of which 5 were waited for; matrix products, arithmetic and copies ran while one was open for 20% of the time, Pallas kernels for 24%

profile of v4, /device:TPU:4, one launch (start us, length us, event | category | flops | bytes accessed | tf_op | source)
XLA Modules:
  0.0 1278.2 jit_solution(7909413243779604280)
XLA Ops:
  10.9 3.4 constant_dynamic-slice_fusion.13
  14.3 3.0 constant_dynamic-slice_fusion.11
  17.3 4.3 concatenate.78.near
  21.6 4.3 concatenate.79.far
  25.9 125.9 %front.1 = (bf16[4,2,256,2304]{3,2,1,0:T(8,128)(2,1)}, bf16[256,2304]{1,0:T(8,128)(2,1)}, f32[8,2304]{1,0:T(8,128)}, bf16[2,2,576,1728]{3,2,1,0:T(8,128)(2,1)}, ...) custom-call(bf16[256,2304]{1,0:T(8,128)(2,1)} %bitcast.87, ...), custom_call_target="tpu_custom_call" | custom-call | flops 109999996928 | tf_op jit(solution)/shard_map/front/pallas_call | solution.py:301
  151.8 5.0 constant_dynamic-slice_fusion.2
  156.9 5.0 constant_dynamic-slice_fusion.3
  168.9 5.7 collective-permute-start
  174.6 12.8 %fusion.9.k_raw = f32[2048,576]{1,0:T(8,128)} fusion(bf16[2048,2304]{1,0:T(8,128)(2,1)} %bitcast.78, bf16[2304,1728]{1,0:T(8,128)(2,1)} %bitcast.96), kind=kOutput, calls=%fused_computation.39 | convolution fusion | flops 5435817984 | bytes 17104896 | tf_op jit(solution)/shard_map/dot_general | solution.py:27
  187.4 12.0 convolution_convert_fusion.6.v_ref
  199.4 2.6 constant_dynamic-slice_fusion.10
  202.0 7.2 fusion.11.q_raw
  210.2 42.8 %attend_forward.1 = (bf16[1024,576]{1,0:T(8,128)(2,1)}, bf16[2048,576]{1,0:T(8,128)(2,1)}, bf16[1024,576]{1,0:T(8,128)(2,1)}, f32[1024,576]{1,0:T(8,128)}) custom-call(f32[1024,576]{1,0:T(8,128)} %fusion.11.q_raw, f32[2048,576]{1,0:T(8,128)} %fusion.9.k_raw, bf16[2048,576]{1,0:T(8,128)(2,1)} %convolution_convert_fusion.6.v_ref, ...), custom_call_target="tpu_custom_call" | custom-call | flops 43000000512 | tf_op jit(solution)/shard_map/attend_forward/pallas_call | solution.py:1049
  253.0 8.2 convolution_convert_fusion.3
  261.2 48.5 %scatter_rows.3 = f32[256,2304]{1,0:T(8,128)} custom-call(bf16[4,1,256,2304]{3,2,1,0:T(8,128)(2,1)} %bitcast.103), custom_call_target="tpu_custom_call" | custom-call | flops 49999998976 | tf_op jit(solution)/shard_map/scatter_rows/pallas_call | solution.py:442
  309.7 2.8 multiply_reduce_fusion.2
  317.0 44.6 %gather_rows.2 = bf16[4,2,256,2304]{3,2,1,0:T(8,128)(2,1)} custom-call(bf16[256,2304]{1,0:T(8,128)(2,1)} %multiply_convert_fusion.4.block), custom_call_target="tpu_custom_call" | custom-call | flops 44999999488 | tf_op jit(solution)/shard_map/gather_rows/pallas_call | solution.py:136
  362.5 3.8 maximum_select_fusion.3
  366.3 2.7 maximum_select_fusion.2
  370.5 19.9 %fusion.51 = f32[2048,1440]{0,1:T(8,128)S(1)} fusion(bf16[2048,2304]{1,0:T(8,128)(2,1)} %bitcast.90, bf16[2304,1440]{1,0:T(8,128)(2,1)S(1)} %bitcast.74), kind=kOutput, calls=%fused_computation.131 | convolution fusion | flops 13589544960 | bytes 27869184 | tf_op jit(solution)/shard_map/dot_general | solution.py:27
  392.3 3.6 copy-done.4
  397.4 12.1 convolution_convert_fusion.1
  409.6 11.6 all-gather.3.cloned.1.call-done
  421.1 15.6 %multiply_convert_fusion.1 = (bf16[2048,720]{0,1:T(8,128)(2,1)S(1)}, bf16[2048,720]{0,1:T(8,128)(2,1)S(1)}) fusion(f32[2048,1440]{0,1:T(8,128)} %copy-done.4, bf16[2048,2304]{1,0:T(8,128)(2,1)} %all-gather.3.cloned.1.call-done, bf16[1440,2304]{1,0:T(8,128)(2,1)} %param.23, s32[]{:T(128)S(6)} %select_n.144), kind=kOutput, calls=%fused_computation.10 | convolution fusion | flops 6813941760 | bytes 30449668 | tf_op jit(solution)/shard_map/dot_general | solution.py:35
  436.8 3.5 pad_maximum_fusion
  440.5 10.7 convolution_convert_fusion.10
  451.2 11.5 convolution_convert_fusion.8
  462.7 12.5 convolution_convert_fusion.4
  475.2 20.1 %convolution_convert_fusion = bf16[2048,2304]{1,0:T(8,128)(2,1)} fusion(bf16[2304,1440]{1,0:T(8,128)(2,1)} %bitcast.75, bf16[2048,720]{0,1:T(8,128)(2,1)} %copy-done.16, bf16[2048,720]{0,1:T(8,128)(2,1)S(1)} %get-tuple-element.127), kind=kOutput, calls=%fused_computation | convolution fusion | flops 13606060032 | bytes 21970944 | tf_op jit(solution)/shard_map/dot_general | solution.py:35
  495.4 8.8 convolution_convert_fusion.9
  504.2 2.6 pad_maximum_fusion.2
  506.9 8.8 convolution_convert_fusion.7
  515.7 2.6 pad_maximum_fusion.3
  518.5 50.6 %scatter_rows.4 = f32[256,2304]{1,0:T(8,128)} custom-call(bf16[4,2,256,2304]{3,2,1,0:T(8,128)(2,1)} %bitcast.95), custom_call_target="tpu_custom_call" | custom-call | flops 49999998976 | tf_op jit(solution)/shard_map/scatter_rows/pallas_call | solution.py:442
  569.1 3.0 multiply_reduce_fusion
  572.8 3.5 multiply_convert_fusion.3.block
  576.3 42.6 %gather_rows.3 = bf16[4,1,256,2304]{3,2,1,0:T(8,128)(2,1)} custom-call(bf16[256,2304]{1,0:T(8,128)(2,1)} %multiply_convert_fusion.3.block), custom_call_target="tpu_custom_call" | custom-call | flops 44999999488 | tf_op jit(solution)/shard_map/gather_rows/pallas_call | solution.py:136
  618.9 7.3 convolution_convert_fusion.13.g_ref
  626.2 69.9 %attend_backward.1 = (bf16[1024,576]{1,0:T(8,128)(2,1)}, bf16[1024,576]{1,0:T(8,128)(2,1)}, bf16[1024,576]{1,0:T(8,128)(2,1)}, f32[256,2304]{1,0:T(8,128)}) custom-call(bf16[1024,576]{1,0:T(8,128)(2,1)} %get-tuple-element.75.q_ref, bf16[2048,576]{1,0:T(8,128)(2,1)} %get-tuple-element.76.k_ref, bf16[2048,576]{1,0:T(8,128)(2,1)} %convolution_convert_fusion.6.v_ref, ...), custom_call_target="tpu_custom_call" | custom-call | flops 57000001536 | tf_op jit(solution)/shard_map/attend_backward/pallas_call | solution.py:1205
  696.4 5.7 convolution_convert_fusion.5
  704.4 2.4 collective-permute-done.6
  710.8 6.4 concatenate.87
  717.1 14.3 %convolution_convert_fusion.2 = bf16[1024,2304]{1,0:T(8,128)(2,1)} fusion(bf16[1024,1728]{1,0:T(8,128)(2,1)} %concatenate.87, bf16[2304,1728]{1,0:T(8,128)(2,1)} %bitcast.99), kind=kOutput, calls=%fused_computation.14 | convolution fusion | flops 8156086272 | bytes 16220160 | tf_op jit(solution)/shard_map/dot_general | solution.py:35
  731.4 5.9 copy.43
  737.6 45.4 %scatter_rows.5 = f32[256,2304]{1,0:T(8,128)} custom-call(bf16[4,1,256,2304]{3,2,1,0:T(8,128)(2,1)} %bitcast.102), custom_call_target="tpu_custom_call" | custom-call | flops 49999998976 | tf_op jit(solution)/shard_map/scatter_rows/pallas_call | solution.py:442
  783.2 2.5 fusion.23
  786.4 4.4 fusion.27
  790.8 5.8 copy.52
  796.5 7.4 maximum_select_fusion
  803.9 6.9 convolution_convert_fusion.11
  810.8 7.0 convolution_convert_fusion.12
  819.2 2.9 pad_maximum_fusion.1.grads
  822.1 10.5 reduce-scatter.8.cloned.1.call-done.down_part
  832.6 307.1 %reduce_grads.1 = (bf16[48,16,3584]{2,1,0:T(8,128)(2,1)}, bf16[144,16,1792]{2,1,0:T(8,128)(2,1)}, bf16[24,16,3584]{2,1,0:T(8,128)(2,1)}, f32[8,2304]{1,0:T(8,128...) custom-call(bf16[4,12,16,3584]{3,2,1,0:T(8,128)(2,1)} %pad_maximum_f, ...), custom_call_target="tpu_custom_call" | custom-call | flops 299999985664 | tf_op jit(solution)/shard_map/reduce_grads/pallas_call | solution.py:836
  1139.7 1.9 collective-permute-start.7
  1141.7 5.7 collective-permute-start.8
  1148.9 2.5 collective-permute-start.9
  1151.4 1.9 fusion.47
  1155.5 15.3 %maximum_convert_fusion = f32[576,2304]{1,0:T(8,128)} fusion(bf16[192,1152]{1,0:T(8,128)(2,1)S(1)} %get-tuple-element.153, bf16[192,1152]{1,0:T(8,128)(2,1)S(1)} %get-tuple-element.154, bf16[192,1152]{1,0:T(8,128)(2,1)S(1)} %get-tuple-element.152, bf16[192,1152]{1,0:T(8,128)(2,1)S(1)} %get-tuple-element.148, bf16[192,1152]{1,0:T(8,128)(2,1)S(1)} %get-tuple-element.149, ...), kind=kLoop, calls=%fused_computation.52 | loop fusion | flops 15925248 | bytes 7962624 | tf_op jit(solution)/shard_map/convert_element_type | solution.py:1483
  1170.8 12.8 %place_down.1 = f32[1440,2304]{1,0:T(8,128)} custom-call(s32[3]{0:T(128)} %pad_add_fusion.flags, bf16[768,2304]{1,0:T(8,128)(2,1)} %bitcast.104, bf16[768,2304]{1,0:T(8,128)(2,1)} %bitcast.105), custom_call_target="tpu_custom_call" | custom-call | flops 8000000000 | tf_op jit(solution)/shard_map/place_down/pallas_call | solution.py:962
  1183.6 38.1 %collective-permute-done.7 = bf16[256,2304]{1,0:T(8,128)(2,1)S(1)} collective-permute-done((bf16[256,2304]{1,0:T(8,128)(2,1)S(1)}, bf16[256,2304]{1,0:T(8,128)(2,1)S(1)}, u32[]{:S(2)}, u32[]{:S(2)}) %collective-permute-start.7) | collective-permute-done | bytes 1179680 | tf_op jit(solution)/shard_map/ppermute | solution.py:1269
  1221.7 21.8 %collective-permute-done.8 = bf16[256,2304]{1,0:T(8,128)(2,1)} collective-permute-done((bf16[256,2304]{1,0:T(8,128)(2,1)S(1)}, bf16[256,2304]{1,0:T(8,128)(2,1)}, u32[]{:S(2)}, u32[]{:S(2)}) %collective-permute-start.8) | collective-permute-done | bytes 1179680 | tf_op jit(solution)/shard_map/ppermute | solution.py:1269
  1243.5 24.5 %place_rows.1 = (f32[576,2304]{1,0:T(8,128)}, f32[576,2304]{1,0:T(8,128)}, f32[576,2304]{1,0:T(8,128)}, f32[576,5760]{1,0:T(8,128)}, f32[576,5760]{1,0:T(8,128)}) custom-call(s32[3]{0:T(128)} %pad_add_fusion.flags, bf16[48,16,3584]{2,1,0:T(8,128)(2,1)} %get-tuple-element.104.mine, bf16[576,2880]{1,0:T(8,128)(2,1)} %all-gather.5.cloned.1.call-done.near, ...), custom_call_target="tpu_custom_call" | custom-call | flops 24999999488 | tf_op jit(solution)/shard_map/place_rows/pallas_call | solution.py:940
  1269.1 2.4 copy.60
  (136 shorter events, 36.4 us)
Async XLA Ops:
  7.2 413.9 %all-gather.3.cloned.1.call-start = ((), (), s32[]{:S(2)}) async-start(), calls=%async_computation.3 | async-start | bytes 10616832 | tf_op jit(solution)/shard_map/all_gather | solution.py:1360
  10.9 3.4 copy-start.23
  163.6 153.4 %collective-permute-start.1 = (bf16[576,1440]{1,0:T(8,128)(2,1)}, bf16[576,1440]{1,0:T(8,128)(2,1)}, u32[]{:S(2)}, u32[]{:S(2)}) collective-permute-start(bf16[576,1440]{1,0:T(8,128)(2,1)} %pad_maximum_fusion.4), channel_id=1, source_target_pairs={{0,4},{4,0},{1,5},{5,1},{2,6},{6,2},{3,7},{7,3},{8,12},{12,8},{9,1... | collective-permute-start | bytes 4976648 | tf_op jit(solution)/shard_map/ppermute | solution.py:39
  163.7 5.2 copy-start.35
  165.5 151.6 %collective-permute-start.2 = (bf16[576,1440]{1,0:T(8,128)(2,1)}, bf16[576,1440]{1,0:T(8,128)(2,1)}, u32[]{:S(2)}, u32[]{:S(2)}) collective-permute-start(bf16[576,1440]{1,0:T(8,128)(2,1)} %pad_maximum_fusion.5), channel_id=1, source_target_pairs={{0,8},{8,0},{1,9},{9,1},{2,10},{10,2},{3,11},{11,3},{4,12},{12,4},... | collective-permute-start | bytes 4976648 | tf_op jit(solution)/shard_map/ppermute | solution.py:39
  167.2 149.9 %collective-permute-start.3 = (bf16[576,1440]{1,0:T(8,128)(2,1)}, bf16[576,1440]{1,0:T(8,128)(2,1)}, u32[]{:S(2)}, u32[]{:S(2)}) collective-permute-start(bf16[576,1440]{1,0:T(8,128)(2,1)} %pad_maximum_fusion.6), channel_id=1, source_target_pairs={{0,12},{4,8},{8,4},{12,0},{1,13},{5,9},{9,5},{13,1},{2,14},{6,10},... | collective-permute-start | bytes 4976648 | tf_op jit(solution)/shard_map/ppermute | solution.py:1325
  168.9 146.7 %collective-permute-start = (bf16[256,2304]{1,0:T(8,128)(2,1)S(1)}, bf16[256,2304]{1,0:T(8,128)(2,1)S(1)}, u32[]{:S(2)}, u32[]{:S(2)}) collective-permute-start(bf16[256,2304]{1,0:T(8,128)(2,1)S(1)} %bitcast.88), channel_id=1, source_target_pairs={{0,0},{1,4},{2,8},{3,12},{4,1},{5,5},{6,9},{7,13},{8,2},{9,6},{10,... | collective-permute-start | bytes 3538952 | tf_op jit(solution)/shard_map/ppermute | solution.py:1269
  261.2 48.5 %copy-start.5 = (bf16[256,2304]{1,0:T(8,128)(2,1)S(1)}, bf16[256,2304]{1,0:T(8,128)(2,1)}, u32[]{:S(2)}) copy-start(bf16[256,2304]{1,0:T(8,128)(2,1)} %get-tuple-element.64) | copy-start | bytes 3538948
  312.6 1.8 copy-start
  312.6 3.0 copy-start.29
  314.3 1.3 copy-start.24
  315.6 46.1 %copy-start.7 = (bf16[256,2304]{1,0:T(8,128)(2,1)}, bf16[256,2304]{1,0:T(8,128)(2,1)S(1)}, u32[]{:S(2)}) copy-start(bf16[256,2304]{1,0:T(8,128)(2,1)S(1)} %collective-permute-done) | copy-start | bytes 3538948
  317.0 45.0 %copy-start.12 = (bf16[576,720]{1,0:T(8,128)(2,1)S(1)}, bf16[576,720]{1,0:T(8,128)(2,1)}, u32[]{:S(2)}) copy-start(bf16[576,720]{1,0:T(8,128)(2,1)} %get-tuple-element.133) | copy-start | bytes 2488324
  317.0 45.0 %copy-start.13 = (bf16[576,720]{1,0:T(8,128)(2,1)S(1)}, bf16[576,720]{1,0:T(8,128)(2,1)}, u32[]{:S(2)}) copy-start(bf16[576,720]{1,0:T(8,128)(2,1)} %get-tuple-element.129) | copy-start | bytes 2488324
  361.7 264.5 %reduce-scatter.4.cloned.1.call-start = ((), (), s32[]{:S(2)}) async-start(), calls=%async_computation.4 | async-start | bytes 4239360 | tf_op jit(solution)/shard_map/reduce_scatter | solution.py:1399
  370.5 19.9 %copy-start.10 = (bf16[2,2,576,1440]{3,2,1,0:T(8,128)(2,1)}, bf16[2,2,576,1440]{3,2,1,0:T(8,128)(2,1)S(1)}, u32[]{:S(2)}) copy-start(bf16[2,2,576,1440]{3,2,1,0:T(8,128)(2,1)S(1)} %maximum_select_fusion.1) | copy-start | bytes 19906564
  390.4 5.5 copy-start.4
  395.8 1.6 copy-start.14
  436.7 14.4 %copy-start.16 = (bf16[2048,720]{0,1:T(8,128)(2,1)}, bf16[2048,720]{0,1:T(8,128)(2,1)S(1)}, u32[]{:S(2)}) copy-start(bf16[2048,720]{0,1:T(8,128)(2,1)S(1)} %get-tuple-element.128) | copy-start | bytes 8847364
  440.2 55.1 %collective-permute-start.4 = (bf16[2048,1440]{0,1:T(8,128)(2,1)}, bf16[2048,1440]{0,1:T(8,128)(2,1)}, u32[]{:S(2)}, u32[]{:S(2)}) collective-permute-start(bf16[2048,1440]{0,1:T(8,128)(2,1)} %pad_maximum_fusion), channel_id=1, source_target_pairs={{0,4},{4,0},{1,5},{5,1},{2,6},{6,2},{3,7},{7,3},{8,12},{12,8},{9,1... | collective-permute-start | bytes 17694728 | tf_op jit(solution)/shard_map/ppermute | solution.py:39
  451.2 11.5 copy-start.15
  495.3 8.9 copy-start.18
  506.9 8.9 copy-start.17
  518.4 177.7 %reduce-scatter.6.cloned.1.call-start = ((), (), s32[]{:S(2)}) async-start(), calls=%async_computation.5 | async-start | bytes 4239360 | tf_op jit(solution)/shard_map/reduce_scatter | solution.py:1399
  518.4 50.7 %copy-start.1 = (f32[256,2304]{1,0:T(8,128)S(1)}, f32[256,2304]{1,0:T(8,128)}, u32[]{:S(2)}) copy-start(f32[256,2304]{1,0:T(8,128)} %copy-done) | copy-start | bytes 7077892
  518.5 50.7 %copy-start.25 = (f32[2304]{0:T(1024)S(1)}, f32[2304]{0:T(1024)}, u32[]{:S(2)}) copy-start(f32[2304]{0:T(1024)} %copy-done.24) | copy-start | bytes 27652
  518.5 50.7 %copy-start.30 = (f32[256]{0:T(256)S(1)}, f32[256]{0:T(256)}, u32[]{:S(2)}) copy-start(f32[256]{0:T(256)} %copy-done.29) | copy-start | bytes 3076
  569.1 3.6 copy-start.8
  572.7 249.4 %all-gather.5.cloned.1.call-start = ((), (), s32[]{:S(2)}) async-start(), calls=%async_computation.6 | async-start | bytes 4239360 | tf_op jit(solution)/shard_map/all_gather | solution.py:1423
  576.3 42.6 %copy-start.34 = (bf16[576,2304]{1,0:T(8,128)(2,1)S(1)}, bf16[576,2304]{1,0:T(8,128)(2,1)}, u32[]{:S(2)}) copy-start(bf16[576,2304]{1,0:T(8,128)(2,1)} %w_out.1) | copy-start | bytes 7962628
  696.2 136.5 %reduce-scatter.8.cloned.1.call-start = ((), (), s32[]{:S(2)}) async-start(), calls=%async_computation.7 | async-start | bytes 4423680 | tf_op jit(solution)/shard_map/reduce_scatter | solution.py:1399
  696.4 8.0 copy-start.33
  696.4 8.0 copy-start.28
  703.3 3.5 collective-permute-start.6
  708.5 1.7 copy-start.19
  708.6 2.2 copy-start.20
  737.3 53.5 %collective-permute-start.5 = (bf16[1024,1728]{0,1:T(8,128)(2,1)}, bf16[1024,1728]{0,1:T(8,128)(2,1)}, u32[]{:S(2)}, u32[]{:S(2)}) collective-permute-start(bf16[1024,1728]{0,1:T(8,128)(2,1)} %copy.43), channel_id=1, source_target_pairs={{0,4},{4,0},{1,5},{5,1},{2,6},{6,2},{3,7},{7,3},{8,12},{12,8},{9,1... | collective-permute-start | bytes 10616840 | tf_op jit(solution)/shard_map/ppermute | solution.py:39
  737.6 45.5 %copy-start.6 = (bf16[256,2304]{1,0:T(8,128)(2,1)S(1)}, bf16[256,2304]{1,0:T(8,128)(2,1)}, u32[]{:S(2)}) copy-start(bf16[256,2304]{1,0:T(8,128)(2,1)} %get-tuple-element.64) | copy-start | bytes 3538948
  737.6 45.5 %copy-start.27 = (f32[2304]{0:T(1024)S(1)}, f32[2304]{0:T(1024)}, u32[]{:S(2)}) copy-start(f32[2304]{0:T(1024)} %get-tuple-element.123) | copy-start | bytes 27652
  737.6 48.7 %copy-start.3 = (f32[256,2304]{1,0:T(8,128)S(1)}, f32[256,2304]{1,0:T(8,128)}, u32[]{:S(2)}) copy-start(f32[256,2304]{1,0:T(8,128)} %scatter_rows.4) | copy-start | bytes 7077892
  783.1 3.3 copy-start.2
  783.1 3.3 copy-start.9
  783.1 3.3 copy-start.26
  783.1 3.3 copy-start.31
  783.1 3.3 copy-start.32
  817.8 1.4 copy-start.11
  832.6 307.1 %copy-start.22 = (bf16[256,2304]{1,0:T(8,128)(2,1)S(1)}, bf16[256,2304]{1,0:T(8,128)(2,1)}, u32[]{:S(2)}) copy-start(bf16[256,2304]{1,0:T(8,128)(2,1)} %get-tuple-element.102) | copy-start | bytes 3538948
  832.6 309.0 %copy-start.21 = (bf16[256,2304]{1,0:T(8,128)(2,1)S(1)}, bf16[256,2304]{1,0:T(8,128)(2,1)}, u32[]{:S(2)}) copy-start(bf16[256,2304]{1,0:T(8,128)(2,1)} %get-tuple-element.103) | copy-start | bytes 3538948
  1139.7 82.0 %collective-permute-start.7 = (bf16[256,2304]{1,0:T(8,128)(2,1)S(1)}, bf16[256,2304]{1,0:T(8,128)(2,1)S(1)}, u32[]{:S(2)}, u32[]{:S(2)}) collective-permute-start(bf16[256,2304]{1,0:T(8,128)(2,1)S(1)} %copy-done.22), channel_id=1, source_target_pairs={{0,0},{1,4},{2,8},{3,12},{4,1},{5,5},{6,9},{7,13},{8,2},{9,6},{10,... | collective-permute-start | bytes 3538952 | tf_op jit(solution)/shard_map/ppermute | solution.py:1269
  1141.7 101.9 %collective-permute-start.8 = (bf16[256,2304]{1,0:T(8,128)(2,1)S(1)}, bf16[256,2304]{1,0:T(8,128)(2,1)}, u32[]{:S(2)}, u32[]{:S(2)}) collective-permute-start(bf16[256,2304]{1,0:T(8,128)(2,1)S(1)} %copy-done.21), channel_id=1, source_target_pairs={{0,0},{1,4},{2,8},{3,12},{4,1},{5,5},{6,9},{7,13},{8,2},{9,6},{10,... | collective-permute-start | bytes 3538952 | tf_op jit(solution)/shard_map/ppermute | solution.py:1269
  1148.9 94.6 %collective-permute-start.9 = (bf16[576,2880]{1,0:T(8,128)(2,1)}, bf16[576,2880]{1,0:T(8,128)(2,1)}, u32[]{:S(2)}, u32[]{:S(2)}) collective-permute-start(bf16[576,2880]{1,0:T(8,128)(2,1)} %all-gather.5.cloned.1.call-done.near), channel_id=1, source_target_pairs={{0,16},{16,0},{1,17},{17,1},{2,18},{18,2},{3,19},{19,3},{4,20},{20... | collective-permute-start | bytes 9953288 | tf_op jit(solution)/shard_map/ppermute | solution.py:39
Sparse Core Ops, SparseCore 0:
  361.9 59.2 all-gather.2
  518.5 64.6 reduce-scatter.3
  586.1 64.4 reduce-scatter.5
  696.3 68.5 all-gather.4
  767.6 64.9 reduce-scatter.7

commit v5 on v4

--- a/solution.py
+++ b/solution.py
@@ -667,7 +667,7 @@
 
     ready = [
         (far_part, far_all, far_x, 0),
-        (down_part, down_all, down_x, 3),
+        (down_part, down_all, down_x, 0),
     ]
     counts = [part.shape[0] // PIECE for part, _, _, _ in ready]
 
@@ -1412,15 +1412,14 @@
     give = lax.dynamic_slice_in_dim(grad_out_part, (1 - c) * half, half, 1)
     grad_out_half = (keep.astype(F32) + swap(give, "c").astype(F32)).astype(BF16)
 
-    grad_context, ff_far = lax.optimization_barrier((grad_context, ff_far))
+    grad_context, ff_near = lax.optimization_barrier((grad_context, ff_near))
+    ff_near = lax.all_gather(ff_near, "z", axis=0, tiled=True)
     grad_query, grad_key, grad_value, mlp_out = attend_backward(
         query, key, value, grad_context, lse, tables, limits, mlp_part, pieces, 8
     )
     grad_qkv = jnp.concatenate([grad_query, grad_key, grad_value], 1)
 
     query_part = dot_nt(grad_qkv, w_qkv).astype(BF16)
-    ff_near = lax.optimization_barrier((ff_near, grad_query))[0]
-    ff_near = lax.all_gather(ff_near, "z", axis=0, tiled=True)
     grad_normed_one = scatter_rows(query_part, 1, 6)
     grad_qkv_side = swap(grad_qkv, "c")
     grad_qkv_all = (

time: 1290 us -> 1270 us (0.984)
  Pallas kernels: 815 us -> 797 us
    pallas_call x1, Pallas kernels: 307 us -> 290 us  [reduce_grads(): pl.pallas_call(reduce_kernel, out_shape=(shape((4 * UNITS, UNIT, cols), B...]
  transfers between devices with their start and end apart: 15 -> 15, of which waited for: 5 -> 5; matrix products, arithmetic and copies ran while one was open for 20% -> 21% of each run, Pallas kernels for 24% -> 25%
where the time goes in v5:
time: 1270 us; the launch traced here: 1260 us
  Pallas kernels  797 us (63%)
  matrix products  202 us (16%)
  waiting for transfers between devices  85.8 us (7%)
  other arithmetic  72.2 us (6%)
  local copies, waits for them, and re-layouts  68.3 us (5%)
  starting transfers between devices  18.7 us (1%)
  between operations  15 us (1%)
    pallas_call x1, Pallas kernels, reduce_grads(): pl.pallas_call(reduce_kernel, out_shape=(shape((4 * UNITS, UNIT, cols), B...  290 us
    pallas_call x3, Pallas kernels, scatter_rows(): pl.pallas_call(partial(scatter_kernel, cores), out_shape=jax.ShapeDtypeSt...  144 us
    pallas_call x1, Pallas kernels, front(): pl.pallas_call(partial(front_kernel, docs), out_shape=(shape((4, 2, rows,...  126 us
    pallas_call x2, Pallas kernels, gather_rows(): pl.pallas_call(partial(gather_kernel, cores), out_shape=jax.ShapeDtypeStr...  87.1 us
    dot_general x6, matrix products, dot(): return jnp.dot(left, right, preferred_element_type=F32)  72.1 us
    dot_general x8, matrix products, dot_tn(): lax.dot_general(left, right, (((0,), (0,)), ((), ())), preferred_element_...  72 us
    pallas_call x1, Pallas kernels, attend_backward(): pl.pallas_call(partial(backward_kernel, spans, width), grid=(steps + 1,),...  69.5 us
    ppermute x3, waiting for transfers between devices, turned(): return lax.ppermute(block, ('y', 'c', 'z'), turn_pairs)  63.7 us
  transfers between devices with their start and end apart: 15, of which 5 were waited for; matrix products, arithmetic and copies ran while one was open for 21% of the time, Pallas kernels for 25%

profile of v5, /device:TPU:4, one launch (start us, length us, event | category | flops | bytes accessed | tf_op | source)
XLA Modules:
  0.0 1259.1 jit_solution(5572868188120869893)
XLA Ops:
  10.9 3.4 constant_dynamic-slice_fusion.13
  14.3 3.0 constant_dynamic-slice_fusion.11
  17.3 4.3 concatenate.78.near
  21.6 4.3 concatenate.79.far
  25.9 125.9 %front.1 = (bf16[4,2,256,2304]{3,2,1,0:T(8,128)(2,1)}, bf16[256,2304]{1,0:T(8,128)(2,1)}, f32[8,2304]{1,0:T(8,128)}, bf16[2,2,576,1728]{3,2,1,0:T(8,128)(2,1)}, ...) custom-call(bf16[256,2304]{1,0:T(8,128)(2,1)} %bitcast.87, ...), custom_call_target="tpu_custom_call" | custom-call | flops 109999996928 | tf_op jit(solution)/shard_map/front/pallas_call | solution.py:301
  151.8 5.0 constant_dynamic-slice_fusion.2
  156.8 5.0 constant_dynamic-slice_fusion.3
  168.9 5.7 collective-permute-start
  174.5 12.8 %fusion.9.k_raw = f32[2048,576]{1,0:T(8,128)} fusion(bf16[2048,2304]{1,0:T(8,128)(2,1)} %bitcast.78, bf16[2304,1728]{1,0:T(8,128)(2,1)} %bitcast.96), kind=kOutput, calls=%fused_computation.39 | convolution fusion | flops 5435817984 | bytes 17104896 | tf_op jit(solution)/shard_map/dot_general | solution.py:27
  187.4 12.0 convolution_convert_fusion.6.v_ref
  199.3 2.6 constant_dynamic-slice_fusion.10
  202.0 7.2 fusion.11.q_raw
  210.2 42.8 %attend_forward.1 = (bf16[1024,576]{1,0:T(8,128)(2,1)}, bf16[2048,576]{1,0:T(8,128)(2,1)}, bf16[1024,576]{1,0:T(8,128)(2,1)}, f32[1024,576]{1,0:T(8,128)}) custom-call(f32[1024,576]{1,0:T(8,128)} %fusion.11.q_raw, f32[2048,576]{1,0:T(8,128)} %fusion.9.k_raw, bf16[2048,576]{1,0:T(8,128)(2,1)} %convolution_convert_fusion.6.v_ref, ...), custom_call_target="tpu_custom_call" | custom-call | flops 43000000512 | tf_op jit(solution)/shard_map/attend_forward/pallas_call | solution.py:1049
  253.0 8.2 convolution_convert_fusion.3
  261.2 48.5 %scatter_rows.3 = f32[256,2304]{1,0:T(8,128)} custom-call(bf16[4,1,256,2304]{3,2,1,0:T(8,128)(2,1)} %bitcast.103), custom_call_target="tpu_custom_call" | custom-call | flops 49999998976 | tf_op jit(solution)/shard_map/scatter_rows/pallas_call | solution.py:442
  309.7 2.8 multiply_reduce_fusion.2
  317.0 44.6 %gather_rows.2 = bf16[4,2,256,2304]{3,2,1,0:T(8,128)(2,1)} custom-call(bf16[256,2304]{1,0:T(8,128)(2,1)} %multiply_convert_fusion.4.block), custom_call_target="tpu_custom_call" | custom-call | flops 44999999488 | tf_op jit(solution)/shard_map/gather_rows/pallas_call | solution.py:136
  362.5 3.8 maximum_select_fusion.3
  366.2 2.7 maximum_select_fusion.2
  370.4 19.9 %fusion.51 = f32[2048,1440]{0,1:T(8,128)S(1)} fusion(bf16[2048,2304]{1,0:T(8,128)(2,1)} %bitcast.90, bf16[2304,1440]{1,0:T(8,128)(2,1)S(1)} %bitcast.74), kind=kOutput, calls=%fused_computation.131 | convolution fusion | flops 13589544960 | bytes 27869184 | tf_op jit(solution)/shard_map/dot_general | solution.py:27
  390.3 1.9 multiply_convert_fusion.2
  392.2 3.6 copy-done.5
  397.3 12.1 convolution_convert_fusion.1
  409.5 11.6 all-gather.3.cloned.1.call-done
  421.1 15.6 %multiply_convert_fusion.1 = (bf16[2048,720]{0,1:T(8,128)(2,1)S(1)}, bf16[2048,720]{0,1:T(8,128)(2,1)S(1)}) fusion(f32[2048,1440]{0,1:T(8,128)} %copy-done.5, bf16[2048,2304]{1,0:T(8,128)(2,1)} %all-gather.3.cloned.1.call-done, bf16[1440,2304]{1,0:T(8,128)(2,1)} %param.23, s32[]{:T(128)S(6)} %select_n.144), kind=kOutput, calls=%fused_computation.10 | convolution fusion | flops 6813941760 | bytes 30449668 | tf_op jit(solution)/shard_map/dot_general | solution.py:35
  436.7 3.5 pad_maximum_fusion
  440.4 10.7 convolution_convert_fusion.10
  451.1 11.5 convolution_convert_fusion.8
  462.7 12.5 convolution_convert_fusion.4
  475.2 20.1 %convolution_convert_fusion = bf16[2048,2304]{1,0:T(8,128)(2,1)} fusion(bf16[2304,1440]{1,0:T(8,128)(2,1)} %bitcast.75, bf16[2048,720]{0,1:T(8,128)(2,1)} %copy-done.17, bf16[2048,720]{0,1:T(8,128)(2,1)S(1)} %get-tuple-element.125), kind=kOutput, calls=%fused_computation | convolution fusion | flops 13606060032 | bytes 21970944 | tf_op jit(solution)/shard_map/dot_general | solution.py:35
  495.3 8.8 convolution_convert_fusion.9
  504.2 2.6 pad_maximum_fusion.2
  506.8 8.8 convolution_convert_fusion.7
  515.7 2.6 pad_maximum_fusion.3
  518.5 50.4 %scatter_rows.4 = f32[256,2304]{1,0:T(8,128)} custom-call(bf16[4,2,256,2304]{3,2,1,0:T(8,128)(2,1)} %bitcast.95), custom_call_target="tpu_custom_call" | custom-call | flops 49999998976 | tf_op jit(solution)/shard_map/scatter_rows/pallas_call | solution.py:442
  568.9 2.5 multiply_reduce_fusion
  573.4 42.5 %gather_rows.3 = bf16[4,1,256,2304]{3,2,1,0:T(8,128)(2,1)} custom-call(bf16[256,2304]{1,0:T(8,128)(2,1)} %multiply_convert_fusion.3.block), custom_call_target="tpu_custom_call" | custom-call | flops 44999999488 | tf_op jit(solution)/shard_map/gather_rows/pallas_call | solution.py:136
  615.9 8.1 convolution_convert_fusion.13.g_ref
  624.7 5.7 convolution_convert_fusion.5
  632.2 2.7 collective-permute-done.6
  637.9 69.5 %attend_backward.1 = (bf16[1024,576]{1,0:T(8,128)(2,1)}, bf16[1024,576]{1,0:T(8,128)(2,1)}, bf16[1024,576]{1,0:T(8,128)(2,1)}, f32[256,2304]{1,0:T(8,128)}) custom-call(bf16[1024,576]{1,0:T(8,128)(2,1)} %get-tuple-element.74.q_ref, bf16[2048,576]{1,0:T(8,128)(2,1)} %get-tuple-element.75.k_ref, bf16[2048,576]{1,0:T(8,128)(2,1)} %convolution_convert_fusion.6.v_ref, ...), custom_call_target="tpu_custom_call" | custom-call | flops 57000001536 | tf_op jit(solution)/shard_map/attend_backward/pallas_call | solution.py:1205
  707.4 7.0 concatenate.87
  714.4 14.5 %convolution_convert_fusion.2 = bf16[1024,2304]{1,0:T(8,128)(2,1)} fusion(bf16[1024,1728]{1,0:T(8,128)(2,1)} %concatenate.87, bf16[2304,1728]{1,0:T(8,128)(2,1)} %bitcast.99), kind=kOutput, calls=%fused_computation.14 | convolution fusion | flops 8156086272 | bytes 16220160 | tf_op jit(solution)/shard_map/dot_general | solution.py:35
  728.9 5.9 copy.43
  735.2 45.3 %scatter_rows.5 = f32[256,2304]{1,0:T(8,128)} custom-call(bf16[4,1,256,2304]{3,2,1,0:T(8,128)(2,1)} %bitcast.102), custom_call_target="tpu_custom_call" | custom-call | flops 49999998976 | tf_op jit(solution)/shard_map/scatter_rows/pallas_call | solution.py:442
  780.6 2.5 fusion.23
  783.9 4.4 fusion.27
  788.3 5.8 copy.52
  794.1 7.4 maximum_select_fusion
  801.5 6.9 convolution_convert_fusion.11
  808.4 6.9 convolution_convert_fusion.12
  816.7 2.9 pad_maximum_fusion.1.grads
  819.6 7.1 reduce-scatter.8.cloned.1.call-done.down_part
  826.7 289.7 %reduce_grads.1 = (bf16[48,16,3584]{2,1,0:T(8,128)(2,1)}, bf16[144,16,1792]{2,1,0:T(8,128)(2,1)}, bf16[24,16,3584]{2,1,0:T(8,128)(2,1)}, f32[8,2304]{1,0:T(8,128...) custom-call(bf16[4,12,16,3584]{3,2,1,0:T(8,128)(2,1)} %pad_maximum_f, ...), custom_call_target="tpu_custom_call" | custom-call | flops 299999985664 | tf_op jit(solution)/shard_map/reduce_grads/pallas_call | solution.py:836
  1116.5 3.7 collective-permute-start.7
  1120.2 3.9 collective-permute-start.8
  1125.6 2.5 collective-permute-start.9
  1128.1 1.9 fusion.47
  1132.2 15.4 %maximum_convert_fusion = f32[576,2304]{1,0:T(8,128)} fusion(bf16[192,1152]{1,0:T(8,128)(2,1)S(1)} %get-tuple-element.151, bf16[192,1152]{1,0:T(8,128)(2,1)S(1)} %get-tuple-element.152, bf16[192,1152]{1,0:T(8,128)(2,1)S(1)} %get-tuple-element.150, bf16[192,1152]{1,0:T(8,128)(2,1)S(1)} %get-tuple-element.146, bf16[192,1152]{1,0:T(8,128)(2,1)S(1)} %get-tuple-element.147, ...), kind=kLoop, calls=%fused_computation.52 | loop fusion | flops 15925248 | bytes 7962624 | tf_op jit(solution)/shard_map/convert_element_type | solution.py:1482
  1147.7 12.8 %place_down.1 = f32[1440,2304]{1,0:T(8,128)} custom-call(s32[3]{0:T(128)} %pad_add_fusion.flags, bf16[768,2304]{1,0:T(8,128)(2,1)} %bitcast.104, bf16[768,2304]{1,0:T(8,128)(2,1)} %bitcast.105), custom_call_target="tpu_custom_call" | custom-call | flops 8000000000 | tf_op jit(solution)/shard_map/place_down/pallas_call | solution.py:962
  1160.5 39.1 %collective-permute-done.7 = bf16[256,2304]{1,0:T(8,128)(2,1)S(1)} collective-permute-done((bf16[256,2304]{1,0:T(8,128)(2,1)S(1)}, bf16[256,2304]{1,0:T(8,128)(2,1)S(1)}, u32[]{:S(2)}, u32[]{:S(2)}) %collective-permute-start.7) | collective-permute-done | bytes 1179680 | tf_op jit(solution)/shard_map/ppermute | solution.py:1269
  1199.5 24.7 %collective-permute-done.8 = bf16[256,2304]{1,0:T(8,128)(2,1)} collective-permute-done((bf16[256,2304]{1,0:T(8,128)(2,1)S(1)}, bf16[256,2304]{1,0:T(8,128)(2,1)}, u32[]{:S(2)}, u32[]{:S(2)}) %collective-permute-start.8) | collective-permute-done | bytes 1179680 | tf_op jit(solution)/shard_map/ppermute | solution.py:1269
  1224.2 24.5 %place_rows.1 = (f32[576,2304]{1,0:T(8,128)}, f32[576,2304]{1,0:T(8,128)}, f32[576,2304]{1,0:T(8,128)}, f32[576,5760]{1,0:T(8,128)}, f32[576,5760]{1,0:T(8,128)}) custom-call(s32[3]{0:T(128)} %pad_add_fusion.flags, bf16[48,16,3584]{2,1,0:T(8,128)(2,1)} %get-tuple-element.102.mine, bf16[576,2880]{1,0:T(8,128)(2,1)} %all-gather.5.cloned.1.call-done.near, ...), custom_call_target="tpu_custom_call" | custom-call | flops 24999999488 | tf_op jit(solution)/shard_map/place_rows/pallas_call | solution.py:940
  1249.8 2.4 copy.60
  (132 shorter events, 34.9 us)
Async XLA Ops:
  7.2 413.9 %all-gather.3.cloned.1.call-start = ((), (), s32[]{:S(2)}) async-start(), calls=%async_computation.3 | async-start | bytes 10616832 | tf_op jit(solution)/shard_map/all_gather | solution.py:1360
  10.9 3.4 copy-start.22
  163.6 153.4 %collective-permute-start.1 = (bf16[576,1440]{1,0:T(8,128)(2,1)}, bf16[576,1440]{1,0:T(8,128)(2,1)}, u32[]{:S(2)}, u32[]{:S(2)}) collective-permute-start(bf16[576,1440]{1,0:T(8,128)(2,1)} %pad_maximum_fusion.4), channel_id=1, source_target_pairs={{0,4},{4,0},{1,5},{5,1},{2,6},{6,2},{3,7},{7,3},{8,12},{12,8},{9,1... | collective-permute-start | bytes 4976648 | tf_op jit(solution)/shard_map/ppermute | solution.py:39
  163.7 5.2 copy-start.33
  165.4 151.6 %collective-permute-start.2 = (bf16[576,1440]{1,0:T(8,128)(2,1)}, bf16[576,1440]{1,0:T(8,128)(2,1)}, u32[]{:S(2)}, u32[]{:S(2)}) collective-permute-start(bf16[576,1440]{1,0:T(8,128)(2,1)} %pad_maximum_fusion.5), channel_id=1, source_target_pairs={{0,8},{8,0},{1,9},{9,1},{2,10},{10,2},{3,11},{11,3},{4,12},{12,4},... | collective-permute-start | bytes 4976648 | tf_op jit(solution)/shard_map/ppermute | solution.py:39
  167.2 149.8 %collective-permute-start.3 = (bf16[576,1440]{1,0:T(8,128)(2,1)}, bf16[576,1440]{1,0:T(8,128)(2,1)}, u32[]{:S(2)}, u32[]{:S(2)}) collective-permute-start(bf16[576,1440]{1,0:T(8,128)(2,1)} %pad_maximum_fusion.6), channel_id=1, source_target_pairs={{0,12},{4,8},{8,4},{12,0},{1,13},{5,9},{9,5},{13,1},{2,14},{6,10},... | collective-permute-start | bytes 4976648 | tf_op jit(solution)/shard_map/ppermute | solution.py:1325
  168.9 146.7 %collective-permute-start = (bf16[256,2304]{1,0:T(8,128)(2,1)S(1)}, bf16[256,2304]{1,0:T(8,128)(2,1)S(1)}, u32[]{:S(2)}, u32[]{:S(2)}) collective-permute-start(bf16[256,2304]{1,0:T(8,128)(2,1)S(1)} %bitcast.88), channel_id=1, source_target_pairs={{0,0},{1,4},{2,8},{3,12},{4,1},{5,5},{6,9},{7,13},{8,2},{9,6},{10,... | collective-permute-start | bytes 3538952 | tf_op jit(solution)/shard_map/ppermute | solution.py:1269
  261.2 48.5 %copy-start.6 = (bf16[256,2304]{1,0:T(8,128)(2,1)S(1)}, bf16[256,2304]{1,0:T(8,128)(2,1)}, u32[]{:S(2)}) copy-start(bf16[256,2304]{1,0:T(8,128)(2,1)} %get-tuple-element.63) | copy-start | bytes 3538948
  312.5 1.7 copy-start
  312.5 3.0 copy-start.27
  314.3 1.3 copy-start.23
  315.6 46.1 %copy-start.8 = (bf16[256,2304]{1,0:T(8,128)(2,1)}, bf16[256,2304]{1,0:T(8,128)(2,1)S(1)}, u32[]{:S(2)}) copy-start(bf16[256,2304]{1,0:T(8,128)(2,1)S(1)} %collective-permute-done) | copy-start | bytes 3538948
  317.0 45.0 %copy-start.13 = (bf16[576,720]{1,0:T(8,128)(2,1)S(1)}, bf16[576,720]{1,0:T(8,128)(2,1)}, u32[]{:S(2)}) copy-start(bf16[576,720]{1,0:T(8,128)(2,1)} %get-tuple-element.131) | copy-start | bytes 2488324
  317.0 45.0 %copy-start.14 = (bf16[576,720]{1,0:T(8,128)(2,1)S(1)}, bf16[576,720]{1,0:T(8,128)(2,1)}, u32[]{:S(2)}) copy-start(bf16[576,720]{1,0:T(8,128)(2,1)} %get-tuple-element.127) | copy-start | bytes 2488324
  361.7 262.3 %reduce-scatter.4.cloned.1.call-start = ((), (), s32[]{:S(2)}) async-start(), calls=%async_computation.4 | async-start | bytes 4239360 | tf_op jit(solution)/shard_map/reduce_scatter | solution.py:1399
  370.4 19.9 %copy-start.11 = (bf16[2,2,576,1440]{3,2,1,0:T(8,128)(2,1)}, bf16[2,2,576,1440]{3,2,1,0:T(8,128)(2,1)S(1)}, u32[]{:S(2)}) copy-start(bf16[2,2,576,1440]{3,2,1,0:T(8,128)(2,1)S(1)} %maximum_select_fusion.1) | copy-start | bytes 19906564
  390.3 5.5 copy-start.5
  395.7 1.6 copy-start.15
  436.7 14.4 %copy-start.17 = (bf16[2048,720]{0,1:T(8,128)(2,1)}, bf16[2048,720]{0,1:T(8,128)(2,1)S(1)}, u32[]{:S(2)}) copy-start(bf16[2048,720]{0,1:T(8,128)(2,1)S(1)} %get-tuple-element.126) | copy-start | bytes 8847364
  440.2 55.1 %collective-permute-start.4 = (bf16[2048,1440]{0,1:T(8,128)(2,1)}, bf16[2048,1440]{0,1:T(8,128)(2,1)}, u32[]{:S(2)}, u32[]{:S(2)}) collective-permute-start(bf16[2048,1440]{0,1:T(8,128)(2,1)} %pad_maximum_fusion), channel_id=1, source_target_pairs={{0,4},{4,0},{1,5},{5,1},{2,6},{6,2},{3,7},{7,3},{8,12},{12,8},{9,1... | collective-permute-start | bytes 17694728 | tf_op jit(solution)/shard_map/ppermute | solution.py:39
  451.1 11.5 copy-start.16
  495.3 8.9 copy-start.19
  506.8 8.9 copy-start.18
  518.4 301.2 %all-gather.5.cloned.1.call-start = ((), (), s32[]{:S(2)}) async-start(), calls=%async_computation.5 | async-start | bytes 4239360 | tf_op jit(solution)/shard_map/all_gather | solution.py:1416
  518.4 50.4 %copy-start.1 = (f32[256,2304]{1,0:T(8,128)S(1)}, f32[256,2304]{1,0:T(8,128)}, u32[]{:S(2)}) copy-start(f32[256,2304]{1,0:T(8,128)} %copy-done) | copy-start | bytes 7077892
  518.4 50.4 %copy-start.24 = (f32[2304]{0:T(1024)S(1)}, f32[2304]{0:T(1024)}, u32[]{:S(2)}) copy-start(f32[2304]{0:T(1024)} %copy-done.23) | copy-start | bytes 27652
  518.4 50.4 %copy-start.28 = (f32[256]{0:T(256)S(1)}, f32[256]{0:T(256)}, u32[]{:S(2)}) copy-start(f32[256]{0:T(256)} %copy-done.27) | copy-start | bytes 3076
  568.9 2.5 copy-start.3
  568.9 2.7 copy-start.9
  571.6 1.8 copy-start.30
  624.0 195.5 %reduce-scatter.6.cloned.1.call-start = ((), (), s32[]{:S(2)}) async-start(), calls=%async_computation.6 | async-start | bytes 4239360 | tf_op jit(solution)/shard_map/reduce_scatter | solution.py:1399
  624.6 202.1 %reduce-scatter.8.cloned.1.call-start = ((), (), s32[]{:S(2)}) async-start(), calls=%async_computation.7 | async-start | bytes 4423680 | tf_op jit(solution)/shard_map/reduce_scatter | solution.py:1399
  624.7 7.5 copy-start.32
  631.5 3.4 collective-permute-start.6
  734.8 53.5 %collective-permute-start.5 = (bf16[1024,1728]{0,1:T(8,128)(2,1)}, bf16[1024,1728]{0,1:T(8,128)(2,1)}, u32[]{:S(2)}, u32[]{:S(2)}) collective-permute-start(bf16[1024,1728]{0,1:T(8,128)(2,1)} %copy.43), channel_id=1, source_target_pairs={{0,4},{4,0},{1,5},{5,1},{2,6},{6,2},{3,7},{7,3},{8,12},{12,8},{9,1... | collective-permute-start | bytes 10616840 | tf_op jit(solution)/shard_map/ppermute | solution.py:39
  735.2 45.4 %copy-start.7 = (bf16[256,2304]{1,0:T(8,128)(2,1)S(1)}, bf16[256,2304]{1,0:T(8,128)(2,1)}, u32[]{:S(2)}) copy-start(bf16[256,2304]{1,0:T(8,128)(2,1)} %get-tuple-element.63) | copy-start | bytes 3538948
  735.2 45.4 %copy-start.26 = (f32[2304]{0:T(1024)S(1)}, f32[2304]{0:T(1024)}, u32[]{:S(2)}) copy-start(f32[2304]{0:T(1024)} %get-tuple-element.121) | copy-start | bytes 27652
  735.2 48.6 %copy-start.4 = (f32[256,2304]{1,0:T(8,128)S(1)}, f32[256,2304]{1,0:T(8,128)}, u32[]{:S(2)}) copy-start(f32[256,2304]{1,0:T(8,128)} %scatter_rows.4) | copy-start | bytes 7077892
  780.5 3.3 copy-start.2
  780.6 3.3 copy-start.10
  780.6 3.3 copy-start.25
  780.6 3.3 copy-start.29
  780.6 3.3 copy-start.31
  815.3 1.3 copy-start.12
  826.7 289.8 %copy-start.21 = (bf16[256,2304]{1,0:T(8,128)(2,1)S(1)}, bf16[256,2304]{1,0:T(8,128)(2,1)}, u32[]{:S(2)}) copy-start(bf16[256,2304]{1,0:T(8,128)(2,1)} %get-tuple-element.100) | copy-start | bytes 3538948
  826.7 293.5 %copy-start.20 = (bf16[256,2304]{1,0:T(8,128)(2,1)S(1)}, bf16[256,2304]{1,0:T(8,128)(2,1)}, u32[]{:S(2)}) copy-start(bf16[256,2304]{1,0:T(8,128)(2,1)} %get-tuple-element.101) | copy-start | bytes 3538948
  1116.5 83.1 %collective-permute-start.7 = (bf16[256,2304]{1,0:T(8,128)(2,1)S(1)}, bf16[256,2304]{1,0:T(8,128)(2,1)S(1)}, u32[]{:S(2)}, u32[]{:S(2)}) collective-permute-start(bf16[256,2304]{1,0:T(8,128)(2,1)S(1)} %copy-done.21), channel_id=1, source_target_pairs={{0,0},{1,4},{2,8},{3,12},{4,1},{5,5},{6,9},{7,13},{8,2},{9,6},{10,... | collective-permute-start | bytes 3538952 | tf_op jit(solution)/shard_map/ppermute | solution.py:1269
  1120.2 104.0 %collective-permute-start.8 = (bf16[256,2304]{1,0:T(8,128)(2,1)S(1)}, bf16[256,2304]{1,0:T(8,128)(2,1)}, u32[]{:S(2)}, u32[]{:S(2)}) collective-permute-start(bf16[256,2304]{1,0:T(8,128)(2,1)S(1)} %copy-done.20), channel_id=1, source_target_pairs={{0,0},{1,4},{2,8},{3,12},{4,1},{5,5},{6,9},{7,13},{8,2},{9,6},{10,... | collective-permute-start | bytes 3538952 | tf_op jit(solution)/shard_map/ppermute | solution.py:1269
  1125.6 98.5 %collective-permute-start.9 = (bf16[576,2880]{1,0:T(8,128)(2,1)}, bf16[576,2880]{1,0:T(8,128)(2,1)}, u32[]{:S(2)}, u32[]{:S(2)}) collective-permute-start(bf16[576,2880]{1,0:T(8,128)(2,1)} %all-gather.5.cloned.1.call-done.near), channel_id=1, source_target_pairs={{0,16},{16,0},{1,17},{17,1},{2,18},{18,2},{3,19},{19,3},{4,20},{20... | collective-permute-start | bytes 9953288 | tf_op jit(solution)/shard_map/ppermute | solution.py:39
Sparse Core Ops, SparseCore 0:
  361.8 59.2 all-gather.2
  518.5 64.6 reduce-scatter.3
  624.1 67.5 all-gather.4
  694.5 62.8 reduce-scatter.5
  760.1 66.5 reduce-scatter.7

commit v6 on v5

--- a/solution.py
+++ b/solution.py
@@ -881,9 +881,9 @@
     )(grads, gain, far, down)
 
 
-def rows_kernel(cols_f, cols_h, flags, mine, near, far, near_x, far_x, *refs):
+def qkv_kernel(cols_h, flags, mine, *refs):
     sources, outs = refs[:4], refs[4:]
-    here_x, here_y, core = flags[0], flags[1], flags[2]
+    here_x, here_y = flags[0], flags[1]
     rows, cols = outs[0].shape[0], mine.shape[-1]
     own = mine[...].reshape(rows, cols)
     full = [
@@ -900,6 +900,10 @@
         outs[kind][...] = jnp.concatenate(
             [full[i][j][:, first : first + cols_h] for j in range(2) for i in range(2)], 1
         ).astype(F32)
+
+
+def ff_kernel(cols_f, flags, near, far, near_x, far_x, *outs):
+    here_x, here_y, core = flags[0], flags[1], flags[2]
     by_x = [(near[...], far[...]), (near_x[...], far_x[...])]
     full = [
         [
@@ -921,33 +925,45 @@
                     first = (2 + kind) * cols_f
                     side = full[i][j][:, first : first + cols_f]
                     pieces.append(jnp.where(core == k, own, side))
-        outs[3 + kind][...] = jnp.concatenate(pieces, 1).astype(F32)
-
-
-def place_rows(flags, mine, summed, near, far, near_x, far_x, rows_d, cols_f, cols_h):
+        outs[kind][...] = jnp.concatenate(pieces, 1).astype(F32)
+
+
+def row_target(width):
+    return pl.BlockSpec((48, width), lambda s: (s, 0))
+
+
+def place_qkv(flags, mine, summed, rows_d, cols_h):
     cols = summed.shape[-1]
-    shape = jax.ShapeDtypeStruct
 
     def source(i, j):
         return pl.BlockSpec((PARTS, UNIT, cols), lambda s: ((2 * i + j) * 12 + s, 0, 0))
 
-    def target(width):
-        return pl.BlockSpec((48, width), lambda s: (s, 0))
-
     own = pl.BlockSpec((PARTS, UNIT, cols), lambda s: (s + s // 3, 0, 0))
-    ff = pl.BlockSpec((48, 4 * cols_f), lambda s: (s, 0))
-    widths = (4 * cols_h,) * 3 + (8 * cols_f,) * 2
     return pl.pallas_call(
-        partial(rows_kernel, cols_f, cols_h),
+        partial(qkv_kernel, cols_h),
         grid=(rows_d // 48,),
-        out_shape=tuple(shape((rows_d, width), F32) for width in widths),
-        in_specs=[pl.BlockSpec(memory_space=pltpu.SMEM), own] + [ff] * 4
+        out_shape=(jax.ShapeDtypeStruct((rows_d, 4 * cols_h), F32),) * 3,
+        in_specs=[pl.BlockSpec(memory_space=pltpu.SMEM), own]
         + [source(i, j) for i in range(2) for j in range(2)],
-        out_specs=tuple(target(width) for width in widths),
+        out_specs=(row_target(4 * cols_h),) * 3,
         compiler_params=pltpu.CompilerParams(vmem_limit_bytes=VMEM_LIMIT),
-        cost_estimate=cost(25),
-        name="place_rows",
-    )(flags, mine, near, far, near_x, far_x, summed, summed, summed, summed)
+        cost_estimate=cost(9),
+        name="place_qkv",
+    )(flags, mine, summed, summed, summed, summed)
+
+
+def place_ff(flags, near, far, near_x, far_x, rows_d, cols_f):
+    ff = row_target(4 * cols_f)
+    return pl.pallas_call(
+        partial(ff_kernel, cols_f),
+        grid=(rows_d // 48,),
+        out_shape=(jax.ShapeDtypeStruct((rows_d, 8 * cols_f), F32),) * 2,
+        in_specs=[pl.BlockSpec(memory_space=pltpu.SMEM)] + [ff] * 4,
+        out_specs=(row_target(8 * cols_f),) * 2,
+        compiler_params=pltpu.CompilerParams(vmem_limit_bytes=VMEM_LIMIT),
+        cost_estimate=cost(16),
+        name="place_ff",
+    )(flags, near, far, near_x, far_x)
 
 
 def down_kernel(per_x, flags, own, side, out):
@@ -1482,10 +1498,8 @@
         return grad.astype(F32)
 
     flags = jnp.stack([x, y, c]).astype(jnp.int32)
-    *qkv_all, gate_all, up_all = place_rows(
-        flags, mine, summed, ff_near, far_y, near_x, far_x,
-        rows_d, cols_f, cols_h,
-    )
+    qkv_all = place_qkv(flags, mine, summed, rows_d, cols_h)
+    gate_all, up_all = place_ff(flags, ff_near, far_y, near_x, far_x, rows_d, cols_f)
     ff_all = (gate_all, up_all)
     down_all = place_down(flags, down_own, down_side, cols_f)
     out_mine = mine.reshape(4, UNITS, UNIT, 2 * width)[:, OUT_AT:, :, : 3 * half]

time: 1270 us -> 1260 us (level)
  waiting for transfers between devices: 85.8 us -> 72.5 us
    ppermute x3, waiting for transfers between devices: 63.7 us -> 50.4 us  [turned(): return lax.ppermute(block, ('y', 'c', 'z'), turn_pairs)]
    pallas_call x1 -> x2, Pallas kernels: 24.5 us -> 31.6 us  [the longest x1 18.1 us: place_ff(): pl.pallas_call(partial(ff_kernel, cols_f), grid=(rows_d // 48,), out_shap...]
  transfers between devices with their start and end apart: 15 -> 15, of which waited for: 5 -> 5; matrix products, arithmetic and copies ran while one was open for 21% -> 21% of each run, Pallas kernels for 25% -> 26%
where the time goes in v6:
time: 1260 us; the launch traced here: 1250 us
  Pallas kernels  804 us (64%)
  matrix products  202 us (16%)
  waiting for transfers between devices  72.5 us (6%)
  other arithmetic  71.9 us (6%)
  local copies, waits for them, and re-layouts  69.7 us (6%)
  starting transfers between devices  18.8 us (1%)
  between operations  14.9 us (1%)
    pallas_call x1, Pallas kernels, reduce_grads(): pl.pallas_call(reduce_kernel, out_shape=(shape((4 * UNITS, UNIT, cols), B...  290 us
    pallas_call x3, Pallas kernels, scatter_rows(): pl.pallas_call(partial(scatter_kernel, cores), out_shape=jax.ShapeDtypeSt...  144 us
    pallas_call x1, Pallas kernels, front(): pl.pallas_call(partial(front_kernel, docs), out_shape=(shape((4, 2, rows,...  126 us
    pallas_call x2, Pallas kernels, gather_rows(): pl.pallas_call(partial(gather_kernel, cores), out_shape=jax.ShapeDtypeStr...  87.1 us
    dot_general x6, matrix products, dot(): return jnp.dot(left, right, preferred_element_type=F32)  72.1 us
    dot_general x8, matrix products, dot_tn(): lax.dot_general(left, right, (((0,), (0,)), ((), ())), preferred_element_...  72 us
    pallas_call x1, Pallas kernels, attend_backward(): pl.pallas_call(partial(backward_kernel, spans, width), grid=(steps + 1,),...  69.5 us
    dot_general x4, matrix products, dot_nt(): lax.dot_general(left, right, (((1,), (1,)), ((), ())), preferred_element_...  58.3 us
  transfers between devices with their start and end apart: 15, of which 5 were waited for; matrix products, arithmetic and copies ran while one was open for 21% of the time, Pallas kernels for 26%

profile of v6, /device:TPU:4, one launch (start us, length us, event | category | flops | bytes accessed | tf_op | source)
XLA Modules:
  0.0 1254.2 jit_solution(16613525079514603414)
XLA Ops:
  10.9 3.4 constant_dynamic-slice_fusion.13
  14.3 3.0 constant_dynamic-slice_fusion.11
  17.3 4.3 concatenate.78.near
  21.6 4.3 concatenate.79.far
  25.9 125.9 %front.1 = (bf16[4,2,256,2304]{3,2,1,0:T(8,128)(2,1)}, bf16[256,2304]{1,0:T(8,128)(2,1)}, f32[8,2304]{1,0:T(8,128)}, bf16[2,2,576,1728]{3,2,1,0:T(8,128)(2,1)}, ...) custom-call(bf16[256,2304]{1,0:T(8,128)(2,1)} %bitcast.86, ...), custom_call_target="tpu_custom_call" | custom-call | flops 109999996928 | tf_op jit(solution)/shard_map/front/pallas_call | solution.py:301
  151.8 5.0 constant_dynamic-slice_fusion.2
  156.8 5.0 constant_dynamic-slice_fusion.3
  168.9 5.7 collective-permute-start
  174.5 12.8 %fusion.9.k_raw = f32[2048,576]{1,0:T(8,128)} fusion(bf16[2048,2304]{1,0:T(8,128)(2,1)} %bitcast.79, bf16[2304,1728]{1,0:T(8,128)(2,1)} %bitcast.95), kind=kOutput, calls=%fused_computation.39 | convolution fusion | flops 5435817984 | bytes 17104896 | tf_op jit(solution)/shard_map/dot_general | solution.py:27
  187.4 12.0 convolution_convert_fusion.6.v_ref
  199.3 2.6 constant_dynamic-slice_fusion.10
  202.0 7.2 fusion.11.q_raw
  210.2 42.8 %attend_forward.1 = (bf16[1024,576]{1,0:T(8,128)(2,1)}, bf16[2048,576]{1,0:T(8,128)(2,1)}, bf16[1024,576]{1,0:T(8,128)(2,1)}, f32[1024,576]{1,0:T(8,128)}) custom-call(f32[1024,576]{1,0:T(8,128)} %fusion.11.q_raw, f32[2048,576]{1,0:T(8,128)} %fusion.9.k_raw, bf16[2048,576]{1,0:T(8,128)(2,1)} %convolution_convert_fusion.6.v_ref, ...), custom_call_target="tpu_custom_call" | custom-call | flops 43000000512 | tf_op jit(solution)/shard_map/attend_forward/pallas_call | solution.py:1065
  253.0 8.2 convolution_convert_fusion.3
  261.2 48.5 %scatter_rows.3 = f32[256,2304]{1,0:T(8,128)} custom-call(bf16[4,1,256,2304]{3,2,1,0:T(8,128)(2,1)} %bitcast.102), custom_call_target="tpu_custom_call" | custom-call | flops 49999998976 | tf_op jit(solution)/shard_map/scatter_rows/pallas_call | solution.py:442
  309.7 2.8 multiply_reduce_fusion.2
  317.0 44.6 %gather_rows.2 = bf16[4,2,256,2304]{3,2,1,0:T(8,128)(2,1)} custom-call(bf16[256,2304]{1,0:T(8,128)(2,1)} %multiply_convert_fusion.4.block), custom_call_target="tpu_custom_call" | custom-call | flops 44999999488 | tf_op jit(solution)/shard_map/gather_rows/pallas_call | solution.py:136
  362.5 3.8 maximum_select_fusion.3
  366.2 2.7 maximum_select_fusion.2
  370.4 19.9 %fusion.51 = f32[2048,1440]{0,1:T(8,128)S(1)} fusion(bf16[2048,2304]{1,0:T(8,128)(2,1)} %bitcast.89, bf16[2304,1440]{1,0:T(8,128)(2,1)S(1)} %bitcast.75), kind=kOutput, calls=%fused_computation.131 | convolution fusion | flops 13589544960 | bytes 27869184 | tf_op jit(solution)/shard_map/dot_general | solution.py:27
  392.2 3.6 copy-done.5
  397.3 12.1 convolution_convert_fusion.1
  409.5 11.6 all-gather.3.cloned.1.call-done
  421.1 15.6 %multiply_convert_fusion.1 = (bf16[2048,720]{0,1:T(8,128)(2,1)S(1)}, bf16[2048,720]{0,1:T(8,128)(2,1)S(1)}) fusion(f32[2048,1440]{0,1:T(8,128)} %copy-done.5, bf16[2048,2304]{1,0:T(8,128)(2,1)} %all-gather.3.cloned.1.call-done, bf16[1440,2304]{1,0:T(8,128)(2,1)} %param.23, s32[]{:T(128)S(6)} %select_n.144), kind=kOutput, calls=%fused_computation.10 | convolution fusion | flops 6813941760 | bytes 30449668 | tf_op jit(solution)/shard_map/dot_general | solution.py:35
  436.7 3.5 pad_maximum_fusion
  440.4 10.7 convolution_convert_fusion.10
  451.1 11.5 convolution_convert_fusion.8
  462.7 12.5 convolution_convert_fusion.4
  475.2 20.1 %convolution_convert_fusion = bf16[2048,2304]{1,0:T(8,128)(2,1)} fusion(bf16[2304,1440]{1,0:T(8,128)(2,1)} %bitcast.76, bf16[2048,720]{0,1:T(8,128)(2,1)} %copy-done.17, bf16[2048,720]{0,1:T(8,128)(2,1)S(1)} %get-tuple-element.125), kind=kOutput, calls=%fused_computation | convolution fusion | flops 13606060032 | bytes 21970944 | tf_op jit(solution)/shard_map/dot_general | solution.py:35
  495.3 8.8 convolution_convert_fusion.9
  504.2 2.6 pad_maximum_fusion.2
  506.8 8.8 convolution_convert_fusion.7
  515.7 2.6 pad_maximum_fusion.3
  518.5 50.4 %scatter_rows.4 = f32[256,2304]{1,0:T(8,128)} custom-call(bf16[4,2,256,2304]{3,2,1,0:T(8,128)(2,1)} %bitcast.94), custom_call_target="tpu_custom_call" | custom-call | flops 49999998976 | tf_op jit(solution)/shard_map/scatter_rows/pallas_call | solution.py:442
  568.9 2.5 multiply_reduce_fusion
  573.4 42.5 %gather_rows.3 = bf16[4,1,256,2304]{3,2,1,0:T(8,128)(2,1)} custom-call(bf16[256,2304]{1,0:T(8,128)(2,1)} %multiply_convert_fusion.3.block), custom_call_target="tpu_custom_call" | custom-call | flops 44999999488 | tf_op jit(solution)/shard_map/gather_rows/pallas_call | solution.py:136
  615.9 8.1 convolution_convert_fusion.13.g_ref
  624.7 5.7 convolution_convert_fusion.5
  632.2 2.7 collective-permute-done.6
  637.9 69.5 %attend_backward.1 = (bf16[1024,576]{1,0:T(8,128)(2,1)}, bf16[1024,576]{1,0:T(8,128)(2,1)}, bf16[1024,576]{1,0:T(8,128)(2,1)}, f32[256,2304]{1,0:T(8,128)}) custom-call(bf16[1024,576]{1,0:T(8,128)(2,1)} %get-tuple-element.74.q_ref, bf16[2048,576]{1,0:T(8,128)(2,1)} %get-tuple-element.75.k_ref, bf16[2048,576]{1,0:T(8,128)(2,1)} %convolution_convert_fusion.6.v_ref, ...), custom_call_target="tpu_custom_call" | custom-call | flops 57000001536 | tf_op jit(solution)/shard_map/attend_backward/pallas_call | solution.py:1221
  707.4 7.0 concatenate.87
  714.4 14.5 %convolution_convert_fusion.2 = bf16[1024,2304]{1,0:T(8,128)(2,1)} fusion(bf16[1024,1728]{1,0:T(8,128)(2,1)} %concatenate.87, bf16[2304,1728]{1,0:T(8,128)(2,1)} %bitcast.98), kind=kOutput, calls=%fused_computation.14 | convolution fusion | flops 8156086272 | bytes 16220160 | tf_op jit(solution)/shard_map/dot_general | solution.py:35
  728.9 5.9 copy.43
  735.2 45.3 %scatter_rows.5 = f32[256,2304]{1,0:T(8,128)} custom-call(bf16[4,1,256,2304]{3,2,1,0:T(8,128)(2,1)} %bitcast.101), custom_call_target="tpu_custom_call" | custom-call | flops 49999998976 | tf_op jit(solution)/shard_map/scatter_rows/pallas_call | solution.py:442
  780.6 2.5 fusion.23
  783.9 4.4 fusion.27
  788.3 5.8 copy.52
  794.1 7.4 maximum_select_fusion
  801.5 6.9 convolution_convert_fusion.11
  808.4 6.9 convolution_convert_fusion.12
  816.7 2.9 pad_maximum_fusion.1.grads
  819.6 7.1 reduce-scatter.8.cloned.1.call-done.down_part
  826.7 289.7 %reduce_grads.1 = (bf16[48,16,3584]{2,1,0:T(8,128)(2,1)}, bf16[144,16,1792]{2,1,0:T(8,128)(2,1)}, bf16[24,16,3584]{2,1,0:T(8,128)(2,1)}, f32[8,2304]{1,0:T(8,128...) custom-call(bf16[4,12,16,3584]{3,2,1,0:T(8,128)(2,1)} %pad_maximum_f, ...), custom_call_target="tpu_custom_call" | custom-call | flops 299999985664 | tf_op jit(solution)/shard_map/reduce_grads/pallas_call | solution.py:836
  1116.4 3.7 collective-permute-start.7
  1120.2 3.9 collective-permute-start.8
  1127.4 2.5 collective-permute-start.9
  1132.2 13.1 %place_down.1 = f32[1440,2304]{1,0:T(8,128)} custom-call(s32[3]{0:T(128)} %pad_add_fusion.flags, bf16[768,2304]{1,0:T(8,128)(2,1)} %bitcast.103, bf16[768,2304]{1,0:T(8,128)(2,1)} %bitcast.104), custom_call_target="tpu_custom_call" | custom-call | flops 8000000000 | tf_op jit(solution)/shard_map/place_down/pallas_call | solution.py:978
  1145.3 15.1 %maximum_convert_fusion = f32[576,2304]{1,0:T(8,128)} fusion(bf16[192,1152]{1,0:T(8,128)(2,1)S(1)} %get-tuple-element.151, bf16[192,1152]{1,0:T(8,128)(2,1)S(1)} %get-tuple-element.152, bf16[192,1152]{1,0:T(8,128)(2,1)S(1)} %get-tuple-element.150, bf16[192,1152]{1,0:T(8,128)(2,1)S(1)} %get-tuple-element.146, bf16[192,1152]{1,0:T(8,128)(2,1)S(1)} %get-tuple-element.147, ...), kind=kLoop, calls=%fused_computation.52 | loop fusion | flops 15925248 | bytes 7962624 | tf_op jit(solution)/shard_map/convert_element_type | solution.py:1498
  1160.4 13.5 %place_qkv.1 = (f32[576,2304]{1,0:T(8,128)}, f32[576,2304]{1,0:T(8,128)}, f32[576,2304]{1,0:T(8,128)}) custom-call(s32[3]{0:T(128)} %pad_add_fusion.flags, bf16[48,16,3584]{2,1,0:T(8,128)(2,1)} %get-tuple-element.102.mine, bf16[144,16,1792]{2,1,0:T(8,128)(2,1)} %get-tuple-element.103.refs_0_.refs_1_.refs_2_.refs_3_, ...), custom_call_target="tpu_custom_call" | custom-call | flops 8999999488 | tf_op jit(solution)/shard_map/place_qkv/pallas_call | solution.py:942
  1173.9 25.9 %collective-permute-done.7 = bf16[256,2304]{1,0:T(8,128)(2,1)} collective-permute-done((bf16[256,2304]{1,0:T(8,128)(2,1)}, bf16[256,2304]{1,0:T(8,128)(2,1)}, u32[]{:S(2)}, u32[]{:S(2)}) %collective-permute-start.7) | collective-permute-done | bytes 1179680 | tf_op jit(solution)/shard_map/ppermute | solution.py:1285
  1199.8 24.5 %collective-permute-done.8 = bf16[256,2304]{1,0:T(8,128)(2,1)} collective-permute-done((bf16[256,2304]{1,0:T(8,128)(2,1)S(1)}, bf16[256,2304]{1,0:T(8,128)(2,1)}, u32[]{:S(2)}, u32[]{:S(2)}) %collective-permute-start.8) | collective-permute-done | bytes 1179680 | tf_op jit(solution)/shard_map/ppermute | solution.py:1285
  1224.3 18.1 %place_ff.1 = (f32[576,5760]{1,0:T(8,128)}, f32[576,5760]{1,0:T(8,128)}) custom-call(s32[3]{0:T(128)} %pad_add_fusion.flags, bf16[576,2880]{1,0:T(8,128)(2,1)} %all-gather.5.cloned.1.call-done.near, bf16[576,2880]{1,0:T(8,128)(2,1)} %bitcast.105, bf16[576,2880]{1,0:T(8,128)(2,1)} %collective-permute-done.9.near_x, bf16[576,2880]{1,0:T(8,128)(2,1)} %bitcast.106), custom_call_target="tpu_custom_call" | custom-call | flops 16000000000 | tf_op jit(solution)/shard_map/place_ff/pallas_call | solution.py:957
  1242.4 2.4 copy.59
  1244.8 2.4 copy.60
  (131 shorter events, 37.6 us)
Async XLA Ops:
  7.2 413.9 %all-gather.3.cloned.1.call-start = ((), (), s32[]{:S(2)}) async-start(), calls=%async_computation.3 | async-start | bytes 10616832 | tf_op jit(solution)/shard_map/all_gather | solution.py:1376
  10.9 3.4 copy-start.21
  163.6 153.4 %collective-permute-start.1 = (bf16[576,1440]{1,0:T(8,128)(2,1)}, bf16[576,1440]{1,0:T(8,128)(2,1)}, u32[]{:S(2)}, u32[]{:S(2)}) collective-permute-start(bf16[576,1440]{1,0:T(8,128)(2,1)} %pad_maximum_fusion.4), channel_id=1, source_target_pairs={{0,4},{4,0},{1,5},{5,1},{2,6},{6,2},{3,7},{7,3},{8,12},{12,8},{9,1... | collective-permute-start | bytes 4976648 | tf_op jit(solution)/shard_map/ppermute | solution.py:39
  163.7 5.2 copy-start.32
  165.4 151.6 %collective-permute-start.2 = (bf16[576,1440]{1,0:T(8,128)(2,1)}, bf16[576,1440]{1,0:T(8,128)(2,1)}, u32[]{:S(2)}, u32[]{:S(2)}) collective-permute-start(bf16[576,1440]{1,0:T(8,128)(2,1)} %pad_maximum_fusion.5), channel_id=1, source_target_pairs={{0,8},{8,0},{1,9},{9,1},{2,10},{10,2},{3,11},{11,3},{4,12},{12,4},... | collective-permute-start | bytes 4976648 | tf_op jit(solution)/shard_map/ppermute | solution.py:39
  167.2 149.8 %collective-permute-start.3 = (bf16[576,1440]{1,0:T(8,128)(2,1)}, bf16[576,1440]{1,0:T(8,128)(2,1)}, u32[]{:S(2)}, u32[]{:S(2)}) collective-permute-start(bf16[576,1440]{1,0:T(8,128)(2,1)} %pad_maximum_fusion.6), channel_id=1, source_target_pairs={{0,12},{4,8},{8,4},{12,0},{1,13},{5,9},{9,5},{13,1},{2,14},{6,10},... | collective-permute-start | bytes 4976648 | tf_op jit(solution)/shard_map/ppermute | solution.py:1341
  168.9 146.7 %collective-permute-start = (bf16[256,2304]{1,0:T(8,128)(2,1)S(1)}, bf16[256,2304]{1,0:T(8,128)(2,1)S(1)}, u32[]{:S(2)}, u32[]{:S(2)}) collective-permute-start(bf16[256,2304]{1,0:T(8,128)(2,1)S(1)} %bitcast.87), channel_id=1, source_target_pairs={{0,0},{1,4},{2,8},{3,12},{4,1},{5,5},{6,9},{7,13},{8,2},{9,6},{10,... | collective-permute-start | bytes 3538952 | tf_op jit(solution)/shard_map/ppermute | solution.py:1285
  261.2 48.5 %copy-start.6 = (bf16[256,2304]{1,0:T(8,128)(2,1)S(1)}, bf16[256,2304]{1,0:T(8,128)(2,1)}, u32[]{:S(2)}) copy-start(bf16[256,2304]{1,0:T(8,128)(2,1)} %get-tuple-element.63) | copy-start | bytes 3538948
  312.5 1.7 copy-start
  312.5 3.0 copy-start.26
  314.3 1.3 copy-start.22
  315.6 46.1 %copy-start.8 = (bf16[256,2304]{1,0:T(8,128)(2,1)}, bf16[256,2304]{1,0:T(8,128)(2,1)S(1)}, u32[]{:S(2)}) copy-start(bf16[256,2304]{1,0:T(8,128)(2,1)S(1)} %collective-permute-done) | copy-start | bytes 3538948
  317.0 45.0 %copy-start.13 = (bf16[576,720]{1,0:T(8,128)(2,1)S(1)}, bf16[576,720]{1,0:T(8,128)(2,1)}, u32[]{:S(2)}) copy-start(bf16[576,720]{1,0:T(8,128)(2,1)} %get-tuple-element.131) | copy-start | bytes 2488324
  317.0 45.0 %copy-start.14 = (bf16[576,720]{1,0:T(8,128)(2,1)S(1)}, bf16[576,720]{1,0:T(8,128)(2,1)}, u32[]{:S(2)}) copy-start(bf16[576,720]{1,0:T(8,128)(2,1)} %get-tuple-element.127) | copy-start | bytes 2488324
  361.7 262.3 %reduce-scatter.4.cloned.1.call-start = ((), (), s32[]{:S(2)}) async-start(), calls=%async_computation.4 | async-start | bytes 4239360 | tf_op jit(solution)/shard_map/reduce_scatter | solution.py:1415
  370.4 19.9 %copy-start.11 = (bf16[2,2,576,1440]{3,2,1,0:T(8,128)(2,1)}, bf16[2,2,576,1440]{3,2,1,0:T(8,128)(2,1)S(1)}, u32[]{:S(2)}) copy-start(bf16[2,2,576,1440]{3,2,1,0:T(8,128)(2,1)S(1)} %maximum_select_fusion.1) | copy-start | bytes 19906564
  390.3 5.5 copy-start.5
  395.7 1.6 copy-start.15
  436.7 14.4 %copy-start.17 = (bf16[2048,720]{0,1:T(8,128)(2,1)}, bf16[2048,720]{0,1:T(8,128)(2,1)S(1)}, u32[]{:S(2)}) copy-start(bf16[2048,720]{0,1:T(8,128)(2,1)S(1)} %get-tuple-element.126) | copy-start | bytes 8847364
  440.2 55.1 %collective-permute-start.4 = (bf16[2048,1440]{0,1:T(8,128)(2,1)}, bf16[2048,1440]{0,1:T(8,128)(2,1)}, u32[]{:S(2)}, u32[]{:S(2)}) collective-permute-start(bf16[2048,1440]{0,1:T(8,128)(2,1)} %pad_maximum_fusion), channel_id=1, source_target_pairs={{0,4},{4,0},{1,5},{5,1},{2,6},{6,2},{3,7},{7,3},{8,12},{12,8},{9,1... | collective-permute-start | bytes 17694728 | tf_op jit(solution)/shard_map/ppermute | solution.py:39
  451.1 11.5 copy-start.16
  495.3 8.9 copy-start.19
  506.8 8.9 copy-start.18
  518.4 301.2 %all-gather.5.cloned.1.call-start = ((), (), s32[]{:S(2)}) async-start(), calls=%async_computation.5 | async-start | bytes 4239360 | tf_op jit(solution)/shard_map/all_gather | solution.py:1432
  518.4 50.4 %copy-start.1 = (f32[256,2304]{1,0:T(8,128)S(1)}, f32[256,2304]{1,0:T(8,128)}, u32[]{:S(2)}) copy-start(f32[256,2304]{1,0:T(8,128)} %copy-done) | copy-start | bytes 7077892
  518.4 50.4 %copy-start.23 = (f32[2304]{0:T(1024)S(1)}, f32[2304]{0:T(1024)}, u32[]{:S(2)}) copy-start(f32[2304]{0:T(1024)} %copy-done.22) | copy-start | bytes 27652
  518.4 50.4 %copy-start.27 = (f32[256]{0:T(256)S(1)}, f32[256]{0:T(256)}, u32[]{:S(2)}) copy-start(f32[256]{0:T(256)} %copy-done.26) | copy-start | bytes 3076
  568.9 2.5 copy-start.3
  568.9 2.7 copy-start.9
  571.6 1.8 copy-start.29
  624.0 195.5 %reduce-scatter.6.cloned.1.call-start = ((), (), s32[]{:S(2)}) async-start(), calls=%async_computation.6 | async-start | bytes 4239360 | tf_op jit(solution)/shard_map/reduce_scatter | solution.py:1415
  624.6 202.1 %reduce-scatter.8.cloned.1.call-start = ((), (), s32[]{:S(2)}) async-start(), calls=%async_computation.7 | async-start | bytes 4423680 | tf_op jit(solution)/shard_map/reduce_scatter | solution.py:1415
  624.7 7.5 copy-start.31
  631.5 3.4 collective-permute-start.6
  734.8 53.5 %collective-permute-start.5 = (bf16[1024,1728]{0,1:T(8,128)(2,1)}, bf16[1024,1728]{0,1:T(8,128)(2,1)}, u32[]{:S(2)}, u32[]{:S(2)}) collective-permute-start(bf16[1024,1728]{0,1:T(8,128)(2,1)} %copy.43), channel_id=1, source_target_pairs={{0,4},{4,0},{1,5},{5,1},{2,6},{6,2},{3,7},{7,3},{8,12},{12,8},{9,1... | collective-permute-start | bytes 10616840 | tf_op jit(solution)/shard_map/ppermute | solution.py:39
  735.2 45.4 %copy-start.7 = (bf16[256,2304]{1,0:T(8,128)(2,1)S(1)}, bf16[256,2304]{1,0:T(8,128)(2,1)}, u32[]{:S(2)}) copy-start(bf16[256,2304]{1,0:T(8,128)(2,1)} %get-tuple-element.63) | copy-start | bytes 3538948
  735.2 45.4 %copy-start.25 = (f32[2304]{0:T(1024)S(1)}, f32[2304]{0:T(1024)}, u32[]{:S(2)}) copy-start(f32[2304]{0:T(1024)} %get-tuple-element.121) | copy-start | bytes 27652
  735.2 48.6 %copy-start.4 = (f32[256,2304]{1,0:T(8,128)S(1)}, f32[256,2304]{1,0:T(8,128)}, u32[]{:S(2)}) copy-start(f32[256,2304]{1,0:T(8,128)} %scatter_rows.4) | copy-start | bytes 7077892
  780.5 3.3 copy-start.2
  780.6 3.3 copy-start.10
  780.6 3.3 copy-start.24
  780.6 3.3 copy-start.28
  780.6 3.3 copy-start.30
  815.3 1.3 copy-start.12
  826.7 293.4 %copy-start.20 = (bf16[256,2304]{1,0:T(8,128)(2,1)S(1)}, bf16[256,2304]{1,0:T(8,128)(2,1)}, u32[]{:S(2)}) copy-start(bf16[256,2304]{1,0:T(8,128)(2,1)} %get-tuple-element.101) | copy-start | bytes 3538948
  1116.4 83.4 %collective-permute-start.7 = (bf16[256,2304]{1,0:T(8,128)(2,1)}, bf16[256,2304]{1,0:T(8,128)(2,1)}, u32[]{:S(2)}, u32[]{:S(2)}) collective-permute-start(bf16[256,2304]{1,0:T(8,128)(2,1)} %get-tuple-element.100), channel_id=1, source_target_pairs={{0,0},{1,4},{2,8},{3,12},{4,1},{5,5},{6,9},{7,13},{8,2},{9,6},{10,... | collective-permute-start | bytes 3538952 | tf_op jit(solution)/shard_map/ppermute | solution.py:1285
  1120.2 104.2 %collective-permute-start.8 = (bf16[256,2304]{1,0:T(8,128)(2,1)S(1)}, bf16[256,2304]{1,0:T(8,128)(2,1)}, u32[]{:S(2)}, u32[]{:S(2)}) collective-permute-start(bf16[256,2304]{1,0:T(8,128)(2,1)S(1)} %copy-done.20), channel_id=1, source_target_pairs={{0,0},{1,4},{2,8},{3,12},{4,1},{5,5},{6,9},{7,13},{8,2},{9,6},{10,... | collective-permute-start | bytes 3538952 | tf_op jit(solution)/shard_map/ppermute | solution.py:1285
  1127.4 96.9 %collective-permute-start.9 = (bf16[576,2880]{1,0:T(8,128)(2,1)}, bf16[576,2880]{1,0:T(8,128)(2,1)}, u32[]{:S(2)}, u32[]{:S(2)}) collective-permute-start(bf16[576,2880]{1,0:T(8,128)(2,1)} %all-gather.5.cloned.1.call-done.near), channel_id=1, source_target_pairs={{0,16},{16,0},{1,17},{17,1},{2,18},{18,2},{3,19},{19,3},{4,20},{20... | collective-permute-start | bytes 9953288 | tf_op jit(solution)/shard_map/ppermute | solution.py:39
Sparse Core Ops, SparseCore 0:
  361.8 59.2 all-gather.2
  518.5 64.6 reduce-scatter.3
  624.1 67.5 all-gather.4
  694.5 62.8 reduce-scatter.5
  760.1 66.5 reduce-scatter.7
